TPU v7x, 32 devices: a whole 2x2x4 slice. The times are simulated.
32 devices in a mesh: seq: 8 (over z, y), head: 4 (over x, core).
Axes of the slice: x: 2, y: 2, z: 4, core: 2. Of those that a mesh axis runs over, the one named last changes fastest.
Arguments:
- queries: bfloat16 [3072, 1536], P('seq', 'head'), may hold values from -34.5 to 34.5
- out_grad: bfloat16 [3072, 1536], P('seq', 'head'), may hold values from -48 to 48
- tile_mask: int32 [24, 2], P('seq'), may hold values from 0 to 1, as said below
- slot_caption: int32 [8, 2], replicated, may hold values from 0 to 2, as said below
- caption_cache: bfloat16 [2, 16, 512, 1536], P(None, 'seq', None, 'head'), may hold values from -6.1 to 6.1, as said below
- key_weight: bfloat16 [1536, 1536], P(None, 'head'), may hold values from -0.15625 to 0.15625
- value_weight: bfloat16 [1536, 1536], P(None, 'head'), may hold values from -0.15625 to 0.15625
Outputs:
- query_grad: bfloat16 [3072, 1536], P('seq', 'head')
- text_grad: bfloat16 [2, 512, 1536], P(None, 'seq', 'head')
Inputs may be any that keep to these rules, and one draw needn't show every extreme that they name: `tile_mask`: each row has exactly one 1; it marks the slot of its seq index whose caption the tile reads. `slot_caption`: row d lists the captions that the tiles of seq index d read, each once; one entry always names a caption, the other names another caption or is 2 for an empty slot, and no tile points to an empty slot. A caption's tiles are consecutive and lie on consecutive seq indices; a seq index holds at most one caption boundary; every caption is read. `caption_cache`: slots that hold the same caption hold equal copies of its keys and values.
All inputs are finite; a program needn't handle non-finite values.
Results may differ from a plain program's by a relative error of at most 0.0096.
Values may be sent and summed in bfloat16 or wider, within the bound.
No kernel may reach another device: no remote copies, remote signals or barrier semaphores. Data moves between devices by JAX's collectives and lax.ppermute only.
A program may use at most 64 MiB of HBM per device.

v0:
```python
import math

import jax
import jax.numpy as jnp
from jax import lax
from jax.sharding import PartitionSpec as P

D = 1536
DH = 128
L = 512
TILE = 128
SPAN = 4


def shards(queries, out_grad, tile_mask, slot_caption, caption_cache, key_weight, value_weight):
    highest = lax.Precision.HIGHEST
    rows_here, width = queries.shape
    head_count = width // DH
    tile_count = rows_here // TILE
    slot_count = tile_mask.shape[1]
    inv_root = 1.0 / math.sqrt(DH)
    query_tiles = queries.reshape(tile_count, TILE, head_count, DH)
    grad_tiles = out_grad.reshape(tile_count, TILE, head_count, DH)
    slot_onehot = tile_mask.astype(jnp.float32)
    slot_lo = tile_mask.astype(jnp.bfloat16)
    key_rows = jnp.einsum(
        "ts,sjc->tjc", slot_lo, caption_cache[0], preferred_element_type=jnp.float32
    )
    key_rows = key_rows.astype(jnp.bfloat16).reshape(tile_count, L, head_count, DH)
    value_rows = jnp.einsum(
        "ts,sjc->tjc", slot_lo, caption_cache[1], preferred_element_type=jnp.float32
    )
    value_rows = value_rows.astype(jnp.bfloat16).reshape(tile_count, L, head_count, DH)
    scores = (
        jnp.einsum("tqhe,tjhe->thqj", query_tiles, key_rows, preferred_element_type=jnp.float32)
        * inv_root
    )
    row_max = jnp.max(scores, axis=-1, keepdims=True)
    exp_scores = jnp.exp(scores - row_max)
    attention = exp_scores / jnp.sum(exp_scores, axis=-1, keepdims=True)
    attention_lo = attention.astype(jnp.bfloat16)
    context = jnp.einsum(
        "thqj,tjhe->tqhe", attention_lo, value_rows, preferred_element_type=jnp.float32
    )
    row_dot = jnp.transpose(jnp.sum(grad_tiles.astype(jnp.float32) * context, axis=-1), (0, 2, 1))
    attention_grad = jnp.einsum(
        "tqhe,tjhe->thqj", grad_tiles, value_rows, preferred_element_type=jnp.float32
    )
    score_grad = attention * (attention_grad - row_dot[..., None])
    score_lo = score_grad.astype(jnp.bfloat16)
    query_grad = (
        jnp.einsum("thqj,tjhe->tqhe", score_lo, key_rows, preferred_element_type=jnp.float32)
        * inv_root
    )
    query_grad = query_grad.astype(jnp.bfloat16).reshape(rows_here, width)
    key_pieces = (
        jnp.einsum("thqj,tqhe->tjhe", score_lo, query_tiles, preferred_element_type=jnp.float32)
        * inv_root
    )
    value_pieces = jnp.einsum(
        "thqj,tqhe->tjhe", attention_lo, grad_tiles, preferred_element_type=jnp.float32
    )
    key_part = jnp.einsum("ts,tjhe->sjhe", slot_onehot, key_pieces, precision=highest)
    key_part = key_part.astype(jnp.bfloat16).reshape(slot_count, L, width)
    value_part = jnp.einsum("ts,tjhe->sjhe", slot_onehot, value_pieces, precision=highest)
    value_part = value_part.astype(jnp.bfloat16).reshape(slot_count, L, width)
    seq_count = lax.axis_size("seq")
    caption_count = seq_count // SPAN
    block_rows = L // seq_count
    flat_table = slot_caption.T.reshape(1, slot_count * seq_count)
    selector = (flat_table == jnp.arange(caption_count, dtype=jnp.int32)[:, None]).astype(
        jnp.float32
    )
    payload = jnp.stack([key_part, value_part]).reshape(2, slot_count, seq_count, block_rows, width)
    received = lax.all_to_all(payload, "seq", split_axis=2, concat_axis=2, tiled=True)
    received = received.reshape(2, slot_count * seq_count, block_rows * width).astype(jnp.float32)
    merged = jnp.einsum("cm,kmx->kcx", selector, received, precision=highest)
    merged = merged.reshape(2, caption_count * block_rows, width)
    summed = jnp.dot(merged[0], key_weight.astype(jnp.float32).T, precision=highest)
    summed = summed + jnp.dot(merged[1], value_weight.astype(jnp.float32).T, precision=highest)
    summed = summed.reshape(caption_count, block_rows, D)
    text_grad = lax.psum_scatter(summed, "head", scatter_dimension=2, tiled=True).astype(
        jnp.bfloat16
    )
    return (query_grad, text_grad)


def solution(mesh):
    placed = (
        P("seq", "head"),
        P("seq", "head"),
        P("seq", None),
        P(),
        P(None, "seq", None, "head"),
        P(None, "head"),
        P(None, "head"),
    )
    return jax.shard_map(
        shards,
        mesh=mesh,
        in_specs=placed,
        out_specs=(P("seq", "head"), P(None, "seq", "head")),
        check_vma=False,
    )
```

profile of v0, /device:TPU:0, one launch (start us, length us, event | category | flops | bytes accessed | tf_op | source)
XLA Modules:
  0.0 151.3 jit_solution(3961999689173194765)
XLA Ops:
  7.2 1.6 %fusion.55 = (bf16[1,2,512,384]{3,2,1,0:T(8,128)(2,1)S(1)}, bf16[1,2,512,384]{3,2,1,0:T(8,128)(2,1)S(1)}) fusion(bf16[2,2,512,384]{3,2,1,0:T(8,128)(2,1)} %param.11), kind=kLoop, calls=%fused_computation.51 | loop fusion | bytes 3145728 | tf_op jit(solution)/shard_map/slice | solution.py:31
  8.8 3.4 %convolution_convert_fusion.1 = bf16[3,512,384]{2,0,1:T(4,128)(2,1)} fusion(bf16[1,2,512,384]{3,2,1,0:T(8,128)(2,1)S(1)} %get-tuple-element.3, s32[3,2]{0,1:T(2,128)S(1)} %copy-done.8), kind=kOutput, calls=%fused_computation.17 | convolution fusion | flops 2949126 | bytes 1966104 | tf_op jit(solution)/shard_map/ts,sjc->tjc/dot_general | solution.py:26
  12.3 2.6 %copy.36 = bf16[3,512,384]{1,2,0:T(8,128)(2,1)S(1)} copy(bf16[3,512,384]{2,0,1:T(4,128)(2,1)} %convolution_convert_fusion.1) | data formatting | bytes 2359296 | tf_op jit(solution)/shard_map/convert_element_type | solution.py:29
  14.9 3.4 %convolution_convert_fusion = bf16[3,512,384]{2,0,1:T(4,128)(2,1)} fusion(bf16[1,2,512,384]{3,2,1,0:T(8,128)(2,1)S(1)} %get-tuple-element.2, s32[3,2]{0,1:T(2,128)S(1)} %copy-done.8), kind=kOutput, calls=%fused_computation.16 | convolution fusion | flops 2949126 | bytes 1966104 | tf_op jit(solution)/shard_map/ts,sjc->tjc/dot_general | solution.py:30
  18.3 3.6 %copy.40 = bf16[3,512,384]{1,2,0:T(8,128)(2,1)} copy(bf16[3,512,384]{2,0,1:T(4,128)(2,1)} %convolution_convert_fusion) | data formatting | bytes 2359296 | tf_op jit(solution)/shard_map/convert_element_type | solution.py:33
  23.6 2.1 %fusion.57 = (f32[3,3,128]{2,1,0:T(4,128)S(1)}, f32[3,3,128,512]{2,3,1,0:T(8,128)}) fusion(f32[3,3,512,128]{3,2,1,0:T(8,128)S(1)} %fusion.30), kind=kOutput, calls=%fused_computation.53 | output fusion | flops 2359807 | bytes 4723200 | tf_op jit(solution)/shard_map/sub | solution.py:39
  25.7 4.8 %convolution_bitcast_fusion.1 = f32[3,512,3,128]{3,1,2,0:T(8,128)} fusion(bf16[3,128,3,128]{1,3,2,0:T(8,128)(2,1)} %copy.43, f32[3,3,128]{2,1,0:T(4,128)S(1)} %get-tuple-element.6, f32[3,3,512,128]{3,2,1,0:T(8,128)} %copy-done.1), kind=kOutput, calls=%fused_computation.15 | convolution fusion | flops 153945728 | bytes 5018112 | tf_op jit(solution)/shard_map/thqj,tqhe->tjhe/dot_general | solution.py:60
  30.5 4.1 %fusion.25 = f32[3,128,3]{1,2,0:T(4,128)} fusion(bf16[3,512,3,128]{1,3,2,0:T(8,128)(2,1)S(1)} %bitcast.100, bf16[3,128,3,128]{1,3,2,0:T(8,128)(2,1)} %copy.43, f32[3,3,128]{2,1,0:T(4,128)S(1)} %get-tuple-element.6, f32[3,3,512,128]{3,2,1,0:T(8,128)} %copy-done.1), kind=kOutput, calls=%fused_computation.27 | convolution fusion | flops 154386944 | bytes 3843072 | tf_op jit(solution)/shard_map/thqj,tjhe->tqhe/dot_general | solution.py:42
  34.7 8.7 %fusion.17 = bf16[2,512,3,128]{3,0,2,1:T(2,128)(2,1)S(1)} fusion(f32[3,512,3,128]{3,1,2,0:T(8,128)} %convolution_bitcast_fusion.1, s32[3,2]{0,1:T(2,128)S(1)} %copy-done.8), kind=kOutput, calls=%fused_computation.21 | convolution fusion | flops 14548998 | bytes 3145752 | tf_op jit(solution)/shard_map/ts,tjhe->sjhe/dot_general | solution.py:65
  43.7 1.5 stack.8
  45.1 2.8 %fusion.5 = bf16[3,3,128,512]{2,3,1,0:T(8,128)(2,1)S(1)} fusion(bf16[3,512,3,128]{1,3,2,0:T(8,128)(2,1)} %bitcast.99, bf16[3,128,3,128]{1,3,2,0:T(8,128)(2,1)} %copy.43, f32[3,3,128]{2,1,0:T(4,128)} %bitcast.103, f32[3,3,128,512]{2,3,1,0:T(8,128)} %get-tuple-element.7, f32[3,3,128]{2,1,0:T(4,128)S(1)} %get-tuple-element.6), kind=kOutput, calls=%fused_computation.8 | convolution fusion | flops 153354240 | bytes 5022720 | tf_op jit(solution)/shard_map/tqhe,tjhe->thqj/dot_general | solution.py:46
  48.4 7.6 %fusion.20 = bf16[2,512,3,128]{3,0,2,1:T(2,128)(2,1)S(1)} fusion(f32[3,512,3,128]{3,1,2,0:T(8,128)S(1)} %multiply_bitcast_fusion, s32[3,2]{0,1:T(2,128)S(1)} %copy-done.8), kind=kOutput, calls=%fused_computation.22 | convolution fusion | flops 14548998 | bytes 3145752 | tf_op jit(solution)/shard_map/ts,tjhe->sjhe/dot_general | solution.py:63
  57.3 3.2 %stack.7 = bf16[1,2,8,64,384]{4,3,2,1,0:T(8,128)(2,1)} reshape(bf16[2,512,3,128]{3,2,1,0:T(4,128)(2,1)} %copy.49) | data formatting | bytes 1572864 | tf_op jit(solution)/shard_map/stack | solution.py:74
  60.6 1.5 %pad_maximum_fusion = bf16[2,2,8,64,384]{4,3,2,1,0:T(8,128)(2,1)S(1)} fusion(bf16[1,2,8,64,384]{4,3,2,1,0:T(8,128)(2,1)} %stack.8, bf16[1,2,8,64,384]{4,3,2,1,0:T(8,128)(2,1)} %stack.7), kind=kLoop, calls=%fused_computation.18 | loop fusion | flops 786432 | bytes 3145728 | tf_op jit(solution)/shard_map/stack | solution.py:74
  62.1 1.3 copy.53
  63.5 7.4 %all-to-all-start = ((bf16[2,2,8,64,384]{4,3,1,0,2:T(8,128)(2,1)}), bf16[2,2,8,64,384]{4,3,1,0,2:T(8,128)(2,1)}, u32[]{:S(2)}, u32[]{:S(2)}) async-start(bf16[2,2,8,64,384]{4,3,1,0,2:T(8,128)(2,1)} %copy.53), calls=%async_computation | async-start | bytes 3145728 | tf_op jit(solution)/shard_map/all_to_all | solution.py:75
  71.0 37.0 %all-to-all-done = bf16[2,2,8,64,384]{4,3,1,0,2:T(8,128)(2,1)} async-done(((bf16[2,2,8,64,384]{4,3,1,0,2:T(8,128)(2,1)}), bf16[2,2,8,64,384]{4,3,1,0,2:T(8,128)(2,1)}, u32[]{:S(2)}, u32[]{:S(2)}) %all-to-all-start) | async-done | bytes 1572896 | tf_op jit(solution)/shard_map/all_to_all | solution.py:75
  108.0 2.3 %copy.54 = bf16[2,2,8,64,384]{4,2,3,1,0:T(8,128)(2,1)S(1)} copy(bf16[2,2,8,64,384]{4,3,1,0,2:T(8,128)(2,1)} %all-to-all-done) | data formatting | bytes 3145728 | tf_op jit(solution)/shard_map/all_to_all | solution.py:75
  111.4 1.8 %squeeze.14 = f32[128,384]{1,0:T(8,128)} reshape(f32[1,2,24576]{2,1,0:T(2,128)} %get-tuple-element.5) | data formatting | bytes 393216 | tf_op jit(solution)/shard_map/squeeze | solution.py:79
  113.2 1.8 %squeeze.15 = f32[128,384]{1,0:T(8,128)} reshape(f32[1,2,24576]{2,1,0:T(2,128)} %get-tuple-element.4) | data formatting | bytes 393216 | tf_op jit(solution)/shard_map/squeeze | solution.py:80
  115.0 2.3 %fusion.58 = f32[128,1536]{1,0:T(8,128)S(1)} fusion(f32[128,384]{1,0:T(8,128)} %squeeze.14, bf16[1536,384]{1,0:T(8,128)(2,1)S(1)} %copy-done), kind=kOutput, calls=%fused_computation.54 | convolution fusion | flops 905969664 | bytes 2162688 | tf_op jit(solution)/shard_map/dot_general | solution.py:79
  117.3 3.1 %convolution_add_fusion = f32[128,1536]{1,0:T(8,128)} fusion(f32[128,1536]{1,0:T(8,128)S(1)} %fusion.58, f32[128,384]{1,0:T(8,128)} %squeeze.15, bf16[1536,384]{1,0:T(8,128)(2,1)S(1)} %copy-done.4), kind=kOutput, calls=%fused_computation.6 | convolution fusion | flops 906166272 | bytes 2949120 | tf_op jit(solution)/shard_map/dot_general | solution.py:80
  123.6 19.3 %reduce-scatter.2.cloned.1.call-done = f32[2,64,384]{2,1,0:T(8,128)} async-done(((f32[2,64,1536]{2,1,0:T(8,128)}), f32[2,64,384]{2,1,0:T(8,128)}) %reduce-scatter.2.cloned.1.call-update) | async-done | bytes 196624 | tf_op jit(solution)/shard_map/reduce_scatter | solution.py:82
  142.9 1.6 %convert_element_type.59 = bf16[2,64,384]{2,1,0:T(8,128)(2,1)} convert(f32[2,64,384]{2,1,0:T(8,128)} %reduce-scatter.2.cloned.1.call-done) | non-fusion elementwise | flops 49152 | bytes 294912 | tf_op jit(solution)/shard_map/convert_element_type | solution.py:82
  (35 shorter events, 8.1 us)
Async XLA Ops:
  7.2 107.8 %copy-start = (bf16[1536,384]{1,0:T(8,128)(2,1)S(1)}, bf16[1536,384]{1,0:T(8,128)(2,1)}, u32[]{:S(2)}) copy-start(bf16[1536,384]{1,0:T(8,128)(2,1)} %param.12) | copy-start | bytes 3538948
  7.2 1.6 %copy-start.8 = (s32[3,2]{0,1:T(2,128)S(1)}, s32[3,2]{0,1:T(2,128)}, u32[]{:S(2)}) copy-start(s32[3,2]{0,1:T(2,128)} %param.9) | copy-start | bytes 76
  14.8 7.1 %copy-start.6 = (bf16[384,384]{1,0:T(8,128)(2,1)S(1)}, bf16[384,384]{1,0:T(8,128)(2,1)}, u32[]{:S(2)}) copy-start(bf16[384,384]{1,0:T(8,128)(2,1)} %param.8) | copy-start | bytes 884740
  18.3 4.6 %copy-start.7 = (bf16[384,384]{1,0:T(8,128)(2,1)S(1)}, bf16[384,384]{1,0:T(8,128)(2,1)}, u32[]{:S(2)}) copy-start(bf16[384,384]{1,0:T(8,128)(2,1)} %param.7) | copy-start | bytes 884740
  23.0 2.7 %copy-start.2 = (bf16[3,128,3,128]{3,2,1,0:T(4,128)(2,1)}, bf16[3,128,3,128]{3,2,1,0:T(4,128)(2,1)S(1)}, u32[]{:S(2)}) copy-start(bf16[3,128,3,128]{3,2,1,0:T(4,128)(2,1)S(1)} %reshape.41) | copy-start | bytes 884740
  23.6 2.1 %copy-start.1 = (f32[3,3,512,128]{3,2,1,0:T(8,128)}, f32[3,3,512,128]{3,2,1,0:T(8,128)S(1)}, u32[]{:S(2)}) copy-start(f32[3,3,512,128]{3,2,1,0:T(8,128)S(1)} %fusion.30) | copy-start | bytes 7077892
  25.7 4.8 %copy-start.5 = (bf16[3,512,384]{1,2,0:T(8,128)(2,1)S(1)}, bf16[3,512,384]{1,2,0:T(8,128)(2,1)}, u32[]{:S(2)}) copy-start(bf16[3,512,384]{1,2,0:T(8,128)(2,1)} %copy.40) | copy-start | bytes 3538948
  45.1 2.8 %copy-start.3 = (bf16[3,128,3,128]{3,2,1,0:T(4,128)(2,1)S(1)}, bf16[3,128,3,128]{3,2,1,0:T(4,128)(2,1)}, u32[]{:S(2)}) copy-start(bf16[3,128,3,128]{3,2,1,0:T(4,128)(2,1)} %copy-done.2) | copy-start | bytes 884740
  63.5 7.5 %copy-start.9 = (s32[8,2]{0,1:T(2,128)S(1)}, s32[8,2]{0,1:T(2,128)}, u32[]{:S(2)}) copy-start(s32[8,2]{0,1:T(2,128)} %param.10) | copy-start | bytes 196
  63.5 44.5 %all-to-all-start = ((bf16[2,2,8,64,384]{4,3,1,0,2:T(8,128)(2,1)}), bf16[2,2,8,64,384]{4,3,1,0,2:T(8,128)(2,1)}, u32[]{:S(2)}, u32[]{:S(2)}) async-start(bf16[2,2,8,64,384]{4,3,1,0,2:T(8,128)(2,1)} %copy.53), calls=%async_computation | async-start | bytes 3145728 | tf_op jit(solution)/shard_map/all_to_all | solution.py:75
  70.9 72.0 %reduce-scatter.2.cloned.1.call-start = ((), (), s32[]{:S(2)}) async-start(), calls=%async_computation.2 | async-start | bytes 983040 | tf_op jit(solution)/shard_map/reduce_scatter | solution.py:82
  115.0 2.3 %copy-start.4 = (bf16[1536,384]{1,0:T(8,128)(2,1)S(1)}, bf16[1536,384]{1,0:T(8,128)(2,1)}, u32[]{:S(2)}) copy-start(bf16[1536,384]{1,0:T(8,128)(2,1)} %param.13) | copy-start | bytes 3538948
Sparse Core Ops, SparseCore 0:
  120.5 22.3 reduce-scatter.1
where the time goes:
time: 152 us; the launch traced here: 151 us
  waiting for transfers between devices  56.3 us (37%)
  matrix products  42.9 us (28%)
  local copies, waits for them, and re-layouts  25.2 us (17%)
  between operations  14.2 us (9%)
  starting transfers between devices  7.44 us (5%)
  other arithmetic  5.23 us (3%)
    all_to_all x1, waiting for transfers between devices, shards(): lax.all_to_all(payload, 'seq', split_axis=2, concat_axis=2, tiled=True)  37 us
    reduce_scatter x1, waiting for transfers between devices, shards(): lax.psum_scatter(summed, 'head', scatter_dimension=2, tiled=True)  19.3 us
    dot_general x1, matrix products, shards(): jnp.einsum('ts,tjhe->sjhe', slot_onehot, value_pieces, precision=highest)  8.72 us
    dot_general x1, matrix products, shards(): jnp.einsum('ts,tjhe->sjhe', slot_onehot, key_pieces, precision=highest)  7.63 us
    all_to_all x1, starting transfers between devices, shards(): lax.all_to_all(payload, 'seq', split_axis=2, concat_axis=2, tiled=True)  7.4 us
    another operation x3, local copies, waits for them, and re-layouts, shards(): jnp.stack([key_part, value_part])  6.03 us
    dot_general x1, matrix products, shards(): jnp.einsum('thqj,tqhe->tjhe', attention_lo, grad_tiles, preferred_element...  4.8 us
    dot_general x1, matrix products, shards(): jnp.einsum('thqj,tjhe->tqhe', attention_lo, value_rows, preferred_element...  4.14 us
  transfers between devices with their start and end apart: 2, of which 2 were waited for; matrix products, arithmetic and copies ran while one was open for 2% of the time, Pallas kernels for 0%

commit v1 on v0

--- a/solution.py
+++ b/solution.py
@@ -1,18 +1,222 @@
+import functools
 import math
 
 import jax
 import jax.numpy as jnp
 from jax import lax
+from jax.experimental import pallas as pl
+from jax.experimental.pallas import tpu as pltpu
 from jax.sharding import PartitionSpec as P
 
-D = 1536
 DH = 128
 L = 512
 TILE = 128
 SPAN = 4
-
-
-def shards(queries, out_grad, tile_mask, slot_caption, caption_cache, key_weight, value_weight):
+F32 = jnp.float32
+BF16 = jnp.bfloat16
+VMEM_LIMIT = 48 * 1024 * 1024
+
+
+def dot(a, b, contract):
+    return lax.dot_general(a, b, ((contract[:1], contract[1:]), ((), ())), preferred_element_type=F32)
+
+
+def tile_slot(mask_ref, tile):
+    return mask_ref[1, tile]
+
+
+def held(caps_ref, d, captions):
+    first, second = caps_ref[0, d], caps_ref[1, d]
+    single = jnp.logical_or(first == captions, second == captions)
+    return single, jnp.where(first == captions, second, first)
+
+
+def main_slot(caps_ref, me, captions):
+    single, caption = held(caps_ref, me, captions)
+    _, other = held(caps_ref, jnp.bitwise_xor(me, 1), captions)
+    first = caps_ref[0, me]
+    return jnp.where(single, jnp.where(first == captions, 1, 0), jnp.where(first == other, 1, 0))
+
+
+def backward(key, value, query, grad):
+    scores = dot(key, query, (1, 1))
+    top = jnp.max(scores, axis=0, keepdims=True)
+    exps = jnp.exp((scores - top) * (1.0 / math.sqrt(DH)))
+    attention = exps / jnp.sum(exps, axis=0, keepdims=True)
+    attention_lo = attention.astype(BF16)
+    attention_grad = dot(value, grad, (1, 1))
+    row_dot = jnp.sum(attention_lo.astype(F32) * attention_grad, axis=0, keepdims=True)
+    score_lo = (attention * (attention_grad - row_dot)).astype(BF16)
+    return attention_lo, score_lo
+
+
+def ship_kernel(captions, tiles, mask_ref, caps_ref, q_ref, g_ref, out_ref):
+    me = lax.axis_index("seq")
+    mine = main_slot(caps_ref, me, captions)
+    odd = jnp.bitwise_and(me, 1)
+    for i in range(tiles - 1):
+        tile = i + 1 - odd
+        keep = (tile_slot(mask_ref, tile) != mine).astype(F32).astype(BF16)
+        rows = pl.ds(pl.multiple_of(tile * TILE, TILE), TILE)
+        out_ref[0, i * TILE : (i + 1) * TILE, :] = q_ref[rows, :] * keep
+        out_ref[1, i * TILE : (i + 1) * TILE, :] = g_ref[rows, :] * keep
+
+
+def own_kernel(captions, tiles, mask_ref, caps_ref, q_ref, g_ref, cache_ref, dq_ref, part_ref, key_t):
+    me = lax.axis_index("seq")
+    mine = main_slot(caps_ref, me, captions)
+    inv_root = 1.0 / math.sqrt(DH)
+    for s in range(cache_ref.shape[1]):
+        key_t[s] = cache_ref[0, s].T
+    probs, grads, queries, outs = [], [], [], []
+    for t in range(tiles):
+        slot = tile_slot(mask_ref, t)
+        rows = slice(t * TILE, (t + 1) * TILE)
+        query, grad = q_ref[rows, :], g_ref[rows, :]
+        attention_lo, score_lo = backward(cache_ref[0, slot], cache_ref[1, slot], query, grad)
+        dq_t = dot(key_t[slot], score_lo, (1, 0)) * inv_root
+        dq_ref[rows, :] = dq_t.T.astype(BF16)
+        keep = (slot == mine).astype(F32).astype(BF16)
+        probs.append(attention_lo)
+        grads.append(score_lo)
+        queries.append(query * keep)
+        outs.append(grad * keep)
+    part_ref[0] = dot(jnp.concatenate(grads, axis=1), jnp.concatenate(queries, axis=0), (1, 0)) * inv_root
+    part_ref[1] = dot(jnp.concatenate(probs, axis=1), jnp.concatenate(outs, axis=0), (1, 0))
+
+
+def text_kernel(
+    captions, heads, head_devices, caps_ref, recv_ref, part_ref, cache_hbm, wk_hbm, wv_hbm, out_ref,
+    key_buf, value_buf, wk_buf, wv_buf, both, sems,
+):
+    me, col = lax.axis_index("seq"), lax.axis_index("head")
+    mine = main_slot(caps_ref, me, captions)
+    copies = [
+        pltpu.make_async_copy(cache_hbm.at[0, mine], key_buf, sems.at[0]),
+        pltpu.make_async_copy(cache_hbm.at[1, mine], value_buf, sems.at[1]),
+        pltpu.make_async_copy(wk_hbm, wk_buf, sems.at[2]),
+        pltpu.make_async_copy(wv_hbm, wv_buf, sems.at[3]),
+    ]
+    for c in copies:
+        c.start()
+    copies[0].wait()
+    copies[1].wait()
+    inv_root = 1.0 / math.sqrt(DH)
+    width = heads * DH
+    tiles = recv_ref.shape[1] // TILE
+    for h in range(heads):
+        cols = slice(h * DH, (h + 1) * DH)
+        key, value = key_buf[:, cols], value_buf[:, cols]
+        probs, grads = [], []
+        for t in range(tiles):
+            rows = slice(t * TILE, (t + 1) * TILE)
+            attention_lo, score_lo = backward(key, value, recv_ref[0, rows, cols], recv_ref[1, rows, cols])
+            probs.append(attention_lo)
+            grads.append(score_lo)
+        dk = dot(jnp.concatenate(grads, axis=1), recv_ref[0, :, cols], (1, 0)) * inv_root
+        dv = dot(jnp.concatenate(probs, axis=1), recv_ref[1, :, cols], (1, 0))
+        both[:, cols] = (part_ref[0, :, cols] + dk).astype(BF16)
+        both[:, width + h * DH : width + (h + 1) * DH] = (part_ref[1, :, cols] + dv).astype(BF16)
+    copies[2].wait()
+    copies[3].wait()
+    rows_out = out_ref.shape[2] * out_ref.shape[1]
+    for rel in range(head_devices):
+        rows = pl.ds(pl.multiple_of(jnp.bitwise_xor(col, rel) * width, width), width)
+        text = dot(both[:, :width], wk_buf[rows, :], (1, 1)) + dot(both[:, width:], wv_buf[rows, :], (1, 1))
+        out_ref[rel] = text.astype(BF16).reshape(out_ref.shape[1:])
+
+
+def swap(array, axis, bit):
+    n = lax.axis_size(axis)
+    return lax.ppermute(array, axis, [(i, i ^ bit) for i in range(n)])
+
+
+def shards_pairs(queries, out_grad, tile_mask, slot_caption, caption_cache, key_weight, value_weight):
+    rows_here, width = queries.shape
+    heads = width // DH
+    tiles = rows_here // TILE
+    slots = tile_mask.shape[1]
+    seq_count, head_devices = lax.axis_size("seq"), lax.axis_size("head")
+    captions = seq_count // SPAN
+    block_rows = L // seq_count
+    mask_t, caps_t = tile_mask.T, slot_caption.T
+    smem = pl.BlockSpec(memory_space=pltpu.SMEM)
+    vmem = pl.BlockSpec(memory_space=pltpu.VMEM)
+    hbm = pl.BlockSpec(memory_space=pl.ANY)
+
+    shipped = pl.pallas_call(
+        functools.partial(ship_kernel, captions, tiles),
+        out_shape=jax.ShapeDtypeStruct((2, (tiles - 1) * TILE, width), BF16),
+        in_specs=[smem, smem, vmem, vmem],
+        out_specs=vmem,
+        compiler_params=pltpu.CompilerParams(vmem_limit_bytes=VMEM_LIMIT),
+        name="ship",
+    )(mask_t, caps_t, queries, out_grad)
+    received = swap(shipped, "seq", 1)
+
+    query_grad, part = pl.pallas_call(
+        functools.partial(own_kernel, captions, tiles),
+        grid=(heads,),
+        out_shape=(
+            jax.ShapeDtypeStruct((rows_here, width), BF16),
+            jax.ShapeDtypeStruct((2, L, width), F32),
+        ),
+        in_specs=[
+            smem,
+            smem,
+            pl.BlockSpec((rows_here, DH), lambda h: (0, h)),
+            pl.BlockSpec((rows_here, DH), lambda h: (0, h)),
+            pl.BlockSpec((2, slots, L, DH), lambda h: (0, 0, 0, h)),
+        ],
+        out_specs=(
+            pl.BlockSpec((rows_here, DH), lambda h: (0, h)),
+            pl.BlockSpec((2, L, DH), lambda h: (0, 0, h)),
+        ),
+        scratch_shapes=[pltpu.VMEM((slots, DH, L), BF16)],
+        compiler_params=pltpu.CompilerParams(vmem_limit_bytes=VMEM_LIMIT),
+        cost_estimate=pl.CostEstimate(
+            flops=12 * rows_here * L * width, bytes_accessed=4_000_000, transcendentals=rows_here * L * heads
+        ),
+        name="own_tiles",
+    )(mask_t, caps_t, queries, out_grad, caption_cache)
+
+    text = pl.pallas_call(
+        functools.partial(text_kernel, captions, heads, head_devices),
+        out_shape=jax.ShapeDtypeStruct((head_devices, seq_count, block_rows, width), BF16),
+        in_specs=[smem, vmem, vmem, hbm, hbm, hbm],
+        out_specs=vmem,
+        scratch_shapes=[
+            pltpu.VMEM((L, width), BF16),
+            pltpu.VMEM((L, width), BF16),
+            pltpu.VMEM(key_weight.shape, BF16),
+            pltpu.VMEM(value_weight.shape, BF16),
+            pltpu.VMEM((L, 2 * width), BF16),
+            pltpu.SemaphoreType.DMA((4,)),
+        ],
+        compiler_params=pltpu.CompilerParams(vmem_limit_bytes=VMEM_LIMIT),
+        name="text",
+    )(caps_t, received, part, caption_cache, key_weight, value_weight)
+
+    bit = 1
+    while bit < head_devices:
+        text = text.reshape((-1, 2) + text.shape[1:])
+        kept, sent = text[:, 0], text[:, 1]
+        text = (kept.astype(F32) + swap(sent, "head", bit).astype(F32)).astype(BF16)
+        bit *= 2
+    arrived = lax.all_to_all(text[0], "seq", split_axis=0, concat_axis=0, tiled=True)
+    table = slot_caption
+    single = jnp.any(table == captions, axis=1)
+    only = jnp.min(table, axis=1)
+    partner = jnp.arange(seq_count) ^ 1
+    mains = jnp.where(single, only, jnp.sum(table, axis=1) - only[partner])
+    chosen = mains[None, :] == jnp.arange(captions)[:, None]
+    text_grad = jnp.sum(
+        jnp.where(chosen[:, :, None, None], arrived[None].astype(F32), 0.0), axis=1
+    ).astype(BF16)
+    return query_grad, text_grad
+
+
+def shards_general(queries, out_grad, tile_mask, slot_caption, caption_cache, key_weight, value_weight):
     highest = lax.Precision.HIGHEST
     rows_here, width = queries.shape
     head_count = width // DH
@@ -67,6 +271,7 @@
     seq_count = lax.axis_size("seq")
     caption_count = seq_count // SPAN
     block_rows = L // seq_count
+    features = key_weight.shape[0]
     flat_table = slot_caption.T.reshape(1, slot_count * seq_count)
     selector = (flat_table == jnp.arange(caption_count, dtype=jnp.int32)[:, None]).astype(
         jnp.float32
@@ -78,7 +283,7 @@
     merged = merged.reshape(2, caption_count * block_rows, width)
     summed = jnp.dot(merged[0], key_weight.astype(jnp.float32).T, precision=highest)
     summed = summed + jnp.dot(merged[1], value_weight.astype(jnp.float32).T, precision=highest)
-    summed = summed.reshape(caption_count, block_rows, D)
+    summed = summed.reshape(caption_count, block_rows, features)
     text_grad = lax.psum_scatter(summed, "head", scatter_dimension=2, tiled=True).astype(
         jnp.bfloat16
     )
@@ -86,6 +291,8 @@
 
 
 def solution(mesh):
+    seq_count, head_devices = mesh.shape["seq"], mesh.shape["head"]
+    pairs = seq_count // SPAN <= 2 and seq_count % 2 == 0 and head_devices & (head_devices - 1) == 0
     placed = (
         P("seq", "head"),
         P("seq", "head"),
@@ -96,7 +303,7 @@
         P(None, "head"),
     )
     return jax.shard_map(
-        shards,
+        shards_pairs if pairs else shards_general,
         mesh=mesh,
         in_specs=placed,
         out_specs=(P("seq", "head"), P(None, "seq", "head")),

time: 152 us -> 56 us (0.37)
  matrix products: 42.9 us -> 0 us
  waiting for transfers between devices: 56.3 us -> 23.3 us
  local copies, waits for them, and re-layouts: 25.2 us -> 5.46 us
  between operations: 14.2 us -> 0.73 us
  Pallas kernels: 0 us -> 13.2 us
  starting transfers between devices: 7.44 us -> 10.9 us
  other arithmetic: 5.23 us -> 2.02 us
    dot_general x13 -> x0, matrix products: 42.9 us -> none  [the longest x1 8.72 us: shards(): jnp.einsum('ts,tjhe->sjhe', slot_onehot, value_pieces, precision=highest)]
    all_to_all x1, waiting for transfers between devices: 37 us -> 10.5 us  [shards_pairs(): lax.all_to_all(text[0], 'seq', split_axis=0, concat_axis=0, tiled=True)]
    reduce_scatter x1 -> x0, waiting for transfers between devices: 19.3 us -> none  [shards(): lax.psum_scatter(summed, 'head', scatter_dimension=2, tiled=True)]
    pallas_call x0 -> x3, Pallas kernels: none -> 13.2 us  [the longest x1 6.6 us: shards_pairs(): pl.pallas_call(functools.partial(own_kernel, captions, tiles), grid=(head...]
    ppermute x0 -> x3, waiting for transfers between devices: none -> 12.8 us  [swap(): return lax.ppermute(array, axis, [(i, i ^ bit) for i in range(n)])]
    convert_element_type x5 -> x0, local copies, waits for them, and re-layouts: 8.92 us -> none  [the longest x1 3.61 us: shards(): value_rows.astype(jnp.bfloat16).reshape(tile_count, L, head_count, DH)]
    another operation x3 -> x0, local copies, waits for them, and re-layouts: 6.03 us -> none  [shards(): jnp.stack([key_part, value_part])]
    ppermute x0 -> x3, starting transfers between devices: none -> 4.88 us  [swap(): return lax.ppermute(array, axis, [(i, i ^ bit) for i in range(n)])]
  transfers between devices with their start and end apart: 2 -> 4, of which waited for: 2 -> 4; matrix products, arithmetic and copies ran while one was open for 2% -> 1% of each run, Pallas kernels for 0% -> 12%
where the time goes in v1:
time: 56 us; the launch traced here: 55.7 us
  waiting for transfers between devices  23.3 us (42%)
  Pallas kernels  13.2 us (24%)
  starting transfers between devices  10.9 us (19%)
  local copies, waits for them, and re-layouts  5.46 us (10%)
  other arithmetic  2.02 us (4%)
  between operations  0.73 us (1%)
    ppermute x3, waiting for transfers between devices, swap(): return lax.ppermute(array, axis, [(i, i ^ bit) for i in range(n)])  12.8 us
    all_to_all x1, waiting for transfers between devices, shards_pairs(): lax.all_to_all(text[0], 'seq', split_axis=0, concat_axis=0, tiled=True)  10.5 us
    pallas_call x1, Pallas kernels, shards_pairs(): pl.pallas_call(functools.partial(own_kernel, captions, tiles), grid=(head...  6.6 us
    all_to_all x1, starting transfers between devices, shards_pairs(): lax.all_to_all(text[0], 'seq', split_axis=0, concat_axis=0, tiled=True)  6.05 us
    pallas_call x1, Pallas kernels, shards_pairs(): pl.pallas_call(functools.partial(text_kernel, captions, heads, head_devic...  6.01 us
    ppermute x3, starting transfers between devices, swap(): return lax.ppermute(array, axis, [(i, i ^ bit) for i in range(n)])  4.88 us
    unnamed x16, local copies, waits for them, and re-layouts  4.69 us
  transfers between devices with their start and end apart: 4, of which 4 were waited for; matrix products, arithmetic and copies ran while one was open for 1% of the time, Pallas kernels for 12%

profile of v1, /device:TPU:0, one launch (start us, length us, event | category | flops | bytes accessed | tf_op | source)
XLA Modules:
  0.0 55.7 jit_solution(3731042036192755577)
XLA Ops:
  0.6 1.0 %copy-done.3 = bf16[384,384]{1,0:T(8,128)(2,1)S(1)} copy-done((bf16[384,384]{1,0:T(8,128)(2,1)S(1)}, bf16[384,384]{1,0:T(8,128)(2,1)}, u32[]{:S(2)}) %copy-start.3) | copy-done | bytes 294936
  1.6 1.0 %copy-done.4 = bf16[384,384]{1,0:T(8,128)(2,1)S(1)} copy-done((bf16[384,384]{1,0:T(8,128)(2,1)S(1)}, bf16[384,384]{1,0:T(8,128)(2,1)}, u32[]{:S(2)}) %copy-start.4) | copy-done | bytes 294936
  2.6 0.7 %copy-done.5 = s32[8,2]{0,1:T(2,128)S(1)} copy-done((s32[8,2]{0,1:T(2,128)S(1)}, s32[8,2]{0,1:T(2,128)}, u32[]{:S(2)}) %copy-start.5) | copy-done | bytes 88
  3.2 0.7 %copy-done.7 = s32[3,2]{0,1:T(2,128)S(1)} copy-done((s32[3,2]{0,1:T(2,128)S(1)}, s32[3,2]{0,1:T(2,128)}, u32[]{:S(2)}) %copy-start.7) | copy-done | bytes 48
  3.9 0.6 %ship.1 = bf16[2,256,384]{2,1,0:T(8,128)(2,1)S(1)} custom-call(s32[2,3]{1,0:T(2,128)S(1)} %bitcast.30, s32[2,8]{1,0:T(2,128)S(1)} %bitcast.27, bf16[384,384]{1,0:T(8,128)(2,1)S(1)} %copy-done.3, bf16[384,384]{1,0:T(8,128)(2,1)S(1)} %copy-done.4), custom_call_target="tpu_custom_call" | custom-call | tf_op jit(solution)/shard_map/ship/pallas_call | solution.py:147
  4.5 3.0 %collective-permute-start = (bf16[2,256,384]{2,1,0:T(8,128)(2,1)S(1)}, bf16[2,256,384]{2,1,0:T(8,128)(2,1)S(1)}, u32[]{:S(2)}, u32[]{:S(2)}) collective-permute-start(bf16[2,256,384]{2,1,0:T(8,128)(2,1)S(1)} %ship.1), channel_id=1, source_target_pairs={{0,4},{4,0},{8,12},{12,8},{16,20},{20,16},{24,28},{28,24},{1,5},{5... | collective-permute-start | bytes 1179656 | tf_op jit(solution)/shard_map/ppermute | solution.py:131
  7.6 1.4 %copy-done = bf16[2,2,512,384]{3,2,1,0:T(8,128)(2,1)S(1)} copy-done((bf16[2,2,512,384]{3,2,1,0:T(8,128)(2,1)S(1)}, bf16[2,2,512,384]{3,2,1,0:T(8,128)(2,1)}, u32[]{:S(2)}) %copy-start) | copy-done | bytes 1572888
  9.0 6.6 %own_tiles.1 = (bf16[384,384]{1,0:T(8,128)(2,1)}, f32[2,512,384]{2,1,0:T(8,128)S(1)}) custom-call(s32[2,3]{1,0:T(2,128)S(1)} %bitcast.31, s32[2,8]{1,0:T(2,128)S(1)} %bitcast.28, bf16[384,384]{1,0:T(8,128)(2,1)S(1)} %copy-done.3, bf16[384,384]{1,0:T(8,128)(2,1)S(1)} %copy-done.4, bf16[2,2,512,384]{3,2,1,0:T(8,128)(2,1)S(1)} %copy-done), custom_call_target="tpu_custom_call" | custom-call | flops 905969664 | bytes 4000000 | tf_op jit(solution)/shard_map/own_tiles/pallas_call | solution.py:157
  15.6 1.1 %collective-permute-done.recv_ref = bf16[2,256,384]{2,1,0:T(8,128)(2,1)S(1)} collective-permute-done((bf16[2,256,384]{2,1,0:T(8,128)(2,1)S(1)}, bf16[2,256,384]{2,1,0:T(8,128)(2,1)S(1)}, u32[]{:S(2)}, u32[]{:S(2)}) %collective-permute-start) | collective-permute-done | bytes 393248 | tf_op jit(solution)/shard_map/ppermute | solution.py:131
  16.7 0.0 copy-done.1
  16.7 6.0 %text.1 = bf16[4,8,64,384]{3,2,1,0:T(8,128)(2,1)S(1)} custom-call(s32[2,8]{1,0:T(2,128)S(1)} %bitcast.29, bf16[2,256,384]{2,1,0:T(8,128)(2,1)S(1)} %collective-permute-done.recv_ref, f32[2,512,384]{2,1,0:T(8,128)S(1)} %get-tuple-element.5.part_ref, bf16[2,2,512,384]{3,2,1,0:T(8,128)(2,1)} %cache_hbm.1, bf16[1536,384]{1,0:T(8,128)(2,1)S(1)} %copy-done.1, ...), custom_call_target="tpu_custom_call" | custom-call | tf_op jit(solution)/shard_map/text/pallas_call | solution.py:183
  22.7 0.1 slice_bitcast_fusion
  22.8 0.1 collective-permute-start.1
  22.9 2.3 %collective-permute-done.1 = bf16[2,8,64,384]{3,2,1,0:T(8,128)(2,1)S(1)} collective-permute-done((bf16[2,8,64,384]{3,2,1,0:T(8,128)(2,1)S(1)}, bf16[2,8,64,384]{3,2,1,0:T(8,128)(2,1)S(1)}, u32[]{:S(2)}, u32[]{:S(2)}) %collective-permute-start.1) | collective-permute-done | bytes 786464 | tf_op jit(solution)/shard_map/ppermute | solution.py:131
  25.2 0.2 fusion.1
  25.4 0.0 copy-start.6
  25.5 1.8 %collective-permute-start.2 = (bf16[1,8,64,384]{3,2,1,0:T(8,128)(2,1)S(1)}, bf16[1,8,64,384]{3,2,1,0:T(8,128)(2,1)S(1)}, u32[]{:S(2)}, u32[]{:S(2)}) collective-permute-start(bf16[1,8,64,384]{3,2,1,0:T(8,128)(2,1)S(1)} %slice_bitcast_fusion.2), channel_id=1, source_target_pairs={{0,2},{1,3},{2,0},{3,1},{4,6},{5,7},{6,4},{7,5},{8,10},{9,11},{10,... | collective-permute-start | bytes 1179656 | tf_op jit(solution)/shard_map/ppermute | solution.py:131
  27.3 9.4 %collective-permute-done.2 = bf16[1,8,64,384]{3,2,1,0:T(8,128)(2,1)S(1)} collective-permute-done((bf16[1,8,64,384]{3,2,1,0:T(8,128)(2,1)S(1)}, bf16[1,8,64,384]{3,2,1,0:T(8,128)(2,1)S(1)}, u32[]{:S(2)}, u32[]{:S(2)}) %collective-permute-start.2) | collective-permute-done | bytes 393248 | tf_op jit(solution)/shard_map/ppermute | solution.py:131
  36.7 0.9 %fusion.3 = bf16[8,64,384]{2,1,0:T(8,128)(2,1)} fusion(bf16[1,8,64,384]{3,2,1,0:T(8,128)(2,1)S(1)} %collective-permute-done.2, bf16[1,2,8,64,384]{4,3,2,1,0:T(8,128)(2,1)S(1)} %fusion.1), kind=kLoop, calls=%fused_computation.9 | loop fusion | flops 786432 | bytes 1179648 | tf_op jit(solution)/shard_map/squeeze | solution.py:206
  37.5 6.1 %all-to-all-start = ((bf16[8,64,384]{2,1,0:T(8,128)(2,1)}), bf16[8,64,384]{2,1,0:T(8,128)(2,1)S(1)}, u32[]{:S(2)}, u32[]{:S(2)}) async-start(bf16[8,64,384]{2,1,0:T(8,128)(2,1)} %fusion.3), calls=%async_computation | async-start | bytes 786432 | tf_op jit(solution)/shard_map/all_to_all | solution.py:206
  43.6 0.6 %gather_fusion = s32[8]{0:T(128)S(1)} fusion(s32[8]{0:T(128)S(1)} %get-tuple-element.7, s32[1024]{0:T(1024)S(1)} %pad_clamp_fusion), kind=kCustom, calls=%fused_computation | custom fusion | bytes 96 | tf_op jit(solution)/shard_map/gather | solution.py:211
  44.3 10.5 %all-to-all-done = bf16[8,64,384]{2,1,0:T(8,128)(2,1)S(1)} async-done(((bf16[8,64,384]{2,1,0:T(8,128)(2,1)}), bf16[8,64,384]{2,1,0:T(8,128)(2,1)S(1)}, u32[]{:S(2)}, u32[]{:S(2)}) %all-to-all-start) | async-done | bytes 393248 | tf_op jit(solution)/shard_map/all_to_all | solution.py:206
  54.8 0.1 convert_element_type.47
  54.8 0.8 %select_reduce_fusion = bf16[2,64,384]{2,1,0:T(8,128)(2,1)} fusion(f32[8,64,384]{2,1,0:T(8,128)S(1)} %convert_element_type.47, pred[2,8]{1,0:T(4,128)(4,1)S(1)} %iota_compare_fusion), kind=kLoop, calls=%fused_computation.3 | loop fusion | flops 737280 | bytes 884752 | tf_op jit(solution)/shard_map/reduce_sum | solution.py:213
  (16 shorter events, 0.1 us)
Async XLA Ops:
  0.6 1.0 %copy-start.3 = (bf16[384,384]{1,0:T(8,128)(2,1)S(1)}, bf16[384,384]{1,0:T(8,128)(2,1)}, u32[]{:S(2)}) copy-start(bf16[384,384]{1,0:T(8,128)(2,1)} %q_ref.3) | copy-start | bytes 884740
  1.6 1.0 %copy-start.4 = (bf16[384,384]{1,0:T(8,128)(2,1)S(1)}, bf16[384,384]{1,0:T(8,128)(2,1)}, u32[]{:S(2)}) copy-start(bf16[384,384]{1,0:T(8,128)(2,1)} %g_ref.3) | copy-start | bytes 884740
  2.6 0.7 %copy-start.5 = (s32[8,2]{0,1:T(2,128)S(1)}, s32[8,2]{0,1:T(2,128)}, u32[]{:S(2)}) copy-start(s32[8,2]{0,1:T(2,128)} %param.10) | copy-start | bytes 196
  3.2 0.7 %copy-start.7 = (s32[3,2]{0,1:T(2,128)S(1)}, s32[3,2]{0,1:T(2,128)}, u32[]{:S(2)}) copy-start(s32[3,2]{0,1:T(2,128)} %param.9) | copy-start | bytes 76
  4.5 12.1 %collective-permute-start = (bf16[2,256,384]{2,1,0:T(8,128)(2,1)S(1)}, bf16[2,256,384]{2,1,0:T(8,128)(2,1)S(1)}, u32[]{:S(2)}, u32[]{:S(2)}) collective-permute-start(bf16[2,256,384]{2,1,0:T(8,128)(2,1)S(1)} %ship.1), channel_id=1, source_target_pairs={{0,4},{4,0},{8,12},{12,8},{16,20},{20,16},{24,28},{28,24},{1,5},{5... | collective-permute-start | bytes 1179656 | tf_op jit(solution)/shard_map/ppermute | solution.py:131
  7.6 1.4 %copy-start = (bf16[2,2,512,384]{3,2,1,0:T(8,128)(2,1)S(1)}, bf16[2,2,512,384]{3,2,1,0:T(8,128)(2,1)}, u32[]{:S(2)}) copy-start(bf16[2,2,512,384]{3,2,1,0:T(8,128)(2,1)} %cache_hbm.1) | copy-start | bytes 4718596
  9.0 7.7 %copy-start.1 = (bf16[1536,384]{1,0:T(8,128)(2,1)S(1)}, bf16[1536,384]{1,0:T(8,128)(2,1)}, u32[]{:S(2)}) copy-start(bf16[1536,384]{1,0:T(8,128)(2,1)} %wk_hbm.1) | copy-start | bytes 3538948
  9.0 7.7 %copy-start.2 = (bf16[1536,384]{1,0:T(8,128)(2,1)S(1)}, bf16[1536,384]{1,0:T(8,128)(2,1)}, u32[]{:S(2)}) copy-start(bf16[1536,384]{1,0:T(8,128)(2,1)} %wv_hbm.1) | copy-start | bytes 3538948
  22.8 2.4 %collective-permute-start.1 = (bf16[2,8,64,384]{3,2,1,0:T(8,128)(2,1)S(1)}, bf16[2,8,64,384]{3,2,1,0:T(8,128)(2,1)S(1)}, u32[]{:S(2)}, u32[]{:S(2)}) collective-permute-start(bf16[2,8,64,384]{3,2,1,0:T(8,128)(2,1)S(1)} %slice_bitcast_fusion), channel_id=1, source_target_pairs={{0,1},{1,0},{2,3},{3,2},{4,5},{5,4},{6,7},{7,6},{8,9},{9,8},{10,11... | collective-permute-start | bytes 2359304 | tf_op jit(solution)/shard_map/ppermute | solution.py:131
  25.4 18.9 %copy-start.6 = (s32[8,2]{0,1:T(2,128)S(1)}, s32[8,2]{0,1:T(2,128)}, u32[]{:S(2)}) copy-start(s32[8,2]{0,1:T(2,128)} %param.10) | copy-start | bytes 196
  25.5 11.2 %collective-permute-start.2 = (bf16[1,8,64,384]{3,2,1,0:T(8,128)(2,1)S(1)}, bf16[1,8,64,384]{3,2,1,0:T(8,128)(2,1)S(1)}, u32[]{:S(2)}, u32[]{:S(2)}) collective-permute-start(bf16[1,8,64,384]{3,2,1,0:T(8,128)(2,1)S(1)} %slice_bitcast_fusion.2), channel_id=1, source_target_pairs={{0,2},{1,3},{2,0},{3,1},{4,6},{5,7},{6,4},{7,5},{8,10},{9,11},{10,... | collective-permute-start | bytes 1179656 | tf_op jit(solution)/shard_map/ppermute | solution.py:131
  37.5 17.2 %all-to-all-start = ((bf16[8,64,384]{2,1,0:T(8,128)(2,1)}), bf16[8,64,384]{2,1,0:T(8,128)(2,1)S(1)}, u32[]{:S(2)}, u32[]{:S(2)}) async-start(bf16[8,64,384]{2,1,0:T(8,128)(2,1)} %fusion.3), calls=%async_computation | async-start | bytes 786432 | tf_op jit(solution)/shard_map/all_to_all | solution.py:206

commit v2 on v0

--- a/solution.py
+++ b/solution.py
@@ -1,18 +1,309 @@
+import functools
 import math
 
 import jax
 import jax.numpy as jnp
 from jax import lax
+from jax.experimental import pallas as pl
+from jax.experimental.pallas import tpu as pltpu
 from jax.sharding import PartitionSpec as P
 
-D = 1536
 DH = 128
 L = 512
 TILE = 128
 SPAN = 4
-
-
-def shards(queries, out_grad, tile_mask, slot_caption, caption_cache, key_weight, value_weight):
+F32 = jnp.float32
+BF16 = jnp.bfloat16
+INV_ROOT = 1.0 / math.sqrt(DH)
+KERNEL_LIMIT = 32 * 1024 * 1024
+SMALL_LIMIT = 8 * 1024 * 1024
+
+
+def dot(a, b, contract):
+    return lax.dot_general(a, b, ((contract[:1], contract[1:]), ((), ())), preferred_element_type=F32)
+
+
+def held(caps_ref, d, captions):
+    first, second = caps_ref[0, d], caps_ref[1, d]
+    single = jnp.logical_or(first == captions, second == captions)
+    return single, jnp.where(first == captions, second, first)
+
+
+def main_slot(caps_ref, d, captions):
+    single, _ = held(caps_ref, d, captions)
+    _, other = held(caps_ref, jnp.bitwise_xor(d, 1), captions)
+    first = caps_ref[0, d]
+    return jnp.where(single, jnp.where(first == captions, 1, 0), jnp.where(first == other, 1, 0))
+
+
+def backward(key, value, query, grad):
+    scores = dot(key, query, (1, 1))
+    top = jnp.max(scores, axis=0, keepdims=True)
+    exps = jnp.exp((scores - top) * INV_ROOT)
+    attention = exps * (1.0 / jnp.sum(exps, axis=0, keepdims=True))
+    attention_lo = attention.astype(BF16)
+    attention_grad = dot(value, grad, (1, 1))
+    row_dot = jnp.sum(attention_lo.astype(F32) * attention_grad, axis=0, keepdims=True)
+    score_lo = (attention * (attention_grad - row_dot)).astype(BF16)
+    return attention_lo, score_lo
+
+
+def fetch(pairs, sems):
+    copies = [pltpu.make_async_copy(a, b, sems.at[i]) for i, (a, b) in enumerate(pairs)]
+    for c in copies:
+        c.start()
+    return copies
+
+
+def stage_kernel(captions, tiles, mask_hbm, caps_hbm, q_hbm, g_hbm, *refs):
+    *sent, mains_ref, mask_ref, caps_ref, q_buf, g_buf, sems = refs
+    me = lax.axis_index("seq")
+    first = 1 - jnp.bitwise_and(me, 1)
+    rows = pl.ds(pl.multiple_of(first * TILE, TILE), (tiles - 1) * TILE)
+    copies = fetch(
+        [(mask_hbm, mask_ref), (caps_hbm, caps_ref), (q_hbm.at[rows], q_buf), (g_hbm.at[rows], g_buf)], sems
+    )
+    for c in copies:
+        c.wait()
+    mine = main_slot(caps_ref, me, captions)
+    for i, out in enumerate(sent):
+        keep = (mask_ref[mine, first + i] == 0).astype(F32).astype(BF16)
+        at = slice(i * TILE, (i + 1) * TILE)
+        out[0] = q_buf[at, :] * keep
+        out[1] = g_buf[at, :] * keep
+    for k in range(mains_ref.shape[0]):
+        source = jnp.bitwise_xor(me, k)
+        main = caps_ref[main_slot(caps_ref, source, captions), source]
+        mains_ref[k : k + 1, :] = jnp.full((1, mains_ref.shape[1]), main, jnp.int32)
+
+
+def own_kernel(
+    captions, tiles, heads, mask_hbm, caps_hbm, q_hbm, g_hbm, cache_hbm, dq_ref, part_ref, main_ref,
+    mask_ref, caps_ref, q_buf, g_buf, cache_buf, sems,
+):
+    me = lax.axis_index("seq")
+    pairs = [(mask_hbm, mask_ref), (caps_hbm, caps_ref), (q_hbm, q_buf), (g_hbm, g_buf)]
+    pairs += [(cache_hbm.at[:, :, :, pl.ds(h * DH, DH)], cache_buf.at[h]) for h in range(heads)]
+    copies = fetch(pairs, sems)
+    for c in copies[:4]:
+        c.wait()
+    mine = main_slot(caps_ref, me, captions)
+    slots = [jnp.where(mask_ref[1, t] == 1, 1, 0) for t in range(tiles)]
+    keeps = [(slot == mine).astype(F32).astype(BF16) for slot in slots]
+    for h in range(heads):
+        cols = slice(h * DH, (h + 1) * DH)
+        copies[4 + h].wait()
+        probs, grads, queries, outs = [], [], [], []
+        for t in range(tiles):
+            rows = slice(t * TILE, (t + 1) * TILE)
+            query, grad = q_buf[rows, cols], g_buf[rows, cols]
+            key, value = cache_buf[h, 0, slots[t]], cache_buf[h, 1, slots[t]]
+            attention_lo, score_lo = backward(key, value, query, grad)
+            dq_ref[rows, cols] = (dot(key.T, score_lo, (1, 0)) * INV_ROOT).T.astype(BF16)
+            probs.append(attention_lo)
+            grads.append(score_lo)
+            queries.append(query * keeps[t])
+            outs.append(grad * keeps[t])
+        part_ref[0, :, cols] = dot(jnp.concatenate(grads, axis=1), jnp.concatenate(queries, axis=0), (1, 0))
+        part_ref[1, :, cols] = dot(jnp.concatenate(probs, axis=1), jnp.concatenate(outs, axis=0), (1, 0))
+        main_ref[0, :, cols] = cache_buf[h, 0, mine]
+        main_ref[1, :, cols] = cache_buf[h, 1, mine]
+
+
+def shipped(heads, recv_ref, main_ref, h):
+    cols = slice(h * DH, (h + 1) * DH)
+    query, grad = recv_ref[0, :, cols], recv_ref[1, :, cols]
+    attention_lo, score_lo = backward(main_ref[0, :, cols], main_ref[1, :, cols], query, grad)
+    return dot(score_lo, query, (1, 0)), dot(attention_lo, grad, (1, 0))
+
+
+def shipped_kernel(heads, recv_ref, main_ref, part_ref, out_ref):
+    for h in range(heads):
+        cols = slice(h * DH, (h + 1) * DH)
+        dk, dv = shipped(heads, recv_ref, main_ref, h)
+        out_ref[0, :, cols] = part_ref[0, :, cols] + dk
+        out_ref[1, :, cols] = part_ref[1, :, cols] + dv
+
+
+def project(both_ref, wk_ref, wv_ref, rel, outs):
+    width = both_ref.shape[1] // 2
+    rows = pl.ds(pl.multiple_of(jnp.bitwise_xor(lax.axis_index("head"), rel) * width, width), width)
+    text = dot(both_ref[:, :width], wk_ref[rows, :], (1, 1)) + dot(both_ref[:, width:], wv_ref[rows, :], (1, 1))
+    text = text.astype(BF16)
+    at = 0
+    for out in outs:
+        out[...] = text[at : at + out.shape[0] * out.shape[1]].reshape(out.shape)
+        at += out.shape[0] * out.shape[1]
+
+
+def first_text_kernel(heads, blocks, chunks, recv_ref, main_ref, part_ref, wk_ref, wv_ref, both_ref, *outs):
+    me = lax.axis_index("seq")
+    width = heads * DH
+    block_rows = L // blocks
+    for h in range(heads):
+        cols = slice(h * DH, (h + 1) * DH)
+        dk, dv = shipped(heads, recv_ref, main_ref, h)
+        dk = ((part_ref[0, :, cols] + dk) * INV_ROOT).astype(BF16)
+        dv = (part_ref[1, :, cols] + dv).astype(BF16)
+        for s in range(blocks):
+            rows = pl.ds(pl.multiple_of(jnp.bitwise_xor(me, s) * block_rows, block_rows), block_rows)
+            both_ref[rows, h * DH : (h + 1) * DH] = dk[s * block_rows : (s + 1) * block_rows]
+            both_ref[rows, width + h * DH : width + (h + 1) * DH] = dv[s * block_rows : (s + 1) * block_rows]
+    project(both_ref, wk_ref, wv_ref, 3, outs[:chunks])
+    project(both_ref, wk_ref, wv_ref, 2, outs[chunks:])
+
+
+def second_text_kernel(chunks, both_ref, wk_ref, wv_ref, *outs):
+    project(both_ref, wk_ref, wv_ref, 1, outs[:chunks])
+    project(both_ref, wk_ref, wv_ref, 0, outs[chunks:])
+
+
+def add_kernel(a_ref, b_ref, out_ref):
+    out_ref[...] = (a_ref[...].astype(F32) + b_ref[...].astype(F32)).astype(BF16)
+
+
+def split_add_kernel(a_ref, b_ref, *outs):
+    for i, out in enumerate(outs):
+        out[...] = (a_ref[i].astype(F32) + b_ref[i].astype(F32)).astype(BF16)
+
+
+def final_kernel(mains_ref, *refs):
+    *blocks, out_ref = refs
+    captions = out_ref.shape[0]
+    totals = [0.0] * captions
+    for k, block in enumerate(blocks):
+        value = block[...].astype(F32)
+        main = jnp.tile(mains_ref[k : k + 1, :], (1, value.shape[1] // mains_ref.shape[1]))
+        for c in range(captions):
+            totals[c] += jnp.where(main == c, value, 0.0)
+    for c in range(captions):
+        out_ref[c] = totals[c].astype(BF16)
+
+
+def swap(array, axis, bit):
+    n = lax.axis_size(axis)
+    return lax.ppermute(array, axis, [(i, i ^ bit) for i in range(n)])
+
+
+def call(kernel, name, out_shape, operands, specs, scratch=(), limit=SMALL_LIMIT, hint_us=1.0):
+    vmem = pl.BlockSpec(memory_space=pltpu.VMEM)
+    return pl.pallas_call(
+        kernel,
+        out_shape=out_shape,
+        in_specs=specs,
+        out_specs=jax.tree.map(lambda _: vmem, out_shape),
+        scratch_shapes=scratch,
+        compiler_params=pltpu.CompilerParams(vmem_limit_bytes=limit),
+        cost_estimate=pl.CostEstimate(flops=0, bytes_accessed=int(hint_us * 3_600_000), transcendentals=0),
+        name=name,
+    )(*operands)
+
+
+def shards_pairs(queries, out_grad, tile_mask, slot_caption, caption_cache, key_weight, value_weight):
+    rows_here, width = queries.shape
+    heads = width // DH
+    tiles = rows_here // TILE
+    slots = tile_mask.shape[1]
+    seq_count, head_devices = lax.axis_size("seq"), lax.axis_size("head")
+    captions = seq_count // SPAN
+    block_rows = L // seq_count
+    chunks = 2
+    per = seq_count // chunks
+    held_back = [
+        pltpu.with_memory_space_constraint(x, pltpu.HBM)
+        for x in (tile_mask.T, slot_caption.T, queries, out_grad, caption_cache)
+    ]
+    mask_t, caps_t = held_back[:2]
+    vmem = pl.BlockSpec(memory_space=pltpu.VMEM)
+    hbm = pl.BlockSpec(memory_space=pltpu.HBM)
+    scalars = [pltpu.SMEM(mask_t.shape, jnp.int32), pltpu.SMEM(caps_t.shape, jnp.int32)]
+
+    def like(*shape, dtype=BF16):
+        return jax.ShapeDtypeStruct(shape, dtype)
+
+    *sent, mains = call(
+        functools.partial(stage_kernel, captions, tiles),
+        "stage",
+        (like(2, TILE, width),) * (tiles - 1) + (like(seq_count, 128, dtype=jnp.int32),),
+        held_back[:4],
+        [hbm] * 4,
+        scalars + [pltpu.VMEM(((tiles - 1) * TILE, width), BF16)] * 2 + [pltpu.SemaphoreType.DMA((4,))],
+    )
+    received = [swap(x, "seq", 1) for x in sent]
+
+    query_grad, part, main = call(
+        functools.partial(own_kernel, captions, tiles, heads),
+        "own_tiles",
+        (like(rows_here, width), like(2, L, width, dtype=F32), like(2, L, width)),
+        held_back,
+        [hbm] * 5,
+        scalars
+        + [pltpu.VMEM((rows_here, width), BF16)] * 2
+        + [pltpu.VMEM((heads, 2, slots, L, DH), BF16), pltpu.SemaphoreType.DMA((4 + heads,))],
+        limit=KERNEL_LIMIT,
+        hint_us=5.0,
+    )
+    for tile in received[:-1]:
+        part = call(
+            functools.partial(shipped_kernel, heads),
+            "shipped_tile",
+            like(2, L, width, dtype=F32),
+            (tile, main, part),
+            [vmem] * 3,
+            limit=KERNEL_LIMIT,
+            hint_us=2.0,
+        )
+    piece = like(per, block_rows, width)
+    both, *pieces = call(
+        functools.partial(first_text_kernel, heads, seq_count, chunks),
+        "first_text",
+        (like(L, 2 * width),) + (piece,) * (2 * chunks),
+        (received[-1], main, part, key_weight, value_weight),
+        [vmem] * 5,
+        limit=KERNEL_LIMIT,
+        hint_us=3.0,
+    )
+    sent_x, kept_x = pieces[:chunks], pieces[chunks:]
+    pieces = call(
+        functools.partial(second_text_kernel, chunks),
+        "second_text",
+        (piece,) * (2 * chunks),
+        (both, key_weight, value_weight),
+        [vmem] * 3,
+        limit=KERNEL_LIMIT,
+        hint_us=1.0,
+    )
+    sent_own, kept_own = pieces[:chunks], pieces[chunks:]
+
+    def add(a, b):
+        return call(add_kernel, "add", like(*a.shape), (a, b), [vmem] * 2)
+
+    order = range(chunks - 1, -1, -1)
+    far = {c: add(kept_x[c], swap(sent_x[c], "head", 1)) for c in order}
+    near = {c: add(kept_own[c], swap(sent_own[c], "head", 1)) for c in order}
+    arrived = [None] * seq_count
+    before = None
+    for c in order:
+        if before is not None:
+            before, far[c] = lax.optimization_barrier((before, far[c]))
+        if before is not None:
+            finish(before, near, arrived, per, call, like, vmem, c + 1)
+        before = swap(far[c], "head", 2)
+    finish(before, near, arrived, per, call, like, vmem, 0)
+    text_grad = call(
+        final_kernel, "final", like(captions, block_rows, width), (mains, *arrived), [vmem] * (1 + seq_count)
+    )
+    return query_grad, text_grad
+
+
+def finish(came, near, arrived, per, call, like, vmem, c):
+    blocks = call(split_add_kernel, "split_add", (like(*came.shape[1:]),) * per, (near[c], came), [vmem] * 2)
+    for i in range(per):
+        k = c * per + i
+        arrived[k] = swap(blocks[i], "seq", k) if k else blocks[i]
+
+
+def shards_general(queries, out_grad, tile_mask, slot_caption, caption_cache, key_weight, value_weight):
     highest = lax.Precision.HIGHEST
     rows_here, width = queries.shape
     head_count = width // DH
@@ -67,6 +358,7 @@
     seq_count = lax.axis_size("seq")
     caption_count = seq_count // SPAN
     block_rows = L // seq_count
+    features = key_weight.shape[0]
     flat_table = slot_caption.T.reshape(1, slot_count * seq_count)
     selector = (flat_table == jnp.arange(caption_count, dtype=jnp.int32)[:, None]).astype(
         jnp.float32
@@ -78,7 +370,7 @@
     merged = merged.reshape(2, caption_count * block_rows, width)
     summed = jnp.dot(merged[0], key_weight.astype(jnp.float32).T, precision=highest)
     summed = summed + jnp.dot(merged[1], value_weight.astype(jnp.float32).T, precision=highest)
-    summed = summed.reshape(caption_count, block_rows, D)
+    summed = summed.reshape(caption_count, block_rows, features)
     text_grad = lax.psum_scatter(summed, "head", scatter_dimension=2, tiled=True).astype(
         jnp.bfloat16
     )
@@ -86,6 +378,8 @@
 
 
 def solution(mesh):
+    seq_count, head_devices = mesh.shape["seq"], mesh.shape["head"]
+    pairs = seq_count // SPAN <= 2 and seq_count % 2 == 0 and head_devices & (head_devices - 1) == 0
     placed = (
         P("seq", "head"),
         P("seq", "head"),
@@ -96,7 +390,7 @@
         P(None, "head"),
     )
     return jax.shard_map(
-        shards,
+        shards_pairs if pairs else shards_general,
         mesh=mesh,
         in_specs=placed,
         out_specs=(P("seq", "head"), P(None, "seq", "head")),

time: 152 us -> 43.4 us (0.29)
  waiting for transfers between devices: 56.3 us -> 9.56 us
  matrix products: 42.9 us -> 0 us
  local copies, waits for them, and re-layouts: 25.2 us -> 0.01 us
  Pallas kernels: 0 us -> 14.7 us
  between operations: 14.2 us -> 0.75 us
  starting transfers between devices: 7.44 us -> 18.2 us
  other arithmetic: 5.23 us -> 0 us
    dot_general x13 -> x0, matrix products: 42.9 us -> none  [the longest x1 8.72 us: shards(): jnp.einsum('ts,tjhe->sjhe', slot_onehot, value_pieces, precision=highest)]
    all_to_all x1 -> x0, waiting for transfers between devices: 37 us -> none  [shards(): lax.all_to_all(payload, 'seq', split_axis=2, concat_axis=2, tiled=True)]
    reduce_scatter x1 -> x0, waiting for transfers between devices: 19.3 us -> none  [shards(): lax.psum_scatter(summed, 'head', scatter_dimension=2, tiled=True)]
    ppermute x0 -> x15, starting transfers between devices: none -> 18.2 us  [swap(): return lax.ppermute(array, axis, [(i, i ^ bit) for i in range(n)])]
    pallas_call x0 -> x12, Pallas kernels: none -> 14.7 us  [call(): pl.pallas_call(kernel, out_shape=out_shape, in_specs=specs, out_specs=jax...]
    ppermute x0 -> x15, waiting for transfers between devices: none -> 9.56 us  [swap(): return lax.ppermute(array, axis, [(i, i ^ bit) for i in range(n)])]
    convert_element_type x5 -> x0, local copies, waits for them, and re-layouts: 8.92 us -> none  [the longest x1 3.61 us: shards(): value_rows.astype(jnp.bfloat16).reshape(tile_count, L, head_count, DH)]
    all_to_all x1 -> x0, starting transfers between devices: 7.4 us -> none  [shards(): lax.all_to_all(payload, 'seq', split_axis=2, concat_axis=2, tiled=True)]
  transfers between devices with their start and end apart: 2 -> 15, of which waited for: 2 -> 6; matrix products, arithmetic and copies ran while one was open for 2% -> 0% of each run, Pallas kernels for 0% -> 23%
where the time goes in v2:
time: 43.4 us; the launch traced here: 43.2 us
  starting transfers between devices  18.2 us (42%)
  Pallas kernels  14.7 us (34%)
  waiting for transfers between devices  9.56 us (22%)
  between operations  0.75 us (2%)
    ppermute x15, starting transfers between devices, swap(): return lax.ppermute(array, axis, [(i, i ^ bit) for i in range(n)])  18.2 us
    pallas_call x12, Pallas kernels, call(): pl.pallas_call(kernel, out_shape=out_shape, in_specs=specs, out_specs=jax...  14.7 us
    ppermute x15, waiting for transfers between devices, swap(): return lax.ppermute(array, axis, [(i, i ^ bit) for i in range(n)])  9.56 us
  transfers between devices with their start and end apart: 15, of which 6 were waited for; matrix products, arithmetic and copies ran while one was open for 0% of the time, Pallas kernels for 23%

profile of v2, /device:TPU:0, one launch (start us, length us, event | category | flops | bytes accessed | tf_op | source)
XLA Modules:
  0.0 43.2 jit_solution(6044189842463052527)
XLA Ops:
  0.6 1.1 %stage.1 = (bf16[2,128,384]{2,1,0:T(8,128)(2,1)S(1)}, bf16[2,128,384]{2,1,0:T(8,128)(2,1)S(1)}, s32[8,128]{1,0:T(8,128)S(1)}) custom-call(s32[2,3]{1,0:T(2,128)} %bitcast.2, s32[2,8]{1,0:T(2,128)} %bitcast.4, bf16[384,384]{1,0:T(8,128)(2,1)} %q_hbm.3, bf16[384,384]{1,0:T(8,128)(2,1)} %g_hbm.3), custom_call_target="tpu_custom_call" | custom-call | bytes 3600000 | tf_op jit(solution)/shard_map/stage/pallas_call | solution.py:190
  1.8 3.0 %collective-permute-start.1 = (bf16[2,128,384]{2,1,0:T(8,128)(2,1)S(1)}, bf16[2,128,384]{2,1,0:T(8,128)(2,1)S(1)}, u32[]{:S(2)}, u32[]{:S(2)}) collective-permute-start(bf16[2,128,384]{2,1,0:T(8,128)(2,1)S(1)} %get-tuple-element.31), channel_id=1, source_target_pairs={{0,4},{4,0},{8,12},{12,8},{16,20},{20,16},{24,28},{28,24},{1,5},{5... | collective-permute-start | bytes 589832 | tf_op jit(solution)/shard_map/ppermute | solution.py:185
  4.8 0.1 collective-permute-start
  4.9 7.1 %own_tiles.1 = (bf16[384,384]{1,0:T(8,128)(2,1)}, f32[2,512,384]{2,1,0:T(8,128)S(1)}, bf16[2,512,384]{2,1,0:T(8,128)(2,1)S(1)}) custom-call(s32[2,3]{1,0:T(2,128)} %bitcast.3, s32[2,8]{1,0:T(2,128)} %bitcast.5, bf16[384,384]{1,0:T(8,128)(2,1)} %q_hbm.3, bf16[384,384]{1,0:T(8,128)(2,1)} %g_hbm.3, bf16[2,2,512,384]{3,2,1,0:T(8,128)(2,1)} %cache_hbm.1), custom_call_target="tpu_custom_call" | custom-call | bytes 18000000 | tf_op jit(solution)/shard_map/own_tiles/pallas_call | solution.py:190
  12.1 1.5 %shipped_tile.1.part_ref = f32[2,512,384]{2,1,0:T(8,128)S(1)} custom-call(bf16[2,128,384]{2,1,0:T(8,128)(2,1)S(1)} %collective-permute-done.1.recv_ref, bf16[2,512,384]{2,1,0:T(8,128)(2,1)S(1)} %get-tuple-element.30.main_ref, f32[2,512,384]{2,1,0:T(8,128)S(1)} %get-tuple-element.32.part_ref), custom_call_target="tpu_custom_call" | custom-call | bytes 7200000 | tf_op jit(solution)/shard_map/shipped_tile/pallas_call | solution.py:190
  13.6 0.3 collective-permute-done.recv_ref
  13.9 2.6 %first_text.1 = (bf16[512,768]{1,0:T(8,128)(2,1)S(1)}, bf16[4,64,384]{2,1,0:T(8,128)(2,1)S(1)}, bf16[4,64,384]{2,1,0:T(8,128)(2,1)S(1)}, bf16[4,64,384]{2,1,0:T(8,128)(2,1)S(1)}, bf16[4,64,384]{2,1,0:T(8,128)(2,1)S(1)}) custom-call(bf16[2,128,384]{2,1,0:T(8,128)(2,1)S(1)} %collective-permute-done.recv_ref, ...), custom_call_target="tpu_custom_call" | custom-call | bytes 10800000 | tf_op jit(solution)/shard_map/first_text/pallas_call | solution.py:190
  16.6 0.5 %collective-permute-start.5 = (bf16[4,64,384]{2,1,0:T(8,128)(2,1)S(1)}, bf16[4,64,384]{2,1,0:T(8,128)(2,1)S(1)}, u32[]{:S(2)}, u32[]{:S(2)}) collective-permute-start(bf16[4,64,384]{2,1,0:T(8,128)(2,1)S(1)} %get-tuple-element.39), channel_id=1, source_target_pairs={{0,1},{1,0},{2,3},{3,2},{4,5},{5,4},{6,7},{7,6},{8,9},{9,8},{10,11... | collective-permute-start | bytes 589832 | tf_op jit(solution)/shard_map/ppermute | solution.py:185
  17.1 0.9 %collective-permute-done.3.b_ref = bf16[4,64,384]{2,1,0:T(8,128)(2,1)S(1)} collective-permute-done((bf16[4,64,384]{2,1,0:T(8,128)(2,1)S(1)}, bf16[4,64,384]{2,1,0:T(8,128)(2,1)S(1)}, u32[]{:S(2)}, u32[]{:S(2)}) %collective-permute-start.3) | collective-permute-done | bytes 196640 | tf_op jit(solution)/shard_map/ppermute | solution.py:185
  18.1 1.8 %collective-permute-start.4 = (bf16[4,64,384]{2,1,0:T(8,128)(2,1)S(1)}, bf16[4,64,384]{2,1,0:T(8,128)(2,1)S(1)}, u32[]{:S(2)}, u32[]{:S(2)}) collective-permute-start(bf16[4,64,384]{2,1,0:T(8,128)(2,1)S(1)} %add.5), channel_id=1, source_target_pairs={{0,2},{1,3},{2,0},{3,1},{4,6},{5,7},{6,4},{7,5},{8,10},{9,11},{10,... | collective-permute-start | bytes 589832 | tf_op jit(solution)/shard_map/ppermute | solution.py:185
  19.9 1.1 %second_text.1 = (bf16[4,64,384]{2,1,0:T(8,128)(2,1)S(1)}, bf16[4,64,384]{2,1,0:T(8,128)(2,1)S(1)}, bf16[4,64,384]{2,1,0:T(8,128)(2,1)S(1)}, bf16[4,64,384]{2,1,0:T(8,128)(2,1)S(1)}) custom-call(bf16[512,768]{1,0:T(8,128)(2,1)S(1)} %get-tuple-element.33.both_ref, bf16[1536,384]{1,0:T(8,128)(2,1)S(1)} %copy-done, bf16[1536,384]{1,0:T(8,128)(2,1)S(1)} %copy-done.1), custom_call_target="tpu_custom_call" | custom-call | bytes 3600000 | tf_op jit(solution)/shard_map/second_text/pallas_call | solution.py:190
  21.1 0.5 %collective-permute-start.2 = (bf16[4,64,384]{2,1,0:T(8,128)(2,1)S(1)}, bf16[4,64,384]{2,1,0:T(8,128)(2,1)S(1)}, u32[]{:S(2)}, u32[]{:S(2)}) collective-permute-start(bf16[4,64,384]{2,1,0:T(8,128)(2,1)S(1)} %get-tuple-element.35), channel_id=1, source_target_pairs={{0,1},{1,0},{2,3},{3,2},{4,5},{5,4},{6,7},{7,6},{8,9},{9,8},{10,11... | collective-permute-start | bytes 589832 | tf_op jit(solution)/shard_map/ppermute | solution.py:185
  21.7 3.5 %collective-permute-done.4.b_ref = bf16[4,64,384]{2,1,0:T(8,128)(2,1)S(1)} collective-permute-done((bf16[4,64,384]{2,1,0:T(8,128)(2,1)S(1)}, bf16[4,64,384]{2,1,0:T(8,128)(2,1)S(1)}, u32[]{:S(2)}, u32[]{:S(2)}) %collective-permute-start.4) | collective-permute-done | bytes 196640 | tf_op jit(solution)/shard_map/ppermute | solution.py:185
  25.1 1.7 %collective-permute-start.6 = (bf16[4,64,384]{2,1,0:T(8,128)(2,1)S(1)}, bf16[4,64,384]{2,1,0:T(8,128)(2,1)S(1)}, u32[]{:S(2)}, u32[]{:S(2)}) collective-permute-start(bf16[4,64,384]{2,1,0:T(8,128)(2,1)S(1)} %add.6), channel_id=1, source_target_pairs={{0,2},{1,3},{2,0},{3,1},{4,6},{5,7},{6,4},{7,5},{8,10},{9,11},{10,... | collective-permute-start | bytes 589832 | tf_op jit(solution)/shard_map/ppermute | solution.py:185
  27.0 2.7 %collective-permute-start.11 = (bf16[64,384]{1,0:T(8,128)(2,1)S(1)}, bf16[64,384]{1,0:T(8,128)(2,1)S(1)}, u32[]{:S(2)}, u32[]{:S(2)}) collective-permute-start(bf16[64,384]{1,0:T(8,128)(2,1)S(1)} %get-tuple-element.48), channel_id=1, source_target_pairs={{0,16},{4,20},{8,24},{12,28},{16,0},{20,4},{24,8},{28,12},{1,17},{... | collective-permute-start | bytes 147464 | tf_op jit(solution)/shard_map/ppermute | solution.py:185
  29.6 1.3 %collective-permute-start.12 = (bf16[64,384]{1,0:T(8,128)(2,1)S(1)}, bf16[64,384]{1,0:T(8,128)(2,1)S(1)}, u32[]{:S(2)}, u32[]{:S(2)}) collective-permute-start(bf16[64,384]{1,0:T(8,128)(2,1)S(1)} %get-tuple-element.49), channel_id=1, source_target_pairs={{0,20},{4,16},{8,28},{12,24},{16,4},{20,0},{24,12},{28,8},{1,21},{... | collective-permute-start | bytes 147464 | tf_op jit(solution)/shard_map/ppermute | solution.py:185
  31.0 3.7 %collective-permute-start.13 = (bf16[64,384]{1,0:T(8,128)(2,1)S(1)}, bf16[64,384]{1,0:T(8,128)(2,1)S(1)}, u32[]{:S(2)}, u32[]{:S(2)}) collective-permute-start(bf16[64,384]{1,0:T(8,128)(2,1)S(1)} %get-tuple-element.50), channel_id=1, source_target_pairs={{0,24},{4,28},{8,16},{12,20},{16,8},{20,12},{24,0},{28,4},{1,25},{... | collective-permute-start | bytes 147464 | tf_op jit(solution)/shard_map/ppermute | solution.py:185
  34.6 0.2 collective-permute-start.14
  34.9 1.6 %collective-permute-start.7 = (bf16[64,384]{1,0:T(8,128)(2,1)S(1)}, bf16[64,384]{1,0:T(8,128)(2,1)S(1)}, u32[]{:S(2)}, u32[]{:S(2)}) collective-permute-start(bf16[64,384]{1,0:T(8,128)(2,1)S(1)} %get-tuple-element.42), channel_id=1, source_target_pairs={{0,4},{4,0},{8,12},{12,8},{16,20},{20,16},{24,28},{28,24},{1,5},{5... | collective-permute-start | bytes 147464 | tf_op jit(solution)/shard_map/ppermute | solution.py:185
  36.4 0.9 %collective-permute-done.12.refs_5_ = bf16[64,384]{1,0:T(8,128)(2,1)S(1)} collective-permute-done((bf16[64,384]{1,0:T(8,128)(2,1)S(1)}, bf16[64,384]{1,0:T(8,128)(2,1)S(1)}, u32[]{:S(2)}, u32[]{:S(2)}) %collective-permute-start.12) | collective-permute-done | bytes 49184 | tf_op jit(solution)/shard_map/ppermute | solution.py:185
  37.3 1.1 %collective-permute-start.9 = (bf16[64,384]{1,0:T(8,128)(2,1)S(1)}, bf16[64,384]{1,0:T(8,128)(2,1)S(1)}, u32[]{:S(2)}, u32[]{:S(2)}) collective-permute-start(bf16[64,384]{1,0:T(8,128)(2,1)S(1)} %get-tuple-element.44), channel_id=1, source_target_pairs={{0,12},{4,8},{8,4},{12,0},{16,28},{20,24},{24,20},{28,16},{1,13},{... | collective-permute-start | bytes 147464 | tf_op jit(solution)/shard_map/ppermute | solution.py:185
  38.4 3.5 %collective-permute-done.14.refs_7_ = bf16[64,384]{1,0:T(8,128)(2,1)S(1)} collective-permute-done((bf16[64,384]{1,0:T(8,128)(2,1)S(1)}, bf16[64,384]{1,0:T(8,128)(2,1)S(1)}, u32[]{:S(2)}, u32[]{:S(2)}) %collective-permute-start.14) | collective-permute-done | bytes 49184 | tf_op jit(solution)/shard_map/ppermute | solution.py:185
  42.0 0.4 %collective-permute-done.9.refs_3_ = bf16[64,384]{1,0:T(8,128)(2,1)S(1)} collective-permute-done((bf16[64,384]{1,0:T(8,128)(2,1)S(1)}, bf16[64,384]{1,0:T(8,128)(2,1)S(1)}, u32[]{:S(2)}, u32[]{:S(2)}) %collective-permute-start.9) | collective-permute-done | bytes 49184 | tf_op jit(solution)/shard_map/ppermute | solution.py:185
  42.4 0.8 %final.1 = bf16[2,64,384]{2,1,0:T(8,128)(2,1)} custom-call(s32[8,128]{1,0:T(8,128)S(1)} %get-tuple-element.28.mains_ref, bf16[64,384]{1,0:T(8,128)(2,1)S(1)} %get-tuple-element.41.refs_0_, bf16[64,384]{1,0:T(8,128)(2,1)S(1)} %collective-permute-done.7.refs_1_, bf16[64,384]{1,0:T(8,128)(2,1)S(1)} %collective-permute-done.8.refs_2_, ...), custom_call_target="tpu_custom_call" | custom-call | bytes 3600000 | tf_op jit(solution)/shard_map/final/pallas_call | solution.py:190
  (22 shorter events, 0.5 us)
Async XLA Ops:
  1.8 10.3 %collective-permute-start.1 = (bf16[2,128,384]{2,1,0:T(8,128)(2,1)S(1)}, bf16[2,128,384]{2,1,0:T(8,128)(2,1)S(1)}, u32[]{:S(2)}, u32[]{:S(2)}) collective-permute-start(bf16[2,128,384]{2,1,0:T(8,128)(2,1)S(1)} %get-tuple-element.31), channel_id=1, source_target_pairs={{0,4},{4,0},{8,12},{12,8},{16,20},{20,16},{24,28},{28,24},{1,5},{5... | collective-permute-start | bytes 589832 | tf_op jit(solution)/shard_map/ppermute | solution.py:185
  4.8 9.1 %collective-permute-start = (bf16[2,128,384]{2,1,0:T(8,128)(2,1)S(1)}, bf16[2,128,384]{2,1,0:T(8,128)(2,1)S(1)}, u32[]{:S(2)}, u32[]{:S(2)}) collective-permute-start(bf16[2,128,384]{2,1,0:T(8,128)(2,1)S(1)} %get-tuple-element.29), channel_id=1, source_target_pairs={{0,4},{4,0},{8,12},{12,8},{16,20},{20,16},{24,28},{28,24},{1,5},{5... | collective-permute-start | bytes 589832 | tf_op jit(solution)/shard_map/ppermute | solution.py:185
  12.0 1.9 %copy-start = (bf16[1536,384]{1,0:T(8,128)(2,1)S(1)}, bf16[1536,384]{1,0:T(8,128)(2,1)}, u32[]{:S(2)}) copy-start(bf16[1536,384]{1,0:T(8,128)(2,1)} %wk_ref.3) | copy-start | bytes 3538948
  12.0 1.9 %copy-start.1 = (bf16[1536,384]{1,0:T(8,128)(2,1)S(1)}, bf16[1536,384]{1,0:T(8,128)(2,1)}, u32[]{:S(2)}) copy-start(bf16[1536,384]{1,0:T(8,128)(2,1)} %wv_ref.3) | copy-start | bytes 3538948
  16.6 1.5 %collective-permute-start.3 = (bf16[4,64,384]{2,1,0:T(8,128)(2,1)S(1)}, bf16[4,64,384]{2,1,0:T(8,128)(2,1)S(1)}, u32[]{:S(2)}, u32[]{:S(2)}) collective-permute-start(bf16[4,64,384]{2,1,0:T(8,128)(2,1)S(1)} %get-tuple-element.37), channel_id=1, source_target_pairs={{0,1},{1,0},{2,3},{3,2},{4,5},{5,4},{6,7},{7,6},{8,9},{9,8},{10,11... | collective-permute-start | bytes 589832 | tf_op jit(solution)/shard_map/ppermute | solution.py:185
  16.6 5.0 %collective-permute-start.5 = (bf16[4,64,384]{2,1,0:T(8,128)(2,1)S(1)}, bf16[4,64,384]{2,1,0:T(8,128)(2,1)S(1)}, u32[]{:S(2)}, u32[]{:S(2)}) collective-permute-start(bf16[4,64,384]{2,1,0:T(8,128)(2,1)S(1)} %get-tuple-element.39), channel_id=1, source_target_pairs={{0,1},{1,0},{2,3},{3,2},{4,5},{5,4},{6,7},{7,6},{8,9},{9,8},{10,11... | collective-permute-start | bytes 589832 | tf_op jit(solution)/shard_map/ppermute | solution.py:185
  18.1 7.0 %collective-permute-start.4 = (bf16[4,64,384]{2,1,0:T(8,128)(2,1)S(1)}, bf16[4,64,384]{2,1,0:T(8,128)(2,1)S(1)}, u32[]{:S(2)}, u32[]{:S(2)}) collective-permute-start(bf16[4,64,384]{2,1,0:T(8,128)(2,1)S(1)} %add.5), channel_id=1, source_target_pairs={{0,2},{1,3},{2,0},{3,1},{4,6},{5,7},{6,4},{7,5},{8,10},{9,11},{10,... | collective-permute-start | bytes 589832 | tf_op jit(solution)/shard_map/ppermute | solution.py:185
  21.0 5.8 %collective-permute-start.10 = (bf16[4,64,384]{2,1,0:T(8,128)(2,1)S(1)}, bf16[4,64,384]{2,1,0:T(8,128)(2,1)S(1)}, u32[]{:S(2)}, u32[]{:S(2)}) collective-permute-start(bf16[4,64,384]{2,1,0:T(8,128)(2,1)S(1)} %get-tuple-element.46), channel_id=1, source_target_pairs={{0,1},{1,0},{2,3},{3,2},{4,5},{5,4},{6,7},{7,6},{8,9},{9,8},{10,11... | collective-permute-start | bytes 589832 | tf_op jit(solution)/shard_map/ppermute | solution.py:185
  21.1 9.8 %collective-permute-start.2 = (bf16[4,64,384]{2,1,0:T(8,128)(2,1)S(1)}, bf16[4,64,384]{2,1,0:T(8,128)(2,1)S(1)}, u32[]{:S(2)}, u32[]{:S(2)}) collective-permute-start(bf16[4,64,384]{2,1,0:T(8,128)(2,1)S(1)} %get-tuple-element.35), channel_id=1, source_target_pairs={{0,1},{1,0},{2,3},{3,2},{4,5},{5,4},{6,7},{7,6},{8,9},{9,8},{10,11... | collective-permute-start | bytes 589832 | tf_op jit(solution)/shard_map/ppermute | solution.py:185
  25.1 9.7 %collective-permute-start.6 = (bf16[4,64,384]{2,1,0:T(8,128)(2,1)S(1)}, bf16[4,64,384]{2,1,0:T(8,128)(2,1)S(1)}, u32[]{:S(2)}, u32[]{:S(2)}) collective-permute-start(bf16[4,64,384]{2,1,0:T(8,128)(2,1)S(1)} %add.6), channel_id=1, source_target_pairs={{0,2},{1,3},{2,0},{3,1},{4,6},{5,7},{6,4},{7,5},{8,10},{9,11},{10,... | collective-permute-start | bytes 589832 | tf_op jit(solution)/shard_map/ppermute | solution.py:185
  27.0 9.5 %collective-permute-start.11 = (bf16[64,384]{1,0:T(8,128)(2,1)S(1)}, bf16[64,384]{1,0:T(8,128)(2,1)S(1)}, u32[]{:S(2)}, u32[]{:S(2)}) collective-permute-start(bf16[64,384]{1,0:T(8,128)(2,1)S(1)} %get-tuple-element.48), channel_id=1, source_target_pairs={{0,16},{4,20},{8,24},{12,28},{16,0},{20,4},{24,8},{28,12},{1,17},{... | collective-permute-start | bytes 147464 | tf_op jit(solution)/shard_map/ppermute | solution.py:185
  29.6 7.7 %collective-permute-start.12 = (bf16[64,384]{1,0:T(8,128)(2,1)S(1)}, bf16[64,384]{1,0:T(8,128)(2,1)S(1)}, u32[]{:S(2)}, u32[]{:S(2)}) collective-permute-start(bf16[64,384]{1,0:T(8,128)(2,1)S(1)} %get-tuple-element.49), channel_id=1, source_target_pairs={{0,20},{4,16},{8,28},{12,24},{16,4},{20,0},{24,12},{28,8},{1,21},{... | collective-permute-start | bytes 147464 | tf_op jit(solution)/shard_map/ppermute | solution.py:185
  31.0 7.5 %collective-permute-start.13 = (bf16[64,384]{1,0:T(8,128)(2,1)S(1)}, bf16[64,384]{1,0:T(8,128)(2,1)S(1)}, u32[]{:S(2)}, u32[]{:S(2)}) collective-permute-start(bf16[64,384]{1,0:T(8,128)(2,1)S(1)} %get-tuple-element.50), channel_id=1, source_target_pairs={{0,24},{4,28},{8,16},{12,20},{16,8},{20,12},{24,0},{28,4},{1,25},{... | collective-permute-start | bytes 147464 | tf_op jit(solution)/shard_map/ppermute | solution.py:185
  34.6 7.3 %collective-permute-start.14 = (bf16[64,384]{1,0:T(8,128)(2,1)S(1)}, bf16[64,384]{1,0:T(8,128)(2,1)S(1)}, u32[]{:S(2)}, u32[]{:S(2)}) collective-permute-start(bf16[64,384]{1,0:T(8,128)(2,1)S(1)} %get-tuple-element.51), channel_id=1, source_target_pairs={{0,28},{4,24},{8,20},{12,16},{16,12},{20,8},{24,4},{28,0},{1,29},{... | collective-permute-start | bytes 147464 | tf_op jit(solution)/shard_map/ppermute | solution.py:185
  34.9 7.1 %collective-permute-start.7 = (bf16[64,384]{1,0:T(8,128)(2,1)S(1)}, bf16[64,384]{1,0:T(8,128)(2,1)S(1)}, u32[]{:S(2)}, u32[]{:S(2)}) collective-permute-start(bf16[64,384]{1,0:T(8,128)(2,1)S(1)} %get-tuple-element.42), channel_id=1, source_target_pairs={{0,4},{4,0},{8,12},{12,8},{16,20},{20,16},{24,28},{28,24},{1,5},{5... | collective-permute-start | bytes 147464 | tf_op jit(solution)/shard_map/ppermute | solution.py:185
  36.4 5.5 %collective-permute-start.8 = (bf16[64,384]{1,0:T(8,128)(2,1)S(1)}, bf16[64,384]{1,0:T(8,128)(2,1)S(1)}, u32[]{:S(2)}, u32[]{:S(2)}) collective-permute-start(bf16[64,384]{1,0:T(8,128)(2,1)S(1)} %get-tuple-element.43), channel_id=1, source_target_pairs={{0,8},{4,12},{8,0},{12,4},{16,24},{20,28},{24,16},{28,20},{1,9},{5... | collective-permute-start | bytes 147464 | tf_op jit(solution)/shard_map/ppermute | solution.py:185
  37.3 5.1 %collective-permute-start.9 = (bf16[64,384]{1,0:T(8,128)(2,1)S(1)}, bf16[64,384]{1,0:T(8,128)(2,1)S(1)}, u32[]{:S(2)}, u32[]{:S(2)}) collective-permute-start(bf16[64,384]{1,0:T(8,128)(2,1)S(1)} %get-tuple-element.44), channel_id=1, source_target_pairs={{0,12},{4,8},{8,4},{12,0},{16,28},{20,24},{24,20},{28,16},{1,13},{... | collective-permute-start | bytes 147464 | tf_op jit(solution)/shard_map/ppermute | solution.py:185

commit v3 on v2

--- a/solution.py
+++ b/solution.py
@@ -15,6 +15,7 @@
 F32 = jnp.float32
 BF16 = jnp.bfloat16
 INV_ROOT = 1.0 / math.sqrt(DH)
+CHUNK = 2
 KERNEL_LIMIT = 32 * 1024 * 1024
 SMALL_LIMIT = 8 * 1024 * 1024
 
@@ -78,8 +79,8 @@
 
 
 def own_kernel(
-    captions, tiles, heads, mask_hbm, caps_hbm, q_hbm, g_hbm, cache_hbm, dq_ref, part_ref, main_ref,
-    mask_ref, caps_ref, q_buf, g_buf, cache_buf, sems,
+    captions, tiles, heads, mask_hbm, caps_hbm, q_hbm, g_hbm, cache_hbm, dq_hbm, part_ref, main_ref,
+    mask_ref, caps_ref, q_buf, g_buf, cache_buf, dq_buf, sems, out_sems,
 ):
     me = lax.axis_index("seq")
     pairs = [(mask_hbm, mask_ref), (caps_hbm, caps_ref), (q_hbm, q_buf), (g_hbm, g_buf)]
@@ -90,6 +91,7 @@
     mine = main_slot(caps_ref, me, captions)
     slots = [jnp.where(mask_ref[1, t] == 1, 1, 0) for t in range(tiles)]
     keeps = [(slot == mine).astype(F32).astype(BF16) for slot in slots]
+    stores = []
     for h in range(heads):
         cols = slice(h * DH, (h + 1) * DH)
         copies[4 + h].wait()
@@ -99,15 +101,26 @@
             query, grad = q_buf[rows, cols], g_buf[rows, cols]
             key, value = cache_buf[h, 0, slots[t]], cache_buf[h, 1, slots[t]]
             attention_lo, score_lo = backward(key, value, query, grad)
-            dq_ref[rows, cols] = (dot(key.T, score_lo, (1, 0)) * INV_ROOT).T.astype(BF16)
             probs.append(attention_lo)
             grads.append(score_lo)
             queries.append(query * keeps[t])
             outs.append(grad * keeps[t])
-        part_ref[0, :, cols] = dot(jnp.concatenate(grads, axis=1), jnp.concatenate(queries, axis=0), (1, 0))
+        score_grads = jnp.concatenate(grads, axis=1)
+        dq_main = dot(cache_buf[h, 0, mine].T, score_grads, (1, 0)) * INV_ROOT
+        dq_other = dot(cache_buf[h, 0, 1 - mine].T, score_grads, (1, 0)) * INV_ROOT
+        for t in range(tiles):
+            rows = slice(t * TILE, (t + 1) * TILE)
+            dq_t = jnp.where(slots[t] == mine, dq_main[:, rows], dq_other[:, rows])
+            dq_buf[h, rows, :] = dq_t.astype(BF16).T
+        store = pltpu.make_async_copy(dq_buf.at[h], dq_hbm.at[:, pl.ds(h * DH, DH)], out_sems.at[h])
+        store.start()
+        stores.append(store)
+        part_ref[0, :, cols] = dot(score_grads, jnp.concatenate(queries, axis=0), (1, 0))
         part_ref[1, :, cols] = dot(jnp.concatenate(probs, axis=1), jnp.concatenate(outs, axis=0), (1, 0))
         main_ref[0, :, cols] = cache_buf[h, 0, mine]
         main_ref[1, :, cols] = cache_buf[h, 1, mine]
+    for store in stores:
+        store.wait()
 
 
 def shipped(heads, recv_ref, main_ref, h):
@@ -125,18 +138,14 @@
         out_ref[1, :, cols] = part_ref[1, :, cols] + dv
 
 
-def project(both_ref, wk_ref, wv_ref, rel, outs):
+def project(both_ref, wk_ref, wv_ref, rel, out_ref):
     width = both_ref.shape[1] // 2
     rows = pl.ds(pl.multiple_of(jnp.bitwise_xor(lax.axis_index("head"), rel) * width, width), width)
     text = dot(both_ref[:, :width], wk_ref[rows, :], (1, 1)) + dot(both_ref[:, width:], wv_ref[rows, :], (1, 1))
-    text = text.astype(BF16)
-    at = 0
-    for out in outs:
-        out[...] = text[at : at + out.shape[0] * out.shape[1]].reshape(out.shape)
-        at += out.shape[0] * out.shape[1]
-
-
-def first_text_kernel(heads, blocks, chunks, recv_ref, main_ref, part_ref, wk_ref, wv_ref, both_ref, *outs):
+    out_ref[...] = text.astype(BF16).reshape(out_ref.shape)
+
+
+def first_text_kernel(heads, blocks, recv_ref, main_ref, part_ref, wk_ref, wv_ref, both_ref, sent_ref, kept_ref):
     me = lax.axis_index("seq")
     width = heads * DH
     block_rows = L // blocks
@@ -149,29 +158,34 @@
             rows = pl.ds(pl.multiple_of(jnp.bitwise_xor(me, s) * block_rows, block_rows), block_rows)
             both_ref[rows, h * DH : (h + 1) * DH] = dk[s * block_rows : (s + 1) * block_rows]
             both_ref[rows, width + h * DH : width + (h + 1) * DH] = dv[s * block_rows : (s + 1) * block_rows]
-    project(both_ref, wk_ref, wv_ref, 3, outs[:chunks])
-    project(both_ref, wk_ref, wv_ref, 2, outs[chunks:])
-
-
-def second_text_kernel(chunks, both_ref, wk_ref, wv_ref, *outs):
-    project(both_ref, wk_ref, wv_ref, 1, outs[:chunks])
-    project(both_ref, wk_ref, wv_ref, 0, outs[chunks:])
-
-
-def add_kernel(a_ref, b_ref, out_ref):
-    out_ref[...] = (a_ref[...].astype(F32) + b_ref[...].astype(F32)).astype(BF16)
-
-
-def split_add_kernel(a_ref, b_ref, *outs):
+    project(both_ref, wk_ref, wv_ref, 3, sent_ref)
+    project(both_ref, wk_ref, wv_ref, 2, kept_ref)
+
+
+def second_text_kernel(both_ref, wk_ref, wv_ref, sent_ref, kept_ref):
+    project(both_ref, wk_ref, wv_ref, 1, sent_ref)
+    project(both_ref, wk_ref, wv_ref, 0, kept_ref)
+
+
+def pair_kernel(kept_ref, came_ref, *outs):
+    at = 0
+    for out in outs:
+        part = slice(at, at + out.shape[0])
+        out[...] = (kept_ref[part].astype(F32) + came_ref[part].astype(F32)).astype(BF16)
+        at += out.shape[0]
+
+
+def cross_kernel(first, kept_ref, came_ref, crossed_ref, *outs):
     for i, out in enumerate(outs):
-        out[...] = (a_ref[i].astype(F32) + b_ref[i].astype(F32)).astype(BF16)
-
-
-def final_kernel(mains_ref, *refs):
+        pair = (kept_ref[first + i].astype(F32) + came_ref[first + i].astype(F32)).astype(BF16)
+        out[...] = (pair.astype(F32) + crossed_ref[i].astype(F32)).astype(BF16)
+
+
+def final_kernel(order, mains_ref, *refs):
     *blocks, out_ref = refs
     captions = out_ref.shape[0]
     totals = [0.0] * captions
-    for k, block in enumerate(blocks):
+    for k, block in zip(order, blocks, strict=True):
         value = block[...].astype(F32)
         main = jnp.tile(mains_ref[k : k + 1, :], (1, value.shape[1] // mains_ref.shape[1]))
         for c in range(captions):
@@ -185,13 +199,13 @@
     return lax.ppermute(array, axis, [(i, i ^ bit) for i in range(n)])
 
 
-def call(kernel, name, out_shape, operands, specs, scratch=(), limit=SMALL_LIMIT, hint_us=1.0):
+def call(kernel, name, out_shape, operands, specs, scratch=(), limit=SMALL_LIMIT, hint_us=1.0, out_specs=None):
     vmem = pl.BlockSpec(memory_space=pltpu.VMEM)
     return pl.pallas_call(
         kernel,
         out_shape=out_shape,
         in_specs=specs,
-        out_specs=jax.tree.map(lambda _: vmem, out_shape),
+        out_specs=out_specs or jax.tree.map(lambda _: vmem, out_shape),
         scratch_shapes=scratch,
         compiler_params=pltpu.CompilerParams(vmem_limit_bytes=limit),
         cost_estimate=pl.CostEstimate(flops=0, bytes_accessed=int(hint_us * 3_600_000), transcendentals=0),
@@ -207,8 +221,6 @@
     seq_count, head_devices = lax.axis_size("seq"), lax.axis_size("head")
     captions = seq_count // SPAN
     block_rows = L // seq_count
-    chunks = 2
-    per = seq_count // chunks
     held_back = [
         pltpu.with_memory_space_constraint(x, pltpu.HBM)
         for x in (tile_mask.T, slot_caption.T, queries, out_grad, caption_cache)
@@ -239,9 +251,15 @@
         [hbm] * 5,
         scalars
         + [pltpu.VMEM((rows_here, width), BF16)] * 2
-        + [pltpu.VMEM((heads, 2, slots, L, DH), BF16), pltpu.SemaphoreType.DMA((4 + heads,))],
+        + [
+            pltpu.VMEM((heads, 2, slots, L, DH), BF16),
+            pltpu.VMEM((heads, rows_here, DH), BF16),
+            pltpu.SemaphoreType.DMA((4 + heads,)),
+            pltpu.SemaphoreType.DMA((heads,)),
+        ],
         limit=KERNEL_LIMIT,
         hint_us=5.0,
+        out_specs=(hbm, vmem, vmem),
     )
     for tile in received[:-1]:
         part = call(
@@ -253,54 +271,55 @@
             limit=KERNEL_LIMIT,
             hint_us=2.0,
         )
-    piece = like(per, block_rows, width)
-    both, *pieces = call(
-        functools.partial(first_text_kernel, heads, seq_count, chunks),
+    blocks = like(seq_count, block_rows, width)
+    both, sent, kept = call(
+        functools.partial(first_text_kernel, heads, seq_count),
         "first_text",
-        (like(L, 2 * width),) + (piece,) * (2 * chunks),
+        (like(L, 2 * width), blocks, blocks),
         (received[-1], main, part, key_weight, value_weight),
         [vmem] * 5,
         limit=KERNEL_LIMIT,
         hint_us=3.0,
     )
-    sent_x, kept_x = pieces[:chunks], pieces[chunks:]
-    pieces = call(
-        functools.partial(second_text_kernel, chunks),
+    sent_own, kept_own = call(
+        second_text_kernel,
         "second_text",
-        (piece,) * (2 * chunks),
+        (blocks, blocks),
         (both, key_weight, value_weight),
         [vmem] * 3,
         limit=KERNEL_LIMIT,
         hint_us=1.0,
     )
-    sent_own, kept_own = pieces[:chunks], pieces[chunks:]
-
-    def add(a, b):
-        return call(add_kernel, "add", like(*a.shape), (a, b), [vmem] * 2)
-
-    order = range(chunks - 1, -1, -1)
-    far = {c: add(kept_x[c], swap(sent_x[c], "head", 1)) for c in order}
-    near = {c: add(kept_own[c], swap(sent_own[c], "head", 1)) for c in order}
-    arrived = [None] * seq_count
-    before = None
-    for c in order:
-        if before is not None:
-            before, far[c] = lax.optimization_barrier((before, far[c]))
-        if before is not None:
-            finish(before, near, arrived, per, call, like, vmem, c + 1)
-        before = swap(far[c], "head", 2)
-    finish(before, near, arrived, per, call, like, vmem, 0)
+    far = call(
+        pair_kernel,
+        "pair",
+        (like(CHUNK, block_rows, width),) * (seq_count // CHUNK),
+        (kept, swap(sent, "head", 1)),
+        [vmem] * 2,
+    )
+    came_own = swap(sent_own, "head", 1)
+    order, arrived = [], []
+    half = seq_count // 2
+    for i in [*range(half // CHUNK, seq_count // CHUNK), *reversed(range(half // CHUNK))]:
+        first = i * CHUNK
+        mine = call(
+            functools.partial(cross_kernel, first),
+            "cross",
+            (like(block_rows, width),) * CHUNK,
+            (kept_own, came_own, swap(far[i], "head", 2)),
+            [vmem] * 3,
+        )
+        for k, block in reversed(list(enumerate(mine, first))):
+            order.append(k)
+            arrived.append(swap(block, "seq", k) if k else block)
     text_grad = call(
-        final_kernel, "final", like(captions, block_rows, width), (mains, *arrived), [vmem] * (1 + seq_count)
+        functools.partial(final_kernel, order),
+        "final",
+        like(captions, block_rows, width),
+        (mains, *arrived),
+        [vmem] * (1 + seq_count),
     )
     return query_grad, text_grad
-
-
-def finish(came, near, arrived, per, call, like, vmem, c):
-    blocks = call(split_add_kernel, "split_add", (like(*came.shape[1:]),) * per, (near[c], came), [vmem] * 2)
-    for i in range(per):
-        k = c * per + i
-        arrived[k] = swap(blocks[i], "seq", k) if k else blocks[i]
 
 
 def shards_general(queries, out_grad, tile_mask, slot_caption, caption_cache, key_weight, value_weight):

time: 43.4 us -> 40.6 us (0.935)
  waiting for transfers between devices: 9.56 us -> 7.06 us
  Pallas kernels: 14.7 us -> 13.2 us
  starting transfers between devices: 18.2 us -> 19.5 us
    ppermute x15, waiting for transfers between devices: 9.56 us -> 7.06 us  [swap(): return lax.ppermute(array, axis, [(i, i ^ bit) for i in range(n)])]
    pallas_call x12 -> x11, Pallas kernels: 14.7 us -> 13.2 us  [call(): pl.pallas_call(kernel, out_shape=out_shape, in_specs=specs, out_specs=out...]
    ppermute x15, starting transfers between devices: 18.2 us -> 19.5 us  [swap(): return lax.ppermute(array, axis, [(i, i ^ bit) for i in range(n)])]
  transfers between devices with their start and end apart: 15 -> 15, of which waited for: 6 -> 5; matrix products, arithmetic and copies ran while one was open for 0% -> 0% of each run, Pallas kernels for 23% -> 21%
where the time goes in v3:
time: 40.6 us; the launch traced here: 40.4 us
  starting transfers between devices  19.5 us (48%)
  Pallas kernels  13.2 us (33%)
  waiting for transfers between devices  7.06 us (17%)
  between operations  0.73 us (2%)
    ppermute x15, starting transfers between devices, swap(): return lax.ppermute(array, axis, [(i, i ^ bit) for i in range(n)])  19.5 us
    pallas_call x11, Pallas kernels, call(): pl.pallas_call(kernel, out_shape=out_shape, in_specs=specs, out_specs=out...  13.2 us
    ppermute x15, waiting for transfers between devices, swap(): return lax.ppermute(array, axis, [(i, i ^ bit) for i in range(n)])  7.06 us
  transfers between devices with their start and end apart: 15, of which 5 were waited for; matrix products, arithmetic and copies ran while one was open for 0% of the time, Pallas kernels for 21%

profile of v3, /device:TPU:0, one launch (start us, length us, event | category | flops | bytes accessed | tf_op | source)
XLA Modules:
  0.0 40.4 jit_solution(16657691665725491840)
XLA Ops:
  0.6 1.1 %stage.1 = (bf16[2,128,384]{2,1,0:T(8,128)(2,1)S(1)}, bf16[2,128,384]{2,1,0:T(8,128)(2,1)S(1)}, s32[8,128]{1,0:T(8,128)S(1)}) custom-call(s32[2,3]{1,0:T(2,128)} %bitcast.2, s32[2,8]{1,0:T(2,128)} %bitcast.4, bf16[384,384]{1,0:T(8,128)(2,1)} %q_hbm.3, bf16[384,384]{1,0:T(8,128)(2,1)} %g_hbm.3), custom_call_target="tpu_custom_call" | custom-call | bytes 3600000 | tf_op jit(solution)/shard_map/stage/pallas_call | solution.py:204
  1.8 3.0 %collective-permute-start.1 = (bf16[2,128,384]{2,1,0:T(8,128)(2,1)S(1)}, bf16[2,128,384]{2,1,0:T(8,128)(2,1)S(1)}, u32[]{:S(2)}, u32[]{:S(2)}) collective-permute-start(bf16[2,128,384]{2,1,0:T(8,128)(2,1)S(1)} %get-tuple-element.29), channel_id=1, source_target_pairs={{0,4},{4,0},{8,12},{12,8},{16,20},{20,16},{24,28},{28,24},{1,5},{5... | collective-permute-start | bytes 589832 | tf_op jit(solution)/shard_map/ppermute | solution.py:199
  4.9 5.6 %own_tiles.1 = (bf16[384,384]{1,0:T(8,128)(2,1)}, f32[2,512,384]{2,1,0:T(8,128)S(1)}, bf16[2,512,384]{2,1,0:T(8,128)(2,1)S(1)}) custom-call(s32[2,3]{1,0:T(2,128)} %bitcast.3, s32[2,8]{1,0:T(2,128)} %bitcast.5, bf16[384,384]{1,0:T(8,128)(2,1)} %q_hbm.3, bf16[384,384]{1,0:T(8,128)(2,1)} %g_hbm.3, bf16[2,2,512,384]{3,2,1,0:T(8,128)(2,1)} %cache_hbm.1), custom_call_target="tpu_custom_call" | custom-call | bytes 18000000 | tf_op jit(solution)/shard_map/own_tiles/pallas_call | solution.py:204
  10.5 1.5 %shipped_tile.1.part_ref = f32[2,512,384]{2,1,0:T(8,128)S(1)} custom-call(bf16[2,128,384]{2,1,0:T(8,128)(2,1)S(1)} %collective-permute-done.1.recv_ref, bf16[2,512,384]{2,1,0:T(8,128)(2,1)S(1)} %get-tuple-element.28.main_ref, f32[2,512,384]{2,1,0:T(8,128)S(1)} %get-tuple-element.30.part_ref), custom_call_target="tpu_custom_call" | custom-call | bytes 7200000 | tf_op jit(solution)/shard_map/shipped_tile/pallas_call | solution.py:204
  12.1 1.8 %collective-permute-done.recv_ref = bf16[2,128,384]{2,1,0:T(8,128)(2,1)S(1)} collective-permute-done((bf16[2,128,384]{2,1,0:T(8,128)(2,1)S(1)}, bf16[2,128,384]{2,1,0:T(8,128)(2,1)S(1)}, u32[]{:S(2)}, u32[]{:S(2)}) %collective-permute-start) | collective-permute-done | bytes 196640 | tf_op jit(solution)/shard_map/ppermute | solution.py:199
  13.9 2.6 %first_text.1 = (bf16[512,768]{1,0:T(8,128)(2,1)S(1)}, bf16[8,64,384]{2,1,0:T(8,128)(2,1)S(1)}, bf16[8,64,384]{2,1,0:T(8,128)(2,1)S(1)}) custom-call(bf16[2,128,384]{2,1,0:T(8,128)(2,1)S(1)} %collective-permute-done.recv_ref, bf16[2,512,384]{2,1,0:T(8,128)(2,1)S(1)} %get-tuple-element.28.main_ref, f32[2,512,384]{2,1,0:T(8,128)S(1)} %shipped_tile.1.part_ref, ...), custom_call_target="tpu_custom_call" | custom-call | bytes 10800000 | tf_op jit(solution)/shard_map/first_text/pallas_call | solution.py:204
  16.6 1.1 %second_text.1 = (bf16[8,64,384]{2,1,0:T(8,128)(2,1)S(1)}, bf16[8,64,384]{2,1,0:T(8,128)(2,1)S(1)}) custom-call(bf16[512,768]{1,0:T(8,128)(2,1)S(1)} %get-tuple-element.31.both_ref, bf16[1536,384]{1,0:T(8,128)(2,1)S(1)} %copy-done, bf16[1536,384]{1,0:T(8,128)(2,1)S(1)} %copy-done.1), custom_call_target="tpu_custom_call" | custom-call | bytes 3600000 | tf_op jit(solution)/shard_map/second_text/pallas_call | solution.py:204
  17.8 0.5 %collective-permute-start.2 = (bf16[8,64,384]{2,1,0:T(8,128)(2,1)S(1)}, bf16[8,64,384]{2,1,0:T(8,128)(2,1)S(1)}, u32[]{:S(2)}, u32[]{:S(2)}) collective-permute-start(bf16[8,64,384]{2,1,0:T(8,128)(2,1)S(1)} %get-tuple-element.33), channel_id=1, source_target_pairs={{0,1},{1,0},{2,3},{3,2},{4,5},{5,4},{6,7},{7,6},{8,9},{9,8},{10,11... | collective-permute-start | bytes 1179656 | tf_op jit(solution)/shard_map/ppermute | solution.py:199
  18.5 1.8 %collective-permute-start.4 = (bf16[2,64,384]{2,1,0:T(8,128)(2,1)S(1)}, bf16[2,64,384]{2,1,0:T(8,128)(2,1)S(1)}, u32[]{:S(2)}, u32[]{:S(2)}) collective-permute-start(bf16[2,64,384]{2,1,0:T(8,128)(2,1)S(1)} %get-tuple-element.36), channel_id=1, source_target_pairs={{0,2},{1,3},{2,0},{3,1},{4,6},{5,7},{6,4},{7,5},{8,10},{9,11},{10,... | collective-permute-start | bytes 294920 | tf_op jit(solution)/shard_map/ppermute | solution.py:199
  20.2 0.3 collective-permute-start.7
  20.5 1.7 %collective-permute-start.10 = (bf16[2,64,384]{2,1,0:T(8,128)(2,1)S(1)}, bf16[2,64,384]{2,1,0:T(8,128)(2,1)S(1)}, u32[]{:S(2)}, u32[]{:S(2)}) collective-permute-start(bf16[2,64,384]{2,1,0:T(8,128)(2,1)S(1)} %get-tuple-element.42), channel_id=1, source_target_pairs={{0,2},{1,3},{2,0},{3,1},{4,6},{5,7},{6,4},{7,5},{8,10},{9,11},{10,... | collective-permute-start | bytes 294920 | tf_op jit(solution)/shard_map/ppermute | solution.py:199
  22.2 0.3 collective-permute-start.13
  22.6 1.5 %collective-permute-done.4.crossed_ref = bf16[2,64,384]{2,1,0:T(8,128)(2,1)S(1)} collective-permute-done((bf16[2,64,384]{2,1,0:T(8,128)(2,1)S(1)}, bf16[2,64,384]{2,1,0:T(8,128)(2,1)S(1)}, u32[]{:S(2)}, u32[]{:S(2)}) %collective-permute-start.4) | collective-permute-done | bytes 98336 | tf_op jit(solution)/shard_map/ppermute | solution.py:199
  24.2 3.9 %collective-permute-start.5 = (bf16[64,384]{1,0:T(8,128)(2,1)S(1)}, bf16[64,384]{1,0:T(8,128)(2,1)S(1)}, u32[]{:S(2)}, u32[]{:S(2)}) collective-permute-start(bf16[64,384]{1,0:T(8,128)(2,1)S(1)} %get-tuple-element.37), channel_id=1, source_target_pairs={{0,20},{4,16},{8,28},{12,24},{16,4},{20,0},{24,12},{28,8},{1,21},{... | collective-permute-start | bytes 147464 | tf_op jit(solution)/shard_map/ppermute | solution.py:199
  28.0 0.3 collective-permute-start.6
  28.4 3.6 %collective-permute-start.8 = (bf16[64,384]{1,0:T(8,128)(2,1)S(1)}, bf16[64,384]{1,0:T(8,128)(2,1)S(1)}, u32[]{:S(2)}, u32[]{:S(2)}) collective-permute-start(bf16[64,384]{1,0:T(8,128)(2,1)S(1)} %get-tuple-element.40), channel_id=1, source_target_pairs={{0,28},{4,24},{8,20},{12,16},{16,12},{20,8},{24,4},{28,0},{1,29},{... | collective-permute-start | bytes 147464 | tf_op jit(solution)/shard_map/ppermute | solution.py:199
  32.0 0.1 collective-permute-start.9
  32.3 0.9 %collective-permute-start.11 = (bf16[64,384]{1,0:T(8,128)(2,1)S(1)}, bf16[64,384]{1,0:T(8,128)(2,1)S(1)}, u32[]{:S(2)}, u32[]{:S(2)}) collective-permute-start(bf16[64,384]{1,0:T(8,128)(2,1)S(1)} %get-tuple-element.43), channel_id=1, source_target_pairs={{0,12},{4,8},{8,4},{12,0},{16,28},{20,24},{24,20},{28,16},{1,13},{... | collective-permute-start | bytes 147464 | tf_op jit(solution)/shard_map/ppermute | solution.py:199
  33.2 2.3 %collective-permute-start.12 = (bf16[64,384]{1,0:T(8,128)(2,1)S(1)}, bf16[64,384]{1,0:T(8,128)(2,1)S(1)}, u32[]{:S(2)}, u32[]{:S(2)}) collective-permute-start(bf16[64,384]{1,0:T(8,128)(2,1)S(1)} %get-tuple-element.44), channel_id=1, source_target_pairs={{0,8},{4,12},{8,0},{12,4},{16,24},{20,28},{24,16},{28,20},{1,9},{5... | collective-permute-start | bytes 147464 | tf_op jit(solution)/shard_map/ppermute | solution.py:199
  35.5 0.4 %collective-permute-start.14 = (bf16[64,384]{1,0:T(8,128)(2,1)S(1)}, bf16[64,384]{1,0:T(8,128)(2,1)S(1)}, u32[]{:S(2)}, u32[]{:S(2)}) collective-permute-start(bf16[64,384]{1,0:T(8,128)(2,1)S(1)} %get-tuple-element.46), channel_id=1, source_target_pairs={{0,4},{4,0},{8,12},{12,8},{16,20},{20,16},{24,28},{28,24},{1,5},{5... | collective-permute-start | bytes 147464 | tf_op jit(solution)/shard_map/ppermute | solution.py:199
  35.9 2.1 %collective-permute-done.9.refs_3_ = bf16[64,384]{1,0:T(8,128)(2,1)S(1)} collective-permute-done((bf16[64,384]{1,0:T(8,128)(2,1)S(1)}, bf16[64,384]{1,0:T(8,128)(2,1)S(1)}, u32[]{:S(2)}, u32[]{:S(2)}) %collective-permute-start.9) | collective-permute-done | bytes 49184 | tf_op jit(solution)/shard_map/ppermute | solution.py:199
  38.0 0.4 %collective-permute-done.12.refs_5_ = bf16[64,384]{1,0:T(8,128)(2,1)S(1)} collective-permute-done((bf16[64,384]{1,0:T(8,128)(2,1)S(1)}, bf16[64,384]{1,0:T(8,128)(2,1)S(1)}, u32[]{:S(2)}, u32[]{:S(2)}) %collective-permute-start.12) | collective-permute-done | bytes 49184 | tf_op jit(solution)/shard_map/ppermute | solution.py:199
  38.5 1.1 %collective-permute-done.14.refs_6_ = bf16[64,384]{1,0:T(8,128)(2,1)S(1)} collective-permute-done((bf16[64,384]{1,0:T(8,128)(2,1)S(1)}, bf16[64,384]{1,0:T(8,128)(2,1)S(1)}, u32[]{:S(2)}, u32[]{:S(2)}) %collective-permute-start.14) | collective-permute-done | bytes 49184 | tf_op jit(solution)/shard_map/ppermute | solution.py:199
  39.6 0.8 %final.1 = bf16[2,64,384]{2,1,0:T(8,128)(2,1)} custom-call(s32[8,128]{1,0:T(8,128)S(1)} %get-tuple-element.26.mains_ref, bf16[64,384]{1,0:T(8,128)(2,1)S(1)} %collective-permute-done.5.refs_0_, bf16[64,384]{1,0:T(8,128)(2,1)S(1)} %collective-permute-done.6.refs_1_, bf16[64,384]{1,0:T(8,128)(2,1)S(1)} %collective-permute-done.8.refs_2_, ...), custom_call_target="tpu_custom_call" | custom-call | bytes 3600000 | tf_op jit(solution)/shard_map/final/pallas_call | solution.py:204
  (21 shorter events, 0.5 us)
Async XLA Ops:
  1.8 8.8 %collective-permute-start.1 = (bf16[2,128,384]{2,1,0:T(8,128)(2,1)S(1)}, bf16[2,128,384]{2,1,0:T(8,128)(2,1)S(1)}, u32[]{:S(2)}, u32[]{:S(2)}) collective-permute-start(bf16[2,128,384]{2,1,0:T(8,128)(2,1)S(1)} %get-tuple-element.29), channel_id=1, source_target_pairs={{0,4},{4,0},{8,12},{12,8},{16,20},{20,16},{24,28},{28,24},{1,5},{5... | collective-permute-start | bytes 589832 | tf_op jit(solution)/shard_map/ppermute | solution.py:199
  4.8 9.1 %collective-permute-start = (bf16[2,128,384]{2,1,0:T(8,128)(2,1)S(1)}, bf16[2,128,384]{2,1,0:T(8,128)(2,1)S(1)}, u32[]{:S(2)}, u32[]{:S(2)}) collective-permute-start(bf16[2,128,384]{2,1,0:T(8,128)(2,1)S(1)} %get-tuple-element.27), channel_id=1, source_target_pairs={{0,4},{4,0},{8,12},{12,8},{16,20},{20,16},{24,28},{28,24},{1,5},{5... | collective-permute-start | bytes 589832 | tf_op jit(solution)/shard_map/ppermute | solution.py:199
  10.5 3.4 %copy-start = (bf16[1536,384]{1,0:T(8,128)(2,1)S(1)}, bf16[1536,384]{1,0:T(8,128)(2,1)}, u32[]{:S(2)}) copy-start(bf16[1536,384]{1,0:T(8,128)(2,1)} %wk_ref.3) | copy-start | bytes 3538948
  10.5 3.4 %copy-start.1 = (bf16[1536,384]{1,0:T(8,128)(2,1)S(1)}, bf16[1536,384]{1,0:T(8,128)(2,1)}, u32[]{:S(2)}) copy-start(bf16[1536,384]{1,0:T(8,128)(2,1)} %wv_ref.3) | copy-start | bytes 3538948
  16.6 1.8 %collective-permute-start.3 = (bf16[8,64,384]{2,1,0:T(8,128)(2,1)S(1)}, bf16[8,64,384]{2,1,0:T(8,128)(2,1)S(1)}, u32[]{:S(2)}, u32[]{:S(2)}) collective-permute-start(bf16[8,64,384]{2,1,0:T(8,128)(2,1)S(1)} %get-tuple-element.35), channel_id=1, source_target_pairs={{0,1},{1,0},{2,3},{3,2},{4,5},{5,4},{6,7},{7,6},{8,9},{9,8},{10,11... | collective-permute-start | bytes 1179656 | tf_op jit(solution)/shard_map/ppermute | solution.py:199
  17.8 4.8 %collective-permute-start.2 = (bf16[8,64,384]{2,1,0:T(8,128)(2,1)S(1)}, bf16[8,64,384]{2,1,0:T(8,128)(2,1)S(1)}, u32[]{:S(2)}, u32[]{:S(2)}) collective-permute-start(bf16[8,64,384]{2,1,0:T(8,128)(2,1)S(1)} %get-tuple-element.33), channel_id=1, source_target_pairs={{0,1},{1,0},{2,3},{3,2},{4,5},{5,4},{6,7},{7,6},{8,9},{9,8},{10,11... | collective-permute-start | bytes 1179656 | tf_op jit(solution)/shard_map/ppermute | solution.py:199
  18.5 5.6 %collective-permute-start.4 = (bf16[2,64,384]{2,1,0:T(8,128)(2,1)S(1)}, bf16[2,64,384]{2,1,0:T(8,128)(2,1)S(1)}, u32[]{:S(2)}, u32[]{:S(2)}) collective-permute-start(bf16[2,64,384]{2,1,0:T(8,128)(2,1)S(1)} %get-tuple-element.36), channel_id=1, source_target_pairs={{0,2},{1,3},{2,0},{3,1},{4,6},{5,7},{6,4},{7,5},{8,10},{9,11},{10,... | collective-permute-start | bytes 294920 | tf_op jit(solution)/shard_map/ppermute | solution.py:199
  20.2 8.2 %collective-permute-start.7 = (bf16[2,64,384]{2,1,0:T(8,128)(2,1)S(1)}, bf16[2,64,384]{2,1,0:T(8,128)(2,1)S(1)}, u32[]{:S(2)}, u32[]{:S(2)}) collective-permute-start(bf16[2,64,384]{2,1,0:T(8,128)(2,1)S(1)} %get-tuple-element.39), channel_id=1, source_target_pairs={{0,2},{1,3},{2,0},{3,1},{4,6},{5,7},{6,4},{7,5},{8,10},{9,11},{10,... | collective-permute-start | bytes 294920 | tf_op jit(solution)/shard_map/ppermute | solution.py:199
  20.5 11.5 %collective-permute-start.10 = (bf16[2,64,384]{2,1,0:T(8,128)(2,1)S(1)}, bf16[2,64,384]{2,1,0:T(8,128)(2,1)S(1)}, u32[]{:S(2)}, u32[]{:S(2)}) collective-permute-start(bf16[2,64,384]{2,1,0:T(8,128)(2,1)S(1)} %get-tuple-element.42), channel_id=1, source_target_pairs={{0,2},{1,3},{2,0},{3,1},{4,6},{5,7},{6,4},{7,5},{8,10},{9,11},{10,... | collective-permute-start | bytes 294920 | tf_op jit(solution)/shard_map/ppermute | solution.py:199
  22.2 10.0 %collective-permute-start.13 = (bf16[2,64,384]{2,1,0:T(8,128)(2,1)S(1)}, bf16[2,64,384]{2,1,0:T(8,128)(2,1)S(1)}, u32[]{:S(2)}, u32[]{:S(2)}) collective-permute-start(bf16[2,64,384]{2,1,0:T(8,128)(2,1)S(1)} %get-tuple-element.45), channel_id=1, source_target_pairs={{0,2},{1,3},{2,0},{3,1},{4,6},{5,7},{6,4},{7,5},{8,10},{9,11},{10,... | collective-permute-start | bytes 294920 | tf_op jit(solution)/shard_map/ppermute | solution.py:199
  24.2 9.0 %collective-permute-start.5 = (bf16[64,384]{1,0:T(8,128)(2,1)S(1)}, bf16[64,384]{1,0:T(8,128)(2,1)S(1)}, u32[]{:S(2)}, u32[]{:S(2)}) collective-permute-start(bf16[64,384]{1,0:T(8,128)(2,1)S(1)} %get-tuple-element.37), channel_id=1, source_target_pairs={{0,20},{4,16},{8,28},{12,24},{16,4},{20,0},{24,12},{28,8},{1,21},{... | collective-permute-start | bytes 147464 | tf_op jit(solution)/shard_map/ppermute | solution.py:199
  28.0 7.5 %collective-permute-start.6 = (bf16[64,384]{1,0:T(8,128)(2,1)S(1)}, bf16[64,384]{1,0:T(8,128)(2,1)S(1)}, u32[]{:S(2)}, u32[]{:S(2)}) collective-permute-start(bf16[64,384]{1,0:T(8,128)(2,1)S(1)} %get-tuple-element.38), channel_id=1, source_target_pairs={{0,16},{4,20},{8,24},{12,28},{16,0},{20,4},{24,8},{28,12},{1,17},{... | collective-permute-start | bytes 147464 | tf_op jit(solution)/shard_map/ppermute | solution.py:199
  28.4 7.5 %collective-permute-start.8 = (bf16[64,384]{1,0:T(8,128)(2,1)S(1)}, bf16[64,384]{1,0:T(8,128)(2,1)S(1)}, u32[]{:S(2)}, u32[]{:S(2)}) collective-permute-start(bf16[64,384]{1,0:T(8,128)(2,1)S(1)} %get-tuple-element.40), channel_id=1, source_target_pairs={{0,28},{4,24},{8,20},{12,16},{16,12},{20,8},{24,4},{28,0},{1,29},{... | collective-permute-start | bytes 147464 | tf_op jit(solution)/shard_map/ppermute | solution.py:199
  32.0 6.0 %collective-permute-start.9 = (bf16[64,384]{1,0:T(8,128)(2,1)S(1)}, bf16[64,384]{1,0:T(8,128)(2,1)S(1)}, u32[]{:S(2)}, u32[]{:S(2)}) collective-permute-start(bf16[64,384]{1,0:T(8,128)(2,1)S(1)} %get-tuple-element.41), channel_id=1, source_target_pairs={{0,24},{4,28},{8,16},{12,20},{16,8},{20,12},{24,0},{28,4},{1,25},{... | collective-permute-start | bytes 147464 | tf_op jit(solution)/shard_map/ppermute | solution.py:199
  32.3 5.8 %collective-permute-start.11 = (bf16[64,384]{1,0:T(8,128)(2,1)S(1)}, bf16[64,384]{1,0:T(8,128)(2,1)S(1)}, u32[]{:S(2)}, u32[]{:S(2)}) collective-permute-start(bf16[64,384]{1,0:T(8,128)(2,1)S(1)} %get-tuple-element.43), channel_id=1, source_target_pairs={{0,12},{4,8},{8,4},{12,0},{16,28},{20,24},{24,20},{28,16},{1,13},{... | collective-permute-start | bytes 147464 | tf_op jit(solution)/shard_map/ppermute | solution.py:199
  33.2 5.3 %collective-permute-start.12 = (bf16[64,384]{1,0:T(8,128)(2,1)S(1)}, bf16[64,384]{1,0:T(8,128)(2,1)S(1)}, u32[]{:S(2)}, u32[]{:S(2)}) collective-permute-start(bf16[64,384]{1,0:T(8,128)(2,1)S(1)} %get-tuple-element.44), channel_id=1, source_target_pairs={{0,8},{4,12},{8,0},{12,4},{16,24},{20,28},{24,16},{28,20},{1,9},{5... | collective-permute-start | bytes 147464 | tf_op jit(solution)/shard_map/ppermute | solution.py:199
  35.5 4.1 %collective-permute-start.14 = (bf16[64,384]{1,0:T(8,128)(2,1)S(1)}, bf16[64,384]{1,0:T(8,128)(2,1)S(1)}, u32[]{:S(2)}, u32[]{:S(2)}) collective-permute-start(bf16[64,384]{1,0:T(8,128)(2,1)S(1)} %get-tuple-element.46), channel_id=1, source_target_pairs={{0,4},{4,0},{8,12},{12,8},{16,20},{20,16},{24,28},{28,24},{1,5},{5... | collective-permute-start | bytes 147464 | tf_op jit(solution)/shard_map/ppermute | solution.py:199

commit v4 on v3

--- a/solution.py
+++ b/solution.py
@@ -15,7 +15,6 @@
 F32 = jnp.float32
 BF16 = jnp.bfloat16
 INV_ROOT = 1.0 / math.sqrt(DH)
-CHUNK = 2
 KERNEL_LIMIT = 32 * 1024 * 1024
 SMALL_LIMIT = 8 * 1024 * 1024
 
@@ -57,7 +56,7 @@
 
 
 def stage_kernel(captions, tiles, mask_hbm, caps_hbm, q_hbm, g_hbm, *refs):
-    *sent, mains_ref, mask_ref, caps_ref, q_buf, g_buf, sems = refs
+    *sent, mask_ref, caps_ref, q_buf, g_buf, sems = refs
     me = lax.axis_index("seq")
     first = 1 - jnp.bitwise_and(me, 1)
     rows = pl.ds(pl.multiple_of(first * TILE, TILE), (tiles - 1) * TILE)
@@ -72,19 +71,17 @@
         at = slice(i * TILE, (i + 1) * TILE)
         out[0] = q_buf[at, :] * keep
         out[1] = g_buf[at, :] * keep
-    for k in range(mains_ref.shape[0]):
-        source = jnp.bitwise_xor(me, k)
-        main = caps_ref[main_slot(caps_ref, source, captions), source]
-        mains_ref[k : k + 1, :] = jnp.full((1, mains_ref.shape[1]), main, jnp.int32)
 
 
 def own_kernel(
-    captions, tiles, heads, mask_hbm, caps_hbm, q_hbm, g_hbm, cache_hbm, dq_hbm, part_ref, main_ref,
-    mask_ref, caps_ref, q_buf, g_buf, cache_buf, dq_buf, sems, out_sems,
+    captions, tiles, heads, mask_hbm, caps_hbm, q_hbm, g_hbm, cache_hbm, wk_hbm, wv_hbm,
+    dq_hbm, part_ref, main_ref, weight_ref, mains_ref, mask_ref, caps_ref, q_buf, g_buf, cache_buf, dq_buf, sems, out_sems,
 ):
     me = lax.axis_index("seq")
     pairs = [(mask_hbm, mask_ref), (caps_hbm, caps_ref), (q_hbm, q_buf), (g_hbm, g_buf)]
     pairs += [(cache_hbm.at[:, :, :, pl.ds(h * DH, DH)], cache_buf.at[h]) for h in range(heads)]
+    width = heads * DH
+    pairs += [(wk_hbm, weight_ref.at[:, pl.ds(0, width)]), (wv_hbm, weight_ref.at[:, pl.ds(width, width)])]
     copies = fetch(pairs, sems)
     for c in copies[:4]:
         c.wait()
@@ -119,8 +116,12 @@
         part_ref[1, :, cols] = dot(jnp.concatenate(probs, axis=1), jnp.concatenate(outs, axis=0), (1, 0))
         main_ref[0, :, cols] = cache_buf[h, 0, mine]
         main_ref[1, :, cols] = cache_buf[h, 1, mine]
-    for store in stores:
-        store.wait()
+    for k in range(mains_ref.shape[0]):
+        source = jnp.bitwise_xor(me, k)
+        main = caps_ref[main_slot(caps_ref, source, captions), source]
+        mains_ref[k : k + 1, :] = jnp.full((1, mains_ref.shape[1]), main, jnp.int32)
+    for copy in stores + copies[4 + heads :]:
+        copy.wait()
 
 
 def shipped(heads, recv_ref, main_ref, h):
@@ -138,65 +139,89 @@
         out_ref[1, :, cols] = part_ref[1, :, cols] + dv
 
 
-def project(both_ref, wk_ref, wv_ref, rel, out_ref):
-    width = both_ref.shape[1] // 2
-    rows = pl.ds(pl.multiple_of(jnp.bitwise_xor(lax.axis_index("head"), rel) * width, width), width)
-    text = dot(both_ref[:, :width], wk_ref[rows, :], (1, 1)) + dot(both_ref[:, width:], wv_ref[rows, :], (1, 1))
-    out_ref[...] = text.astype(BF16).reshape(out_ref.shape)
-
-
-def first_text_kernel(heads, blocks, recv_ref, main_ref, part_ref, wk_ref, wv_ref, both_ref, sent_ref, kept_ref):
-    me = lax.axis_index("seq")
+def project(both_ref, weight_ref, rel, kept_ref, sent_ref):
+    features = kept_ref.shape[2]
+    chip = jnp.right_shift(lax.axis_index("head"), 1)
+    rows = pl.ds(pl.multiple_of(jnp.bitwise_xor(chip, rel) * features, features), features)
+    text = dot(both_ref[...], weight_ref[rows, :], (1, 1)).astype(BF16)
+    half = text.shape[0] // 2
+    kept_ref[...] = text[:half].reshape(kept_ref.shape)
+    sent_ref[...] = text[half:].reshape(sent_ref.shape)
+
+
+def first_text_kernel(heads, blocks, recv_ref, main_ref, part_ref, weight_ref, both_ref, kept_ref, sent_ref):
+    me, core = lax.axis_index("seq"), jnp.bitwise_and(lax.axis_index("head"), 1)
     width = heads * DH
     block_rows = L // blocks
+    places = []
+    for s in range(blocks):
+        rel = jnp.bitwise_xor(jnp.bitwise_xor(me, s), core)
+        pair, quarter = jnp.right_shift(rel, 1), blocks // 4
+        place = jnp.where(pair >= quarter, pair - quarter, 2 * quarter - 1 - pair)
+        place += jnp.bitwise_and(rel, 1) * (blocks // 2)
+        places.append(pl.ds(pl.multiple_of(place * block_rows, block_rows), block_rows))
     for h in range(heads):
         cols = slice(h * DH, (h + 1) * DH)
         dk, dv = shipped(heads, recv_ref, main_ref, h)
         dk = ((part_ref[0, :, cols] + dk) * INV_ROOT).astype(BF16)
         dv = (part_ref[1, :, cols] + dv).astype(BF16)
-        for s in range(blocks):
-            rows = pl.ds(pl.multiple_of(jnp.bitwise_xor(me, s) * block_rows, block_rows), block_rows)
+        for s, rows in enumerate(places):
             both_ref[rows, h * DH : (h + 1) * DH] = dk[s * block_rows : (s + 1) * block_rows]
             both_ref[rows, width + h * DH : width + (h + 1) * DH] = dv[s * block_rows : (s + 1) * block_rows]
-    project(both_ref, wk_ref, wv_ref, 3, sent_ref)
-    project(both_ref, wk_ref, wv_ref, 2, kept_ref)
-
-
-def second_text_kernel(both_ref, wk_ref, wv_ref, sent_ref, kept_ref):
-    project(both_ref, wk_ref, wv_ref, 1, sent_ref)
-    project(both_ref, wk_ref, wv_ref, 0, kept_ref)
+    project(both_ref, weight_ref, 1, kept_ref, sent_ref)
+
+
+def second_text_kernel(both_ref, weight_ref, kept_ref, sent_ref):
+    project(both_ref, weight_ref, 0, kept_ref, sent_ref)
 
 
 def pair_kernel(kept_ref, came_ref, *outs):
-    at = 0
-    for out in outs:
-        part = slice(at, at + out.shape[0])
-        out[...] = (kept_ref[part].astype(F32) + came_ref[part].astype(F32)).astype(BF16)
-        at += out.shape[0]
-
-
-def cross_kernel(first, kept_ref, came_ref, crossed_ref, *outs):
     for i, out in enumerate(outs):
-        pair = (kept_ref[first + i].astype(F32) + came_ref[first + i].astype(F32)).astype(BF16)
-        out[...] = (pair.astype(F32) + crossed_ref[i].astype(F32)).astype(BF16)
-
-
-def final_kernel(order, mains_ref, *refs):
-    *blocks, out_ref = refs
-    captions = out_ref.shape[0]
+        out[...] = (kept_ref[i].astype(F32) + came_ref[i].astype(F32)).astype(BF16)
+
+
+def cross_kernel(i, kept_ref, came_ref, crossed_ref, out_ref):
+    pair = (kept_ref[i].astype(F32) + came_ref[i].astype(F32)).astype(BF16)
+    out_ref[...] = (pair.astype(F32) + crossed_ref[...].astype(F32)).astype(BF16)
+
+
+def caption_kernel(bases, *refs):
+    *blocks, own_ref, mains_ref, kept_ref, sent_ref = refs
+    captions, _, width = kept_ref.shape
+    core = jnp.bitwise_and(lax.axis_index("head"), 1)
     totals = [0.0] * captions
-    for k, block in zip(order, blocks, strict=True):
+    for base, block in zip(bases, blocks, strict=True):
         value = block[...].astype(F32)
-        main = jnp.tile(mains_ref[k : k + 1, :], (1, value.shape[1] // mains_ref.shape[1]))
+        if base == 0:
+            value = jnp.where(core == 0, own_ref[...].astype(F32), value)
+        main = mains_ref[pl.ds(base + core, 1), :]
+        main = jnp.tile(main, (1, value.shape[1] // main.shape[1]))
         for c in range(captions):
             totals[c] += jnp.where(main == c, value, 0.0)
     for c in range(captions):
-        out_ref[c] = totals[c].astype(BF16)
+        low, high = totals[c][:, :width], totals[c][:, width:]
+        kept_ref[c] = jnp.where(core == 0, low, high)
+        sent_ref[c] = jnp.where(core == 0, high, low).astype(BF16)
+
+
+def final_kernel(kept_ref, came_ref, out_ref):
+    out_ref[...] = (kept_ref[...] + came_ref[...].astype(F32)).astype(BF16)
 
 
 def swap(array, axis, bit):
     n = lax.axis_size(axis)
     return lax.ppermute(array, axis, [(i, i ^ bit) for i in range(n)])
+
+
+def send(block, base):
+    seq_count, head_devices = lax.axis_size("seq"), lax.axis_size("head")
+    pairs = []
+    for s in range(seq_count):
+        for h in range(head_devices):
+            target = s ^ base ^ (h & 1)
+            if target != s:
+                pairs.append((s * head_devices + h, target * head_devices + h))
+    return lax.ppermute(block, ("seq", "head"), pairs)
 
 
 def call(kernel, name, out_shape, operands, specs, scratch=(), limit=SMALL_LIMIT, hint_us=1.0, out_specs=None):
@@ -223,7 +248,7 @@
     block_rows = L // seq_count
     held_back = [
         pltpu.with_memory_space_constraint(x, pltpu.HBM)
-        for x in (tile_mask.T, slot_caption.T, queries, out_grad, caption_cache)
+        for x in (tile_mask.T, slot_caption.T, queries, out_grad, caption_cache, key_weight, value_weight)
     ]
     mask_t, caps_t = held_back[:2]
     vmem = pl.BlockSpec(memory_space=pltpu.VMEM)
@@ -233,33 +258,39 @@
     def like(*shape, dtype=BF16):
         return jax.ShapeDtypeStruct(shape, dtype)
 
-    *sent, mains = call(
+    sent = call(
         functools.partial(stage_kernel, captions, tiles),
         "stage",
-        (like(2, TILE, width),) * (tiles - 1) + (like(seq_count, 128, dtype=jnp.int32),),
+        (like(2, TILE, width),) * (tiles - 1),
         held_back[:4],
         [hbm] * 4,
         scalars + [pltpu.VMEM(((tiles - 1) * TILE, width), BF16)] * 2 + [pltpu.SemaphoreType.DMA((4,))],
     )
     received = [swap(x, "seq", 1) for x in sent]
 
-    query_grad, part, main = call(
+    query_grad, part, main, weight, mains = call(
         functools.partial(own_kernel, captions, tiles, heads),
         "own_tiles",
-        (like(rows_here, width), like(2, L, width, dtype=F32), like(2, L, width)),
+        (
+            like(rows_here, width),
+            like(2, L, width, dtype=F32),
+            like(2, L, width),
+            like(key_weight.shape[0], 2 * width),
+            like(seq_count, 128, dtype=jnp.int32),
+        ),
         held_back,
-        [hbm] * 5,
+        [hbm] * 7,
         scalars
         + [pltpu.VMEM((rows_here, width), BF16)] * 2
         + [
             pltpu.VMEM((heads, 2, slots, L, DH), BF16),
             pltpu.VMEM((heads, rows_here, DH), BF16),
-            pltpu.SemaphoreType.DMA((4 + heads,)),
+            pltpu.SemaphoreType.DMA((6 + heads,)),
             pltpu.SemaphoreType.DMA((heads,)),
         ],
         limit=KERNEL_LIMIT,
         hint_us=5.0,
-        out_specs=(hbm, vmem, vmem),
+        out_specs=(hbm, vmem, vmem, vmem, vmem),
     )
     for tile in received[:-1]:
         part = call(
@@ -271,53 +302,51 @@
             limit=KERNEL_LIMIT,
             hint_us=2.0,
         )
-    blocks = like(seq_count, block_rows, width)
-    both, sent, kept = call(
+    half = like(seq_count // 2, block_rows, 2 * width)
+    both, kept, sent = call(
         functools.partial(first_text_kernel, heads, seq_count),
         "first_text",
-        (like(L, 2 * width), blocks, blocks),
-        (received[-1], main, part, key_weight, value_weight),
-        [vmem] * 5,
+        (like(L, 2 * width), half, half),
+        (received[-1], main, part, weight),
+        [vmem] * 4,
         limit=KERNEL_LIMIT,
         hint_us=3.0,
     )
-    sent_own, kept_own = call(
+    kept_own, sent_own = call(
         second_text_kernel,
         "second_text",
-        (blocks, blocks),
-        (both, key_weight, value_weight),
-        [vmem] * 3,
+        (half, half),
+        (both, weight),
+        [vmem] * 2,
         limit=KERNEL_LIMIT,
         hint_us=1.0,
     )
-    far = call(
-        pair_kernel,
-        "pair",
-        (like(CHUNK, block_rows, width),) * (seq_count // CHUNK),
-        (kept, swap(sent, "head", 1)),
-        [vmem] * 2,
-    )
+    block = like(block_rows, 2 * width)
+    far = call(pair_kernel, "pair", (block,) * (seq_count // 2), (kept, swap(sent, "head", 1)), [vmem] * 2)
     came_own = swap(sent_own, "head", 1)
-    order, arrived = [], []
-    half = seq_count // 2
-    for i in [*range(half // CHUNK, seq_count // CHUNK), *reversed(range(half // CHUNK))]:
-        first = i * CHUNK
+    quarter = seq_count // 4
+    bases = [2 * (quarter + i) for i in range(quarter)] + [2 * (quarter - 1 - i) for i in range(quarter)]
+    arrived, own = [], None
+    for i, base in enumerate(bases):
         mine = call(
-            functools.partial(cross_kernel, first),
+            functools.partial(cross_kernel, i),
             "cross",
-            (like(block_rows, width),) * CHUNK,
+            block,
             (kept_own, came_own, swap(far[i], "head", 2)),
             [vmem] * 3,
         )
-        for k, block in reversed(list(enumerate(mine, first))):
-            order.append(k)
-            arrived.append(swap(block, "seq", k) if k else block)
+        if base == 0:
+            own = mine
+        arrived.append(send(mine, base))
+    kept, sent = call(
+        functools.partial(caption_kernel, bases),
+        "captions",
+        (like(captions, block_rows, width, dtype=F32), like(captions, block_rows, width)),
+        (*arrived, own, mains),
+        [vmem] * (2 + len(bases)),
+    )
     text_grad = call(
-        functools.partial(final_kernel, order),
-        "final",
-        like(captions, block_rows, width),
-        (mains, *arrived),
-        [vmem] * (1 + seq_count),
+        final_kernel, "final", like(captions, block_rows, width), (kept, swap(sent, "head", 1)), [vmem] * 2
     )
     return query_grad, text_grad
 
@@ -398,7 +427,7 @@
 
 def solution(mesh):
     seq_count, head_devices = mesh.shape["seq"], mesh.shape["head"]
-    pairs = seq_count // SPAN <= 2 and seq_count % 2 == 0 and head_devices & (head_devices - 1) == 0
+    pairs = seq_count // SPAN <= 2 and seq_count & (seq_count - 1) == 0 and head_devices == 4
     placed = (
         P("seq", "head"),
         P("seq", "head"),

time: 40.6 us -> 37.9 us (0.933)
  starting transfers between devices: 19.5 us -> 14.7 us
  waiting for transfers between devices: 7.06 us -> 9.78 us
  Pallas kernels: 13.2 us -> 12.6 us
    ppermute x15 -> x9, starting transfers between devices: 19.5 us -> 7.92 us  [swap(): return lax.ppermute(array, axis, [(i, i ^ bit) for i in range(n)])]
    ppermute x0 -> x4, starting transfers between devices: none -> 6.74 us  [send(): return lax.ppermute(block, ('seq', 'head'), pairs)]
    ppermute x0 -> x4, waiting for transfers between devices: none -> 4.8 us  [send(): return lax.ppermute(block, ('seq', 'head'), pairs)]
    ppermute x15 -> x9, waiting for transfers between devices: 7.06 us -> 4.99 us  [swap(): return lax.ppermute(array, axis, [(i, i ^ bit) for i in range(n)])]
    pallas_call x11 -> x12, Pallas kernels: 13.2 us -> 12.6 us  [call(): pl.pallas_call(kernel, out_shape=out_shape, in_specs=specs, out_specs=out...]
  transfers between devices with their start and end apart: 15 -> 13, of which waited for: 5 -> 7; matrix products, arithmetic and copies ran while one was open for 0% -> 0% of each run, Pallas kernels for 21% -> 22%
where the time goes in v4:
time: 37.9 us; the launch traced here: 37.7 us
  starting transfers between devices  14.7 us (39%)
  Pallas kernels  12.6 us (33%)
  waiting for transfers between devices  9.78 us (26%)
  between operations  0.75 us (2%)
    pallas_call x12, Pallas kernels, call(): pl.pallas_call(kernel, out_shape=out_shape, in_specs=specs, out_specs=out...  12.6 us
    ppermute x9, starting transfers between devices, swap(): return lax.ppermute(array, axis, [(i, i ^ bit) for i in range(n)])  7.92 us
    ppermute x4, starting transfers between devices, send(): return lax.ppermute(block, ('seq', 'head'), pairs)  6.74 us
    ppermute x9, waiting for transfers between devices, swap(): return lax.ppermute(array, axis, [(i, i ^ bit) for i in range(n)])  4.99 us
    ppermute x4, waiting for transfers between devices, send(): return lax.ppermute(block, ('seq', 'head'), pairs)  4.8 us
  transfers between devices with their start and end apart: 13, of which 7 were waited for; matrix products, arithmetic and copies ran while one was open for 0% of the time, Pallas kernels for 22%

profile of v4, /device:TPU:0, one launch (start us, length us, event | category | flops | bytes accessed | tf_op | source)
XLA Modules:
  0.0 37.7 jit_solution(14001127204835738468)
XLA Ops:
  0.6 1.1 %stage.1 = (bf16[2,128,384]{2,1,0:T(8,128)(2,1)S(1)}, bf16[2,128,384]{2,1,0:T(8,128)(2,1)S(1)}) custom-call(s32[2,3]{1,0:T(2,128)} %bitcast.2, s32[2,8]{1,0:T(2,128)} %bitcast.4, bf16[384,384]{1,0:T(8,128)(2,1)} %q_hbm.3, bf16[384,384]{1,0:T(8,128)(2,1)} %g_hbm.3), custom_call_target="tpu_custom_call" | custom-call | bytes 3600000 | tf_op jit(solution)/shard_map/stage/pallas_call | solution.py:229
  1.8 3.0 %collective-permute-start.1 = (bf16[2,128,384]{2,1,0:T(8,128)(2,1)S(1)}, bf16[2,128,384]{2,1,0:T(8,128)(2,1)S(1)}, u32[]{:S(2)}, u32[]{:S(2)}) collective-permute-start(bf16[2,128,384]{2,1,0:T(8,128)(2,1)S(1)} %get-tuple-element.23), channel_id=1, source_target_pairs={{0,4},{4,0},{8,12},{12,8},{16,20},{20,16},{24,28},{28,24},{1,5},{5... | collective-permute-start | bytes 589832 | tf_op jit(solution)/shard_map/ppermute | solution.py:213
  4.9 5.6 %own_tiles.1 = (bf16[384,384]{1,0:T(8,128)(2,1)}, f32[2,512,384]{2,1,0:T(8,128)S(1)}, bf16[2,512,384]{2,1,0:T(8,128)(2,1)S(1)}, bf16[1536,768]{1,0:T(8,128)(2,1)S(1)}, s32[8,128]{1,0:T(8,128)S(1)}) custom-call(s32[2,3]{1,0:T(2,128)} %bitcast.3, s32[2,8]{1,0:T(2,128)} %bitcast.5, bf16[384,384]{1,0:T(8,128)(2,1)} %q_hbm.3, bf16[384,384]{1,0:T(8,128)(2,1)} %g_hbm.3, ...), custom_call_target="tpu_custom_call" | custom-call | bytes 18000000 | tf_op jit(solution)/shard_map/own_tiles/pallas_call | solution.py:229
  10.5 1.5 %shipped_tile.1.part_ref = f32[2,512,384]{2,1,0:T(8,128)S(1)} custom-call(bf16[2,128,384]{2,1,0:T(8,128)(2,1)S(1)} %collective-permute-done.1.recv_ref, bf16[2,512,384]{2,1,0:T(8,128)(2,1)S(1)} %get-tuple-element.22.main_ref, f32[2,512,384]{2,1,0:T(8,128)S(1)} %get-tuple-element.24.part_ref), custom_call_target="tpu_custom_call" | custom-call | bytes 7200000 | tf_op jit(solution)/shard_map/shipped_tile/pallas_call | solution.py:229
  12.1 1.8 %collective-permute-done.recv_ref = bf16[2,128,384]{2,1,0:T(8,128)(2,1)S(1)} collective-permute-done((bf16[2,128,384]{2,1,0:T(8,128)(2,1)S(1)}, bf16[2,128,384]{2,1,0:T(8,128)(2,1)S(1)}, u32[]{:S(2)}, u32[]{:S(2)}) %collective-permute-start) | collective-permute-done | bytes 196640 | tf_op jit(solution)/shard_map/ppermute | solution.py:213
  13.9 2.3 %first_text.1 = (bf16[512,768]{1,0:T(8,128)(2,1)S(1)}, bf16[4,64,768]{2,1,0:T(8,128)(2,1)S(1)}, bf16[4,64,768]{2,1,0:T(8,128)(2,1)S(1)}) custom-call(bf16[2,128,384]{2,1,0:T(8,128)(2,1)S(1)} %collective-permute-done.recv_ref, bf16[2,512,384]{2,1,0:T(8,128)(2,1)S(1)} %get-tuple-element.22.main_ref, f32[2,512,384]{2,1,0:T(8,128)S(1)} %shipped_tile.1.part_ref, ...), custom_call_target="tpu_custom_call" | custom-call | bytes 10800000 | tf_op jit(solution)/shard_map/first_text/pallas_call | solution.py:229
  16.3 0.8 %second_text.1 = (bf16[4,64,768]{2,1,0:T(8,128)(2,1)S(1)}, bf16[4,64,768]{2,1,0:T(8,128)(2,1)S(1)}) custom-call(bf16[512,768]{1,0:T(8,128)(2,1)S(1)} %get-tuple-element.26.both_ref, bf16[1536,768]{1,0:T(8,128)(2,1)S(1)} %get-tuple-element.25.weight_ref), custom_call_target="tpu_custom_call" | custom-call | bytes 3600000 | tf_op jit(solution)/shard_map/second_text/pallas_call | solution.py:229
  17.1 0.6 %collective-permute-start.2 = (bf16[4,64,768]{2,1,0:T(8,128)(2,1)S(1)}, bf16[4,64,768]{2,1,0:T(8,128)(2,1)S(1)}, u32[]{:S(2)}, u32[]{:S(2)}) collective-permute-start(bf16[4,64,768]{2,1,0:T(8,128)(2,1)S(1)} %get-tuple-element.28), channel_id=1, source_target_pairs={{0,1},{1,0},{2,3},{3,2},{4,5},{5,4},{6,7},{7,6},{8,9},{9,8},{10,11... | collective-permute-start | bytes 1179656 | tf_op jit(solution)/shard_map/ppermute | solution.py:213
  17.7 0.3 collective-permute-done.3.came_ref
  18.0 0.1 pair.1
  18.1 1.8 %collective-permute-start.4 = (bf16[64,768]{1,0:T(8,128)(2,1)S(1)}, bf16[64,768]{1,0:T(8,128)(2,1)S(1)}, u32[]{:S(2)}, u32[]{:S(2)}) collective-permute-start(bf16[64,768]{1,0:T(8,128)(2,1)S(1)} %get-tuple-element.31), channel_id=1, source_target_pairs={{0,2},{1,3},{2,0},{3,1},{4,6},{5,7},{6,4},{7,5},{8,10},{9,11},{10,... | collective-permute-start | bytes 294920 | tf_op jit(solution)/shard_map/ppermute | solution.py:213
  19.9 0.3 collective-permute-start.6
  20.2 1.7 %collective-permute-start.8 = (bf16[64,768]{1,0:T(8,128)(2,1)S(1)}, bf16[64,768]{1,0:T(8,128)(2,1)S(1)}, u32[]{:S(2)}, u32[]{:S(2)}) collective-permute-start(bf16[64,768]{1,0:T(8,128)(2,1)S(1)} %get-tuple-element.33), channel_id=1, source_target_pairs={{0,2},{1,3},{2,0},{3,1},{4,6},{5,7},{6,4},{7,5},{8,10},{9,11},{10,... | collective-permute-start | bytes 294920 | tf_op jit(solution)/shard_map/ppermute | solution.py:213
  21.9 0.3 collective-permute-start.10
  22.2 1.5 %collective-permute-done.4.crossed_ref = bf16[64,768]{1,0:T(8,128)(2,1)S(1)} collective-permute-done((bf16[64,768]{1,0:T(8,128)(2,1)S(1)}, bf16[64,768]{1,0:T(8,128)(2,1)S(1)}, u32[]{:S(2)}, u32[]{:S(2)}) %collective-permute-start.4) | collective-permute-done | bytes 98336 | tf_op jit(solution)/shard_map/ppermute | solution.py:213
  23.8 2.9 %collective-permute-start.5 = (bf16[64,768]{1,0:T(8,128)(2,1)S(1)}, bf16[64,768]{1,0:T(8,128)(2,1)S(1)}, u32[]{:S(2)}, u32[]{:S(2)}) collective-permute-start(bf16[64,768]{1,0:T(8,128)(2,1)S(1)} %cross.4), channel_id=1, source_target_pairs={{0,16},{1,21},{2,18},{3,23},{4,20},{5,17},{6,22},{7,19},{8,24},{9,... | collective-permute-start | bytes 294920 | tf_op jit(solution)/shard_map/ppermute | solution.py:224
  26.8 3.1 %collective-permute-start.7 = (bf16[64,768]{1,0:T(8,128)(2,1)S(1)}, bf16[64,768]{1,0:T(8,128)(2,1)S(1)}, u32[]{:S(2)}, u32[]{:S(2)}) collective-permute-start(bf16[64,768]{1,0:T(8,128)(2,1)S(1)} %cross.5), channel_id=1, source_target_pairs={{0,24},{1,29},{2,26},{3,31},{4,28},{5,25},{6,30},{7,27},{8,16},{9,... | collective-permute-start | bytes 294920 | tf_op jit(solution)/shard_map/ppermute | solution.py:224
  30.1 0.7 %collective-permute-start.11 = (bf16[64,768]{1,0:T(8,128)(2,1)S(1)}, bf16[64,768]{1,0:T(8,128)(2,1)S(1)}, u32[]{:S(2)}, u32[]{:S(2)}) collective-permute-start(bf16[64,768]{1,0:T(8,128)(2,1)S(1)} %cross.7.refs_4_), channel_id=1, source_target_pairs={{1,5},{3,7},{5,1},{7,3},{9,13},{11,15},{13,9},{15,11},{17,21},{19,... | collective-permute-start | bytes 294920 | tf_op jit(solution)/shard_map/ppermute | solution.py:224
  30.7 3.3 %collective-permute-done.5.refs_0_ = bf16[64,768]{1,0:T(8,128)(2,1)S(1)} collective-permute-done((bf16[64,768]{1,0:T(8,128)(2,1)S(1)}, bf16[64,768]{1,0:T(8,128)(2,1)S(1)}, u32[]{:S(2)}, u32[]{:S(2)}) %collective-permute-start.5) | collective-permute-done | bytes 98336 | tf_op jit(solution)/shard_map/ppermute | solution.py:224
  34.0 0.1 collective-permute-done.7.refs_1_
  34.1 1.4 %collective-permute-done.9.refs_2_ = bf16[64,768]{1,0:T(8,128)(2,1)S(1)} collective-permute-done((bf16[64,768]{1,0:T(8,128)(2,1)S(1)}, bf16[64,768]{1,0:T(8,128)(2,1)S(1)}, u32[]{:S(2)}, u32[]{:S(2)}) %collective-permute-start.9) | collective-permute-done | bytes 98336 | tf_op jit(solution)/shard_map/ppermute | solution.py:224
  35.5 0.2 captions.1
  35.8 1.3 %collective-permute-done.12.came_ref = bf16[2,64,384]{2,1,0:T(8,128)(2,1)S(1)} collective-permute-done((bf16[2,64,384]{2,1,0:T(8,128)(2,1)S(1)}, bf16[2,64,384]{2,1,0:T(8,128)(2,1)S(1)}, u32[]{:S(2)}, u32[]{:S(2)}) %collective-permute-start.12) | collective-permute-done | bytes 98336 | tf_op jit(solution)/shard_map/ppermute | solution.py:213
  37.1 0.7 %final.1 = bf16[2,64,384]{2,1,0:T(8,128)(2,1)} custom-call(f32[2,64,384]{2,1,0:T(8,128)S(1)} %get-tuple-element.36.kept_ref, bf16[2,64,384]{2,1,0:T(8,128)(2,1)S(1)} %collective-permute-done.12.came_ref), custom_call_target="tpu_custom_call" | custom-call | bytes 3600000 | tf_op jit(solution)/shard_map/final/pallas_call | solution.py:229
  (14 shorter events, 0.5 us)
Async XLA Ops:
  1.8 8.8 %collective-permute-start.1 = (bf16[2,128,384]{2,1,0:T(8,128)(2,1)S(1)}, bf16[2,128,384]{2,1,0:T(8,128)(2,1)S(1)}, u32[]{:S(2)}, u32[]{:S(2)}) collective-permute-start(bf16[2,128,384]{2,1,0:T(8,128)(2,1)S(1)} %get-tuple-element.23), channel_id=1, source_target_pairs={{0,4},{4,0},{8,12},{12,8},{16,20},{20,16},{24,28},{28,24},{1,5},{5... | collective-permute-start | bytes 589832 | tf_op jit(solution)/shard_map/ppermute | solution.py:213
  4.8 9.1 %collective-permute-start = (bf16[2,128,384]{2,1,0:T(8,128)(2,1)S(1)}, bf16[2,128,384]{2,1,0:T(8,128)(2,1)S(1)}, u32[]{:S(2)}, u32[]{:S(2)}) collective-permute-start(bf16[2,128,384]{2,1,0:T(8,128)(2,1)S(1)} %get-tuple-element.21), channel_id=1, source_target_pairs={{0,4},{4,0},{8,12},{12,8},{16,20},{20,16},{24,28},{28,24},{1,5},{5... | collective-permute-start | bytes 589832 | tf_op jit(solution)/shard_map/ppermute | solution.py:213
  16.2 1.8 %collective-permute-start.3 = (bf16[4,64,768]{2,1,0:T(8,128)(2,1)S(1)}, bf16[4,64,768]{2,1,0:T(8,128)(2,1)S(1)}, u32[]{:S(2)}, u32[]{:S(2)}) collective-permute-start(bf16[4,64,768]{2,1,0:T(8,128)(2,1)S(1)} %get-tuple-element.30), channel_id=1, source_target_pairs={{0,1},{1,0},{2,3},{3,2},{4,5},{5,4},{6,7},{7,6},{8,9},{9,8},{10,11... | collective-permute-start | bytes 1179656 | tf_op jit(solution)/shard_map/ppermute | solution.py:213
  17.1 5.1 %collective-permute-start.2 = (bf16[4,64,768]{2,1,0:T(8,128)(2,1)S(1)}, bf16[4,64,768]{2,1,0:T(8,128)(2,1)S(1)}, u32[]{:S(2)}, u32[]{:S(2)}) collective-permute-start(bf16[4,64,768]{2,1,0:T(8,128)(2,1)S(1)} %get-tuple-element.28), channel_id=1, source_target_pairs={{0,1},{1,0},{2,3},{3,2},{4,5},{5,4},{6,7},{7,6},{8,9},{9,8},{10,11... | collective-permute-start | bytes 1179656 | tf_op jit(solution)/shard_map/ppermute | solution.py:213
  18.1 5.6 %collective-permute-start.4 = (bf16[64,768]{1,0:T(8,128)(2,1)S(1)}, bf16[64,768]{1,0:T(8,128)(2,1)S(1)}, u32[]{:S(2)}, u32[]{:S(2)}) collective-permute-start(bf16[64,768]{1,0:T(8,128)(2,1)S(1)} %get-tuple-element.31), channel_id=1, source_target_pairs={{0,2},{1,3},{2,0},{3,1},{4,6},{5,7},{6,4},{7,5},{8,10},{9,11},{10,... | collective-permute-start | bytes 294920 | tf_op jit(solution)/shard_map/ppermute | solution.py:213
  19.9 6.9 %collective-permute-start.6 = (bf16[64,768]{1,0:T(8,128)(2,1)S(1)}, bf16[64,768]{1,0:T(8,128)(2,1)S(1)}, u32[]{:S(2)}, u32[]{:S(2)}) collective-permute-start(bf16[64,768]{1,0:T(8,128)(2,1)S(1)} %get-tuple-element.32), channel_id=1, source_target_pairs={{0,2},{1,3},{2,0},{3,1},{4,6},{5,7},{6,4},{7,5},{8,10},{9,11},{10,... | collective-permute-start | bytes 294920 | tf_op jit(solution)/shard_map/ppermute | solution.py:213
  20.2 9.7 %collective-permute-start.8 = (bf16[64,768]{1,0:T(8,128)(2,1)S(1)}, bf16[64,768]{1,0:T(8,128)(2,1)S(1)}, u32[]{:S(2)}, u32[]{:S(2)}) collective-permute-start(bf16[64,768]{1,0:T(8,128)(2,1)S(1)} %get-tuple-element.33), channel_id=1, source_target_pairs={{0,2},{1,3},{2,0},{3,1},{4,6},{5,7},{6,4},{7,5},{8,10},{9,11},{10,... | collective-permute-start | bytes 294920 | tf_op jit(solution)/shard_map/ppermute | solution.py:213
  21.9 8.1 %collective-permute-start.10 = (bf16[64,768]{1,0:T(8,128)(2,1)S(1)}, bf16[64,768]{1,0:T(8,128)(2,1)S(1)}, u32[]{:S(2)}, u32[]{:S(2)}) collective-permute-start(bf16[64,768]{1,0:T(8,128)(2,1)S(1)} %get-tuple-element.34), channel_id=1, source_target_pairs={{0,2},{1,3},{2,0},{3,1},{4,6},{5,7},{6,4},{7,5},{8,10},{9,11},{10,... | collective-permute-start | bytes 294920 | tf_op jit(solution)/shard_map/ppermute | solution.py:213
  23.8 10.2 %collective-permute-start.5 = (bf16[64,768]{1,0:T(8,128)(2,1)S(1)}, bf16[64,768]{1,0:T(8,128)(2,1)S(1)}, u32[]{:S(2)}, u32[]{:S(2)}) collective-permute-start(bf16[64,768]{1,0:T(8,128)(2,1)S(1)} %cross.4), channel_id=1, source_target_pairs={{0,16},{1,21},{2,18},{3,23},{4,20},{5,17},{6,22},{7,19},{8,24},{9,... | collective-permute-start | bytes 294920 | tf_op jit(solution)/shard_map/ppermute | solution.py:224
  26.8 7.3 %collective-permute-start.7 = (bf16[64,768]{1,0:T(8,128)(2,1)S(1)}, bf16[64,768]{1,0:T(8,128)(2,1)S(1)}, u32[]{:S(2)}, u32[]{:S(2)}) collective-permute-start(bf16[64,768]{1,0:T(8,128)(2,1)S(1)} %cross.5), channel_id=1, source_target_pairs={{0,24},{1,29},{2,26},{3,31},{4,28},{5,25},{6,30},{7,27},{8,16},{9,... | collective-permute-start | bytes 294920 | tf_op jit(solution)/shard_map/ppermute | solution.py:224
  29.9 5.6 %collective-permute-start.9 = (bf16[64,768]{1,0:T(8,128)(2,1)S(1)}, bf16[64,768]{1,0:T(8,128)(2,1)S(1)}, u32[]{:S(2)}, u32[]{:S(2)}) collective-permute-start(bf16[64,768]{1,0:T(8,128)(2,1)S(1)} %cross.6), channel_id=1, source_target_pairs={{0,8},{1,13},{2,10},{3,15},{4,12},{5,9},{6,14},{7,11},{8,0},{9,5},... | collective-permute-start | bytes 294920 | tf_op jit(solution)/shard_map/ppermute | solution.py:224
  30.1 5.5 %collective-permute-start.11 = (bf16[64,768]{1,0:T(8,128)(2,1)S(1)}, bf16[64,768]{1,0:T(8,128)(2,1)S(1)}, u32[]{:S(2)}, u32[]{:S(2)}) collective-permute-start(bf16[64,768]{1,0:T(8,128)(2,1)S(1)} %cross.7.refs_4_), channel_id=1, source_target_pairs={{1,5},{3,7},{5,1},{7,3},{9,13},{11,15},{13,9},{15,11},{17,21},{19,... | collective-permute-start | bytes 294920 | tf_op jit(solution)/shard_map/ppermute | solution.py:224
  35.7 1.4 %collective-permute-start.12 = (bf16[2,64,384]{2,1,0:T(8,128)(2,1)S(1)}, bf16[2,64,384]{2,1,0:T(8,128)(2,1)S(1)}, u32[]{:S(2)}, u32[]{:S(2)}) collective-permute-start(bf16[2,64,384]{2,1,0:T(8,128)(2,1)S(1)} %get-tuple-element.37), channel_id=1, source_target_pairs={{0,1},{1,0},{2,3},{3,2},{4,5},{5,4},{6,7},{7,6},{8,9},{9,8},{10,11... | collective-permute-start | bytes 294920 | tf_op jit(solution)/shard_map/ppermute | solution.py:213

commit v5 on v4

--- a/solution.py
+++ b/solution.py
@@ -23,17 +23,17 @@
     return lax.dot_general(a, b, ((contract[:1], contract[1:]), ((), ())), preferred_element_type=F32)
 
 
-def held(caps_ref, d, captions):
-    first, second = caps_ref[0, d], caps_ref[1, d]
-    single = jnp.logical_or(first == captions, second == captions)
-    return single, jnp.where(first == captions, second, first)
-
-
-def main_slot(caps_ref, d, captions):
-    single, _ = held(caps_ref, d, captions)
-    _, other = held(caps_ref, jnp.bitwise_xor(d, 1), captions)
-    first = caps_ref[0, d]
-    return jnp.where(single, jnp.where(first == captions, 1, 0), jnp.where(first == other, 1, 0))
+def shipping(mask_ref, caps_ref, me, seq_count, tiles):
+    odd = jnp.bitwise_and(me, 1)
+    ones = mask_ref[1, 0]
+    for t in range(1, tiles):
+        ones += mask_ref[1, t]
+    most = jnp.where(2 * ones > tiles, 1, 0)
+    outer = jnp.where(odd == 0, 0, tiles - 1)
+    at_end = jnp.where(odd == 0, me == 0, me == seq_count - 1)
+    alone = jnp.logical_and(at_end, mask_ref[1 - most, outer] == 1)
+    main = jnp.where(alone, 1 - most, most)
+    return main, tiles - 1 - outer, jnp.where(alone, tiles // 2, outer)
 
 
 def backward(key, value, query, grad):
@@ -55,104 +55,87 @@
     return copies
 
 
-def stage_kernel(captions, tiles, mask_hbm, caps_hbm, q_hbm, g_hbm, *refs):
-    *sent, mask_ref, caps_ref, q_buf, g_buf, sems = refs
+def stage_kernel(seq_count, tiles, mask_hbm, caps_hbm, q_hbm, g_hbm, cache_hbm, *refs):
+    y_ref, z_ref, q_ref, g_ref, cache_ref, flags_ref, caption_ref, mask_ref, caps_ref, sems = refs
     me = lax.axis_index("seq")
-    first = 1 - jnp.bitwise_and(me, 1)
-    rows = pl.ds(pl.multiple_of(first * TILE, TILE), (tiles - 1) * TILE)
     copies = fetch(
-        [(mask_hbm, mask_ref), (caps_hbm, caps_ref), (q_hbm.at[rows], q_buf), (g_hbm.at[rows], g_buf)], sems
-    )
-    for c in copies:
+        [
+            (mask_hbm, mask_ref),
+            (caps_hbm, caps_ref),
+            (q_hbm, q_ref),
+            (g_hbm, g_ref),
+            (cache_hbm.at[:, :, :, pl.ds(0, DH)], cache_ref),
+        ],
+        sems,
+    )
+    for c in copies[:4]:
         c.wait()
-    mine = main_slot(caps_ref, me, captions)
-    for i, out in enumerate(sent):
-        keep = (mask_ref[mine, first + i] == 0).astype(F32).astype(BF16)
-        at = slice(i * TILE, (i + 1) * TILE)
-        out[0] = q_buf[at, :] * keep
-        out[1] = g_buf[at, :] * keep
+    mine, *picked = shipping(mask_ref, caps_ref, me, seq_count, tiles)
+    for tile, out in zip(picked, (y_ref, z_ref), strict=True):
+        keep = (mask_ref[mine, tile] == 0).astype(F32).astype(BF16)
+        at = pl.ds(pl.multiple_of(tile * TILE, TILE), TILE)
+        out[0] = q_ref[at, :] * keep
+        out[1] = g_ref[at, :] * keep
+    lanes = (1, flags_ref.shape[1])
+    for t in range(tiles):
+        flags_ref[t : t + 1, :] = jnp.full(lanes, mask_ref[1, t].astype(F32), F32)
+        flags_ref[tiles + t : tiles + t + 1, :] = jnp.full(lanes, mask_ref[mine, t].astype(F32), F32)
+    flags_ref[2 * tiles : 2 * tiles + 1, :] = jnp.full(lanes, mine.astype(F32), F32)
+    caption_ref[...] = jnp.full(caption_ref.shape, caps_ref[mine, me].astype(F32), F32).astype(BF16)
+    copies[4].wait()
+
+
+def pick(flag, pair):
+    return pair[0] * (1.0 - flag).astype(BF16) + pair[1] * flag.astype(BF16)
 
 
 def own_kernel(
-    captions, tiles, heads, mask_hbm, caps_hbm, q_hbm, g_hbm, cache_hbm, wk_hbm, wv_hbm,
-    dq_hbm, part_ref, main_ref, weight_ref, mains_ref, mask_ref, caps_ref, q_buf, g_buf, cache_buf, dq_buf, sems, out_sems,
+    tiles, heads, flags_ref, q_ref, g_ref, first_ref, cache_hbm, wk_hbm, wv_hbm,
+    dq_hbm, part_ref, main_ref, weight_ref, cache_buf, dq_buf, sems, out_sems,
 ):
-    me = lax.axis_index("seq")
-    pairs = [(mask_hbm, mask_ref), (caps_hbm, caps_ref), (q_hbm, q_buf), (g_hbm, g_buf)]
-    pairs += [(cache_hbm.at[:, :, :, pl.ds(h * DH, DH)], cache_buf.at[h]) for h in range(heads)]
+    pairs = [(cache_hbm.at[:, :, :, pl.ds(h * DH, DH)], cache_buf.at[h - 1]) for h in range(1, heads)]
     width = heads * DH
     pairs += [(wk_hbm, weight_ref.at[:, pl.ds(0, width)]), (wv_hbm, weight_ref.at[:, pl.ds(width, width)])]
     copies = fetch(pairs, sems)
-    for c in copies[:4]:
-        c.wait()
-    mine = main_slot(caps_ref, me, captions)
-    slots = [jnp.where(mask_ref[1, t] == 1, 1, 0) for t in range(tiles)]
-    keeps = [(slot == mine).astype(F32).astype(BF16) for slot in slots]
+    slots = [flags_ref[t : t + 1, :] for t in range(tiles)]
+    keeps = [flags_ref[tiles + t : tiles + t + 1, :] for t in range(tiles)]
+    mine = flags_ref[2 * tiles : 2 * tiles + 1, :]
     stores = []
     for h in range(heads):
         cols = slice(h * DH, (h + 1) * DH)
-        copies[4 + h].wait()
+        if h:
+            copies[h - 1].wait()
+        cache = first_ref if h == 0 else cache_buf.at[h - 1]
+        keys, values = (cache[0, 0], cache[0, 1]), (cache[1, 0], cache[1, 1])
         probs, grads, queries, outs = [], [], [], []
         for t in range(tiles):
             rows = slice(t * TILE, (t + 1) * TILE)
-            query, grad = q_buf[rows, cols], g_buf[rows, cols]
-            key, value = cache_buf[h, 0, slots[t]], cache_buf[h, 1, slots[t]]
-            attention_lo, score_lo = backward(key, value, query, grad)
+            query, grad = q_ref[rows, cols], g_ref[rows, cols]
+            attention_lo, score_lo = backward(pick(slots[t], keys), pick(slots[t], values), query, grad)
             probs.append(attention_lo)
             grads.append(score_lo)
-            queries.append(query * keeps[t])
-            outs.append(grad * keeps[t])
+            queries.append(query * keeps[t].astype(BF16))
+            outs.append(grad * keeps[t].astype(BF16))
         score_grads = jnp.concatenate(grads, axis=1)
-        dq_main = dot(cache_buf[h, 0, mine].T, score_grads, (1, 0)) * INV_ROOT
-        dq_other = dot(cache_buf[h, 0, 1 - mine].T, score_grads, (1, 0)) * INV_ROOT
+        dq = [dot(key.T, score_grads, (1, 0)) * INV_ROOT for key in keys]
         for t in range(tiles):
             rows = slice(t * TILE, (t + 1) * TILE)
-            dq_t = jnp.where(slots[t] == mine, dq_main[:, rows], dq_other[:, rows])
+            dq_t = jnp.where(slots[t] == 1.0, dq[1][:, rows], dq[0][:, rows])
             dq_buf[h, rows, :] = dq_t.astype(BF16).T
         store = pltpu.make_async_copy(dq_buf.at[h], dq_hbm.at[:, pl.ds(h * DH, DH)], out_sems.at[h])
         store.start()
         stores.append(store)
         part_ref[0, :, cols] = dot(score_grads, jnp.concatenate(queries, axis=0), (1, 0))
         part_ref[1, :, cols] = dot(jnp.concatenate(probs, axis=1), jnp.concatenate(outs, axis=0), (1, 0))
-        main_ref[0, :, cols] = cache_buf[h, 0, mine]
-        main_ref[1, :, cols] = cache_buf[h, 1, mine]
-    for k in range(mains_ref.shape[0]):
-        source = jnp.bitwise_xor(me, k)
-        main = caps_ref[main_slot(caps_ref, source, captions), source]
-        mains_ref[k : k + 1, :] = jnp.full((1, mains_ref.shape[1]), main, jnp.int32)
-    for copy in stores + copies[4 + heads :]:
+        main_ref[0, :, cols] = pick(mine, keys)
+        main_ref[1, :, cols] = pick(mine, values)
+    for copy in stores + copies[heads - 1 :]:
         copy.wait()
 
 
-def shipped(heads, recv_ref, main_ref, h):
-    cols = slice(h * DH, (h + 1) * DH)
-    query, grad = recv_ref[0, :, cols], recv_ref[1, :, cols]
-    attention_lo, score_lo = backward(main_ref[0, :, cols], main_ref[1, :, cols], query, grad)
-    return dot(score_lo, query, (1, 0)), dot(attention_lo, grad, (1, 0))
-
-
-def shipped_kernel(heads, recv_ref, main_ref, part_ref, out_ref):
-    for h in range(heads):
-        cols = slice(h * DH, (h + 1) * DH)
-        dk, dv = shipped(heads, recv_ref, main_ref, h)
-        out_ref[0, :, cols] = part_ref[0, :, cols] + dk
-        out_ref[1, :, cols] = part_ref[1, :, cols] + dv
-
-
-def project(both_ref, weight_ref, rel, kept_ref, sent_ref):
-    features = kept_ref.shape[2]
-    chip = jnp.right_shift(lax.axis_index("head"), 1)
-    rows = pl.ds(pl.multiple_of(jnp.bitwise_xor(chip, rel) * features, features), features)
-    text = dot(both_ref[...], weight_ref[rows, :], (1, 1)).astype(BF16)
-    half = text.shape[0] // 2
-    kept_ref[...] = text[:half].reshape(kept_ref.shape)
-    sent_ref[...] = text[half:].reshape(sent_ref.shape)
-
-
-def first_text_kernel(heads, blocks, recv_ref, main_ref, part_ref, weight_ref, both_ref, kept_ref, sent_ref):
+def gather_parts(heads, blocks, y_ref, z_ref, main_ref, part_ref, both_ref):
     me, core = lax.axis_index("seq"), jnp.bitwise_and(lax.axis_index("head"), 1)
-    width = heads * DH
-    block_rows = L // blocks
+    block_rows, width = L // blocks, heads * DH
     places = []
     for s in range(blocks):
         rel = jnp.bitwise_xor(jnp.bitwise_xor(me, s), core)
@@ -162,12 +145,27 @@
         places.append(pl.ds(pl.multiple_of(place * block_rows, block_rows), block_rows))
     for h in range(heads):
         cols = slice(h * DH, (h + 1) * DH)
-        dk, dv = shipped(heads, recv_ref, main_ref, h)
-        dk = ((part_ref[0, :, cols] + dk) * INV_ROOT).astype(BF16)
-        dv = (part_ref[1, :, cols] + dv).astype(BF16)
+        query, grad = y_ref[0, :, cols] + z_ref[0, :, cols], y_ref[1, :, cols] + z_ref[1, :, cols]
+        attention_lo, score_lo = backward(main_ref[0, :, cols], main_ref[1, :, cols], query, grad)
+        dk = ((part_ref[0, :, cols] + dot(score_lo, query, (1, 0))) * INV_ROOT).astype(BF16)
+        dv = (part_ref[1, :, cols] + dot(attention_lo, grad, (1, 0))).astype(BF16)
         for s, rows in enumerate(places):
             both_ref[rows, h * DH : (h + 1) * DH] = dk[s * block_rows : (s + 1) * block_rows]
             both_ref[rows, width + h * DH : width + (h + 1) * DH] = dv[s * block_rows : (s + 1) * block_rows]
+
+
+def project(both_ref, weight_ref, rel, kept_ref, sent_ref):
+    features = kept_ref.shape[2]
+    chip = jnp.right_shift(lax.axis_index("head"), 1)
+    rows = pl.ds(pl.multiple_of(jnp.bitwise_xor(chip, rel) * features, features), features)
+    text = dot(both_ref[...], weight_ref[rows, :], (1, 1)).astype(BF16)
+    half = text.shape[0] // 2
+    kept_ref[...] = text[:half].reshape(kept_ref.shape)
+    sent_ref[...] = text[half:].reshape(sent_ref.shape)
+
+
+def first_text_kernel(heads, blocks, y_ref, z_ref, main_ref, part_ref, weight_ref, both_ref, kept_ref, sent_ref):
+    gather_parts(heads, blocks, y_ref, z_ref, main_ref, part_ref, both_ref)
     project(both_ref, weight_ref, 1, kept_ref, sent_ref)
 
 
@@ -180,28 +178,43 @@
         out[...] = (kept_ref[i].astype(F32) + came_ref[i].astype(F32)).astype(BF16)
 
 
-def cross_kernel(i, kept_ref, came_ref, crossed_ref, out_ref):
+def cross_kernel(i, kept_ref, came_ref, crossed_ref, caption_ref, out_ref):
     pair = (kept_ref[i].astype(F32) + came_ref[i].astype(F32)).astype(BF16)
-    out_ref[...] = (pair.astype(F32) + crossed_ref[...].astype(F32)).astype(BF16)
+    total = (pair.astype(F32) + crossed_ref[...].astype(F32)).astype(BF16)
+    height, lanes = out_ref.shape[1:]
+    across = total.shape[1] // lanes
+    for n in range(out_ref.shape[0] - 1):
+        r, c = n // across * height, n % across * lanes
+        out_ref[n] = total[r : r + height, c : c + lanes]
+    out_ref[out_ref.shape[0] - 1] = caption_ref[...]
 
 
 def caption_kernel(bases, *refs):
-    *blocks, own_ref, mains_ref, kept_ref, sent_ref = refs
-    captions, _, width = kept_ref.shape
+    *blocks, own_ref, kept_ref, sent_ref = refs
+    captions, block_rows, width = kept_ref.shape
+    _, height, lanes = own_ref.shape
+    half = width // lanes
+    across = 2 * half
     core = jnp.bitwise_and(lax.axis_index("head"), 1)
-    totals = [0.0] * captions
-    for base, block in zip(bases, blocks, strict=True):
-        value = block[...].astype(F32)
-        if base == 0:
-            value = jnp.where(core == 0, own_ref[...].astype(F32), value)
-        main = mains_ref[pl.ds(base + core, 1), :]
-        main = jnp.tile(main, (1, value.shape[1] // main.shape[1]))
+    for r in range(block_rows // height):
+        totals = [[0.0] * across for _ in range(captions)]
+        for base, block in zip(bases, blocks, strict=True):
+            caption = block[block.shape[0] - 1].astype(F32)
+            if base == 0:
+                caption = jnp.where(core == 0, own_ref[own_ref.shape[0] - 1].astype(F32), caption)
+            for n in range(across):
+                value = block[r * across + n].astype(F32)
+                if base == 0:
+                    value = jnp.where(core == 0, own_ref[r * across + n].astype(F32), value)
+                for c in range(captions):
+                    totals[c][n] += jnp.where(caption == c, value, 0.0)
+        rows = slice(r * height, (r + 1) * height)
         for c in range(captions):
-            totals[c] += jnp.where(main == c, value, 0.0)
-    for c in range(captions):
-        low, high = totals[c][:, :width], totals[c][:, width:]
-        kept_ref[c] = jnp.where(core == 0, low, high)
-        sent_ref[c] = jnp.where(core == 0, high, low).astype(BF16)
+            for n in range(half):
+                cols = slice(n * lanes, (n + 1) * lanes)
+                low, high = totals[c][n], totals[c][half + n]
+                kept_ref[c, rows, cols] = jnp.where(core == 0, low, high)
+                sent_ref[c, rows, cols] = jnp.where(core == 0, high, low).astype(BF16)
 
 
 def final_kernel(kept_ref, came_ref, out_ref):
@@ -253,64 +266,64 @@
     mask_t, caps_t = held_back[:2]
     vmem = pl.BlockSpec(memory_space=pltpu.VMEM)
     hbm = pl.BlockSpec(memory_space=pltpu.HBM)
-    scalars = [pltpu.SMEM(mask_t.shape, jnp.int32), pltpu.SMEM(caps_t.shape, jnp.int32)]
 
     def like(*shape, dtype=BF16):
         return jax.ShapeDtypeStruct(shape, dtype)
 
-    sent = call(
-        functools.partial(stage_kernel, captions, tiles),
+    to_y, to_z, q_here, g_here, cache_first, flags, caption = call(
+        functools.partial(stage_kernel, seq_count, tiles),
         "stage",
-        (like(2, TILE, width),) * (tiles - 1),
-        held_back[:4],
-        [hbm] * 4,
-        scalars + [pltpu.VMEM(((tiles - 1) * TILE, width), BF16)] * 2 + [pltpu.SemaphoreType.DMA((4,))],
-    )
-    received = [swap(x, "seq", 1) for x in sent]
-
-    query_grad, part, main, weight, mains = call(
-        functools.partial(own_kernel, captions, tiles, heads),
+        (
+            like(2, TILE, width),
+            like(2, TILE, width),
+            like(rows_here, width),
+            like(rows_here, width),
+            like(2, slots, L, DH),
+            like(8 * (-(-(2 * tiles + 1) // 8)), 128, dtype=F32),
+            like(16, 128),
+        ),
+        held_back[:5],
+        [hbm] * 5,
+        [
+            pltpu.SMEM(mask_t.shape, jnp.int32),
+            pltpu.SMEM(caps_t.shape, jnp.int32),
+            pltpu.SemaphoreType.DMA((5,)),
+        ],
+        limit=KERNEL_LIMIT,
+    )
+    from_y = swap(to_y, "seq", 1)
+    from_z = lax.ppermute(to_z, "seq", [(s, (s + (2 if s & 1 else -2)) % seq_count) for s in range(seq_count)])
+
+    query_grad, part, main, weight = call(
+        functools.partial(own_kernel, tiles, heads),
         "own_tiles",
         (
             like(rows_here, width),
             like(2, L, width, dtype=F32),
             like(2, L, width),
             like(key_weight.shape[0], 2 * width),
-            like(seq_count, 128, dtype=jnp.int32),
         ),
-        held_back,
-        [hbm] * 7,
-        scalars
-        + [pltpu.VMEM((rows_here, width), BF16)] * 2
-        + [
-            pltpu.VMEM((heads, 2, slots, L, DH), BF16),
+        (flags, q_here, g_here, cache_first, *held_back[4:]),
+        [vmem] * 4 + [hbm] * 3,
+        [
+            pltpu.VMEM((heads - 1, 2, slots, L, DH), BF16),
             pltpu.VMEM((heads, rows_here, DH), BF16),
-            pltpu.SemaphoreType.DMA((6 + heads,)),
+            pltpu.SemaphoreType.DMA((heads + 1,)),
             pltpu.SemaphoreType.DMA((heads,)),
         ],
         limit=KERNEL_LIMIT,
         hint_us=5.0,
-        out_specs=(hbm, vmem, vmem, vmem, vmem),
-    )
-    for tile in received[:-1]:
-        part = call(
-            functools.partial(shipped_kernel, heads),
-            "shipped_tile",
-            like(2, L, width, dtype=F32),
-            (tile, main, part),
-            [vmem] * 3,
-            limit=KERNEL_LIMIT,
-            hint_us=2.0,
-        )
+        out_specs=(hbm, vmem, vmem, vmem),
+    )
     half = like(seq_count // 2, block_rows, 2 * width)
     both, kept, sent = call(
         functools.partial(first_text_kernel, heads, seq_count),
         "first_text",
         (like(L, 2 * width), half, half),
-        (received[-1], main, part, weight),
-        [vmem] * 4,
+        (from_y, from_z, main, part, weight),
+        [vmem] * 5,
         limit=KERNEL_LIMIT,
-        hint_us=3.0,
+        hint_us=2.0,
     )
     kept_own, sent_own = call(
         second_text_kernel,
@@ -331,19 +344,19 @@
         mine = call(
             functools.partial(cross_kernel, i),
             "cross",
-            block,
-            (kept_own, came_own, swap(far[i], "head", 2)),
-            [vmem] * 3,
+            like(block_rows // 16 * (2 * width // 128) + 1, 16, 128),
+            (kept_own, came_own, swap(far[i], "head", 2), caption),
+            [vmem] * 4,
         )
         if base == 0:
             own = mine
         arrived.append(send(mine, base))
     kept, sent = call(
-        functools.partial(caption_kernel, bases),
+        functools.partial(caption_kernel, bases[::-1]),
         "captions",
         (like(captions, block_rows, width, dtype=F32), like(captions, block_rows, width)),
-        (*arrived, own, mains),
-        [vmem] * (2 + len(bases)),
+        (*reversed(arrived), own),
+        [vmem] * (1 + len(bases)),
     )
     text_grad = call(
         final_kernel, "final", like(captions, block_rows, width), (kept, swap(sent, "head", 1)), [vmem] * 2
@@ -427,7 +440,7 @@
 
 def solution(mesh):
     seq_count, head_devices = mesh.shape["seq"], mesh.shape["head"]
-    pairs = seq_count // SPAN <= 2 and seq_count & (seq_count - 1) == 0 and head_devices == 4
+    pairs = seq_count // SPAN <= 2 and seq_count in (4, 8, 16, 32) and head_devices == 4
     placed = (
         P("seq", "head"),
         P("seq", "head"),

time: 37.9 us -> 36.5 us (0.963)
  Pallas kernels: 12.6 us -> 9.93 us
  starting transfers between devices: 14.7 us -> 17.1 us
  waiting for transfers between devices: 9.78 us -> 8.56 us
    ppermute x0 -> x1, starting transfers between devices: none -> 3.6 us  [shards_pairs(): lax.ppermute(to_z, 'seq', [(s, (s + (2 if s & 1 else -2)) % seq_count) fo...]
    pallas_call x12 -> x11, Pallas kernels: 12.6 us -> 9.93 us  [call(): pl.pallas_call(kernel, out_shape=out_shape, in_specs=specs, out_specs=out...]
    ppermute x4, starting transfers between devices: 6.74 us -> 5.57 us  [send(): return lax.ppermute(block, ('seq', 'head'), pairs)]
    ppermute x9 -> x8, waiting for transfers between devices: 4.99 us -> 4.21 us  [swap(): return lax.ppermute(array, axis, [(i, i ^ bit) for i in range(n)])]
    ppermute x4, waiting for transfers between devices: 4.8 us -> 4.35 us  [send(): return lax.ppermute(block, ('seq', 'head'), pairs)]
    ppermute x9 -> x8, starting transfers between devices: 7.92 us -> 7.9 us  [swap(): return lax.ppermute(array, axis, [(i, i ^ bit) for i in range(n)])]
  transfers between devices with their start and end apart: 13 -> 13, of which waited for: 7 -> 7; matrix products, arithmetic and copies ran while one was open for 0% -> 0% of each run, Pallas kernels for 22% -> 15%
where the time goes in v5:
time: 36.5 us; the launch traced here: 36.3 us
  starting transfers between devices  17.1 us (47%)
  Pallas kernels  9.93 us (27%)
  waiting for transfers between devices  8.56 us (23%)
  between operations  0.74 us (2%)
    pallas_call x11, Pallas kernels, call(): pl.pallas_call(kernel, out_shape=out_shape, in_specs=specs, out_specs=out...  9.93 us
    ppermute x8, starting transfers between devices, swap(): return lax.ppermute(array, axis, [(i, i ^ bit) for i in range(n)])  7.9 us
    ppermute x4, starting transfers between devices, send(): return lax.ppermute(block, ('seq', 'head'), pairs)  5.57 us
    ppermute x4, waiting for transfers between devices, send(): return lax.ppermute(block, ('seq', 'head'), pairs)  4.35 us
    ppermute x8, waiting for transfers between devices, swap(): return lax.ppermute(array, axis, [(i, i ^ bit) for i in range(n)])  4.21 us
    ppermute x1, starting transfers between devices, shards_pairs(): lax.ppermute(to_z, 'seq', [(s, (s + (2 if s & 1 else -2)) % seq_count) fo...  3.6 us
  transfers between devices with their start and end apart: 13, of which 7 were waited for; matrix products, arithmetic and copies ran while one was open for 0% of the time, Pallas kernels for 15%

profile of v5, /device:TPU:0, one launch (start us, length us, event | category | flops | bytes accessed | tf_op | source)
XLA Modules:
  0.0 36.3 jit_solution(2701302164456342786)
XLA Ops:
  0.6 1.3 %stage.1 = (bf16[2,128,384]{2,1,0:T(8,128)(2,1)S(1)}, bf16[2,128,384]{2,1,0:T(8,128)(2,1)S(1)}, bf16[384,384]{1,0:T(8,128)(2,1)S(1)}, bf16[384,384]{1,0:T(8,128)...) custom-call(s32[2,3]{1,0:T(2,128)} %bitcast.2, ...), custom_call_target="tpu_custom_call" | custom-call | bytes 3600000 | tf_op jit(solution)/shard_map/stage/pallas_call | solution.py:242
  1.9 3.0 %collective-permute-start = (bf16[2,128,384]{2,1,0:T(8,128)(2,1)S(1)}, bf16[2,128,384]{2,1,0:T(8,128)(2,1)S(1)}, u32[]{:S(2)}, u32[]{:S(2)}) collective-permute-start(bf16[2,128,384]{2,1,0:T(8,128)(2,1)S(1)} %get-tuple-element.29), channel_id=1, source_target_pairs={{0,4},{4,0},{8,12},{12,8},{16,20},{20,16},{24,28},{28,24},{1,5},{5... | collective-permute-start | bytes 589832 | tf_op jit(solution)/shard_map/ppermute | solution.py:226
  4.9 3.6 %collective-permute-start.1 = (bf16[2,128,384]{2,1,0:T(8,128)(2,1)S(1)}, bf16[2,128,384]{2,1,0:T(8,128)(2,1)S(1)}, u32[]{:S(2)}, u32[]{:S(2)}) collective-permute-start(bf16[2,128,384]{2,1,0:T(8,128)(2,1)S(1)} %get-tuple-element.30), channel_id=1, source_target_pairs={{0,24},{4,12},{8,0},{12,20},{16,8},{20,28},{24,16},{28,4},{1,25},{... | collective-permute-start | bytes 589832 | tf_op jit(solution)/shard_map/ppermute | solution.py:295
  8.5 4.4 %own_tiles.1 = (bf16[384,384]{1,0:T(8,128)(2,1)}, f32[2,512,384]{2,1,0:T(8,128)S(1)}, bf16[2,512,384]{2,1,0:T(8,128)(2,1)S(1)}, bf16[1536,768]{1,0:T(8,128)(2,1)S(1)}) custom-call(f32[8,128]{1,0:T(8,128)S(1)} %get-tuple-element.24.flags_ref, bf16[384,384]{1,0:T(8,128)(2,1)S(1)} %get-tuple-element.25.q_ref, bf16[384,384]{1,0:T(8,128)(2,1)S(1)} %get-tuple-element.26.g_ref, ...), custom_call_target="tpu_custom_call" | custom-call | bytes 18000000 | tf_op jit(solution)/shard_map/own_tiles/pallas_call | solution.py:242
  12.9 2.3 %first_text.1 = (bf16[512,768]{1,0:T(8,128)(2,1)S(1)}, bf16[4,64,768]{2,1,0:T(8,128)(2,1)S(1)}, bf16[4,64,768]{2,1,0:T(8,128)(2,1)S(1)}) custom-call(bf16[2,128,384]{2,1,0:T(8,128)(2,1)S(1)} %collective-permute-done.y_ref, bf16[2,128,384]{2,1,0:T(8,128)(2,1)S(1)} %collective-permute-done.1.z_ref, bf16[2,512,384]{2,1,0:T(8,128)(2,1)S(1)} %get-tuple-element.31.main_ref, ...), custom_call_target="tpu_custom_call" | custom-call | bytes 7200000 | tf_op jit(solution)/shard_map/first_text/pallas_call | solution.py:242
  15.4 0.8 %second_text.1 = (bf16[4,64,768]{2,1,0:T(8,128)(2,1)S(1)}, bf16[4,64,768]{2,1,0:T(8,128)(2,1)S(1)}) custom-call(bf16[512,768]{1,0:T(8,128)(2,1)S(1)} %get-tuple-element.34.both_ref, bf16[1536,768]{1,0:T(8,128)(2,1)S(1)} %get-tuple-element.33.weight_ref), custom_call_target="tpu_custom_call" | custom-call | bytes 3600000 | tf_op jit(solution)/shard_map/second_text/pallas_call | solution.py:242
  16.2 0.6 %collective-permute-start.2 = (bf16[4,64,768]{2,1,0:T(8,128)(2,1)S(1)}, bf16[4,64,768]{2,1,0:T(8,128)(2,1)S(1)}, u32[]{:S(2)}, u32[]{:S(2)}) collective-permute-start(bf16[4,64,768]{2,1,0:T(8,128)(2,1)S(1)} %get-tuple-element.36), channel_id=1, source_target_pairs={{0,1},{1,0},{2,3},{3,2},{4,5},{5,4},{6,7},{7,6},{8,9},{9,8},{10,11... | collective-permute-start | bytes 1179656 | tf_op jit(solution)/shard_map/ppermute | solution.py:226
  16.7 0.3 collective-permute-done.3.came_ref
  17.2 1.6 %collective-permute-start.10 = (bf16[64,768]{1,0:T(8,128)(2,1)S(1)}, bf16[64,768]{1,0:T(8,128)(2,1)S(1)}, u32[]{:S(2)}, u32[]{:S(2)}) collective-permute-start(bf16[64,768]{1,0:T(8,128)(2,1)S(1)} %get-tuple-element.43), channel_id=1, source_target_pairs={{0,2},{1,3},{2,0},{3,1},{4,6},{5,7},{6,4},{7,5},{8,10},{9,11},{10,... | collective-permute-start | bytes 294920 | tf_op jit(solution)/shard_map/ppermute | solution.py:226
  18.7 0.5 %collective-permute-start.8 = (bf16[64,768]{1,0:T(8,128)(2,1)S(1)}, bf16[64,768]{1,0:T(8,128)(2,1)S(1)}, u32[]{:S(2)}, u32[]{:S(2)}) collective-permute-start(bf16[64,768]{1,0:T(8,128)(2,1)S(1)} %get-tuple-element.42), channel_id=1, source_target_pairs={{0,2},{1,3},{2,0},{3,1},{4,6},{5,7},{6,4},{7,5},{8,10},{9,11},{10,... | collective-permute-start | bytes 294920 | tf_op jit(solution)/shard_map/ppermute | solution.py:226
  19.3 1.5 %collective-permute-start.6 = (bf16[64,768]{1,0:T(8,128)(2,1)S(1)}, bf16[64,768]{1,0:T(8,128)(2,1)S(1)}, u32[]{:S(2)}, u32[]{:S(2)}) collective-permute-start(bf16[64,768]{1,0:T(8,128)(2,1)S(1)} %get-tuple-element.41), channel_id=1, source_target_pairs={{0,2},{1,3},{2,0},{3,1},{4,6},{5,7},{6,4},{7,5},{8,10},{9,11},{10,... | collective-permute-start | bytes 294920 | tf_op jit(solution)/shard_map/ppermute | solution.py:226
  20.8 0.5 %collective-permute-start.4 = (bf16[64,768]{1,0:T(8,128)(2,1)S(1)}, bf16[64,768]{1,0:T(8,128)(2,1)S(1)}, u32[]{:S(2)}, u32[]{:S(2)}) collective-permute-start(bf16[64,768]{1,0:T(8,128)(2,1)S(1)} %get-tuple-element.39), channel_id=1, source_target_pairs={{0,2},{1,3},{2,0},{3,1},{4,6},{5,7},{6,4},{7,5},{8,10},{9,11},{10,... | collective-permute-start | bytes 294920 | tf_op jit(solution)/shard_map/ppermute | solution.py:226
  21.3 1.6 %collective-permute-done.10.crossed_ref = bf16[64,768]{1,0:T(8,128)(2,1)S(1)} collective-permute-done((bf16[64,768]{1,0:T(8,128)(2,1)S(1)}, bf16[64,768]{1,0:T(8,128)(2,1)S(1)}, u32[]{:S(2)}, u32[]{:S(2)}) %collective-permute-start.10) | collective-permute-done | bytes 98336 | tf_op jit(solution)/shard_map/ppermute | solution.py:226
  22.9 1.0 %collective-permute-start.11 = (bf16[25,16,128]{2,1,0:T(8,128)(2,1)S(1)}, bf16[25,16,128]{2,1,0:T(8,128)(2,1)S(1)}, u32[]{:S(2)}, u32[]{:S(2)}) collective-permute-start(bf16[25,16,128]{2,1,0:T(8,128)(2,1)S(1)} %cross.7), channel_id=1, source_target_pairs={{0,16},{1,21},{2,18},{3,23},{4,20},{5,17},{6,22},{7,19},{8,24},{9,... | collective-permute-start | bytes 307208 | tf_op jit(solution)/shard_map/ppermute | solution.py:237
  23.9 1.0 %collective-permute-done.8.crossed_ref = bf16[64,768]{1,0:T(8,128)(2,1)S(1)} collective-permute-done((bf16[64,768]{1,0:T(8,128)(2,1)S(1)}, bf16[64,768]{1,0:T(8,128)(2,1)S(1)}, u32[]{:S(2)}, u32[]{:S(2)}) %collective-permute-start.8) | collective-permute-done | bytes 98336 | tf_op jit(solution)/shard_map/ppermute | solution.py:226
  25.0 3.8 %collective-permute-start.9 = (bf16[25,16,128]{2,1,0:T(8,128)(2,1)S(1)}, bf16[25,16,128]{2,1,0:T(8,128)(2,1)S(1)}, u32[]{:S(2)}, u32[]{:S(2)}) collective-permute-start(bf16[25,16,128]{2,1,0:T(8,128)(2,1)S(1)} %cross.6), channel_id=1, source_target_pairs={{0,24},{1,29},{2,26},{3,31},{4,28},{5,25},{6,30},{7,27},{8,16},{9,... | collective-permute-start | bytes 307208 | tf_op jit(solution)/shard_map/ppermute | solution.py:237
  29.1 0.7 %collective-permute-start.5 = (bf16[25,16,128]{2,1,0:T(8,128)(2,1)S(1)}, bf16[25,16,128]{2,1,0:T(8,128)(2,1)S(1)}, u32[]{:S(2)}, u32[]{:S(2)}) collective-permute-start(bf16[25,16,128]{2,1,0:T(8,128)(2,1)S(1)} %cross.4.refs_4_), channel_id=1, source_target_pairs={{1,5},{3,7},{5,1},{7,3},{9,13},{11,15},{13,9},{15,11},{17,21},{19,... | collective-permute-start | bytes 307208 | tf_op jit(solution)/shard_map/ppermute | solution.py:237
  29.7 1.7 %collective-permute-done.11.refs_3_ = bf16[25,16,128]{2,1,0:T(8,128)(2,1)S(1)} collective-permute-done((bf16[25,16,128]{2,1,0:T(8,128)(2,1)S(1)}, bf16[25,16,128]{2,1,0:T(8,128)(2,1)S(1)}, u32[]{:S(2)}, u32[]{:S(2)}) %collective-permute-start.11) | collective-permute-done | bytes 102432 | tf_op jit(solution)/shard_map/ppermute | solution.py:237
  31.4 1.3 %collective-permute-done.9.refs_2_ = bf16[25,16,128]{2,1,0:T(8,128)(2,1)S(1)} collective-permute-done((bf16[25,16,128]{2,1,0:T(8,128)(2,1)S(1)}, bf16[25,16,128]{2,1,0:T(8,128)(2,1)S(1)}, u32[]{:S(2)}, u32[]{:S(2)}) %collective-permute-start.9) | collective-permute-done | bytes 102432 | tf_op jit(solution)/shard_map/ppermute | solution.py:237
  32.6 1.4 %collective-permute-done.7.refs_1_ = bf16[25,16,128]{2,1,0:T(8,128)(2,1)S(1)} collective-permute-done((bf16[25,16,128]{2,1,0:T(8,128)(2,1)S(1)}, bf16[25,16,128]{2,1,0:T(8,128)(2,1)S(1)}, u32[]{:S(2)}, u32[]{:S(2)}) %collective-permute-start.7) | collective-permute-done | bytes 102432 | tf_op jit(solution)/shard_map/ppermute | solution.py:237
  34.1 0.2 captions.1
  34.3 0.1 collective-permute-start.12
  34.4 1.2 %collective-permute-done.12.came_ref = bf16[2,64,384]{2,1,0:T(8,128)(2,1)S(1)} collective-permute-done((bf16[2,64,384]{2,1,0:T(8,128)(2,1)S(1)}, bf16[2,64,384]{2,1,0:T(8,128)(2,1)S(1)}, u32[]{:S(2)}, u32[]{:S(2)}) %collective-permute-start.12) | collective-permute-done | bytes 98336 | tf_op jit(solution)/shard_map/ppermute | solution.py:226
  35.6 0.7 %final.1 = bf16[2,64,384]{2,1,0:T(8,128)(2,1)} custom-call(f32[2,64,384]{2,1,0:T(8,128)S(1)} %get-tuple-element.44.kept_ref, bf16[2,64,384]{2,1,0:T(8,128)(2,1)S(1)} %collective-permute-done.12.came_ref), custom_call_target="tpu_custom_call" | custom-call | bytes 3600000 | tf_op jit(solution)/shard_map/final/pallas_call | solution.py:242
  (13 shorter events, 0.5 us)
Async XLA Ops:
  1.9 11.0 %collective-permute-start = (bf16[2,128,384]{2,1,0:T(8,128)(2,1)S(1)}, bf16[2,128,384]{2,1,0:T(8,128)(2,1)S(1)}, u32[]{:S(2)}, u32[]{:S(2)}) collective-permute-start(bf16[2,128,384]{2,1,0:T(8,128)(2,1)S(1)} %get-tuple-element.29), channel_id=1, source_target_pairs={{0,4},{4,0},{8,12},{12,8},{16,20},{20,16},{24,28},{28,24},{1,5},{5... | collective-permute-start | bytes 589832 | tf_op jit(solution)/shard_map/ppermute | solution.py:226
  4.9 8.0 %collective-permute-start.1 = (bf16[2,128,384]{2,1,0:T(8,128)(2,1)S(1)}, bf16[2,128,384]{2,1,0:T(8,128)(2,1)S(1)}, u32[]{:S(2)}, u32[]{:S(2)}) collective-permute-start(bf16[2,128,384]{2,1,0:T(8,128)(2,1)S(1)} %get-tuple-element.30), channel_id=1, source_target_pairs={{0,24},{4,12},{8,0},{12,20},{16,8},{20,28},{24,16},{28,4},{1,25},{... | collective-permute-start | bytes 589832 | tf_op jit(solution)/shard_map/ppermute | solution.py:295
  15.3 1.8 %collective-permute-start.3 = (bf16[4,64,768]{2,1,0:T(8,128)(2,1)S(1)}, bf16[4,64,768]{2,1,0:T(8,128)(2,1)S(1)}, u32[]{:S(2)}, u32[]{:S(2)}) collective-permute-start(bf16[4,64,768]{2,1,0:T(8,128)(2,1)S(1)} %get-tuple-element.38), channel_id=1, source_target_pairs={{0,1},{1,0},{2,3},{3,2},{4,5},{5,4},{6,7},{7,6},{8,9},{9,8},{10,11... | collective-permute-start | bytes 1179656 | tf_op jit(solution)/shard_map/ppermute | solution.py:226
  16.2 5.1 %collective-permute-start.2 = (bf16[4,64,768]{2,1,0:T(8,128)(2,1)S(1)}, bf16[4,64,768]{2,1,0:T(8,128)(2,1)S(1)}, u32[]{:S(2)}, u32[]{:S(2)}) collective-permute-start(bf16[4,64,768]{2,1,0:T(8,128)(2,1)S(1)} %get-tuple-element.36), channel_id=1, source_target_pairs={{0,1},{1,0},{2,3},{3,2},{4,5},{5,4},{6,7},{7,6},{8,9},{9,8},{10,11... | collective-permute-start | bytes 1179656 | tf_op jit(solution)/shard_map/ppermute | solution.py:226
  17.2 5.7 %collective-permute-start.10 = (bf16[64,768]{1,0:T(8,128)(2,1)S(1)}, bf16[64,768]{1,0:T(8,128)(2,1)S(1)}, u32[]{:S(2)}, u32[]{:S(2)}) collective-permute-start(bf16[64,768]{1,0:T(8,128)(2,1)S(1)} %get-tuple-element.43), channel_id=1, source_target_pairs={{0,2},{1,3},{2,0},{3,1},{4,6},{5,7},{6,4},{7,5},{8,10},{9,11},{10,... | collective-permute-start | bytes 294920 | tf_op jit(solution)/shard_map/ppermute | solution.py:226
  18.7 6.2 %collective-permute-start.8 = (bf16[64,768]{1,0:T(8,128)(2,1)S(1)}, bf16[64,768]{1,0:T(8,128)(2,1)S(1)}, u32[]{:S(2)}, u32[]{:S(2)}) collective-permute-start(bf16[64,768]{1,0:T(8,128)(2,1)S(1)} %get-tuple-element.42), channel_id=1, source_target_pairs={{0,2},{1,3},{2,0},{3,1},{4,6},{5,7},{6,4},{7,5},{8,10},{9,11},{10,... | collective-permute-start | bytes 294920 | tf_op jit(solution)/shard_map/ppermute | solution.py:226
  19.3 9.6 %collective-permute-start.6 = (bf16[64,768]{1,0:T(8,128)(2,1)S(1)}, bf16[64,768]{1,0:T(8,128)(2,1)S(1)}, u32[]{:S(2)}, u32[]{:S(2)}) collective-permute-start(bf16[64,768]{1,0:T(8,128)(2,1)S(1)} %get-tuple-element.41), channel_id=1, source_target_pairs={{0,2},{1,3},{2,0},{3,1},{4,6},{5,7},{6,4},{7,5},{8,10},{9,11},{10,... | collective-permute-start | bytes 294920 | tf_op jit(solution)/shard_map/ppermute | solution.py:226
  20.8 8.2 %collective-permute-start.4 = (bf16[64,768]{1,0:T(8,128)(2,1)S(1)}, bf16[64,768]{1,0:T(8,128)(2,1)S(1)}, u32[]{:S(2)}, u32[]{:S(2)}) collective-permute-start(bf16[64,768]{1,0:T(8,128)(2,1)S(1)} %get-tuple-element.39), channel_id=1, source_target_pairs={{0,2},{1,3},{2,0},{3,1},{4,6},{5,7},{6,4},{7,5},{8,10},{9,11},{10,... | collective-permute-start | bytes 294920 | tf_op jit(solution)/shard_map/ppermute | solution.py:226
  22.9 8.5 %collective-permute-start.11 = (bf16[25,16,128]{2,1,0:T(8,128)(2,1)S(1)}, bf16[25,16,128]{2,1,0:T(8,128)(2,1)S(1)}, u32[]{:S(2)}, u32[]{:S(2)}) collective-permute-start(bf16[25,16,128]{2,1,0:T(8,128)(2,1)S(1)} %cross.7), channel_id=1, source_target_pairs={{0,16},{1,21},{2,18},{3,23},{4,20},{5,17},{6,22},{7,19},{8,24},{9,... | collective-permute-start | bytes 307208 | tf_op jit(solution)/shard_map/ppermute | solution.py:237
  25.0 7.6 %collective-permute-start.9 = (bf16[25,16,128]{2,1,0:T(8,128)(2,1)S(1)}, bf16[25,16,128]{2,1,0:T(8,128)(2,1)S(1)}, u32[]{:S(2)}, u32[]{:S(2)}) collective-permute-start(bf16[25,16,128]{2,1,0:T(8,128)(2,1)S(1)} %cross.6), channel_id=1, source_target_pairs={{0,24},{1,29},{2,26},{3,31},{4,28},{5,25},{6,30},{7,27},{8,16},{9,... | collective-permute-start | bytes 307208 | tf_op jit(solution)/shard_map/ppermute | solution.py:237
  28.9 5.2 %collective-permute-start.7 = (bf16[25,16,128]{2,1,0:T(8,128)(2,1)S(1)}, bf16[25,16,128]{2,1,0:T(8,128)(2,1)S(1)}, u32[]{:S(2)}, u32[]{:S(2)}) collective-permute-start(bf16[25,16,128]{2,1,0:T(8,128)(2,1)S(1)} %cross.5), channel_id=1, source_target_pairs={{0,8},{1,13},{2,10},{3,15},{4,12},{5,9},{6,14},{7,11},{8,0},{9,5},... | collective-permute-start | bytes 307208 | tf_op jit(solution)/shard_map/ppermute | solution.py:237
  29.1 5.0 %collective-permute-start.5 = (bf16[25,16,128]{2,1,0:T(8,128)(2,1)S(1)}, bf16[25,16,128]{2,1,0:T(8,128)(2,1)S(1)}, u32[]{:S(2)}, u32[]{:S(2)}) collective-permute-start(bf16[25,16,128]{2,1,0:T(8,128)(2,1)S(1)} %cross.4.refs_4_), channel_id=1, source_target_pairs={{1,5},{3,7},{5,1},{7,3},{9,13},{11,15},{13,9},{15,11},{17,21},{19,... | collective-permute-start | bytes 307208 | tf_op jit(solution)/shard_map/ppermute | solution.py:237
  34.3 1.4 %collective-permute-start.12 = (bf16[2,64,384]{2,1,0:T(8,128)(2,1)S(1)}, bf16[2,64,384]{2,1,0:T(8,128)(2,1)S(1)}, u32[]{:S(2)}, u32[]{:S(2)}) collective-permute-start(bf16[2,64,384]{2,1,0:T(8,128)(2,1)S(1)} %get-tuple-element.45), channel_id=1, source_target_pairs={{0,1},{1,0},{2,3},{3,2},{4,5},{5,4},{6,7},{7,6},{8,9},{9,8},{10,11... | collective-permute-start | bytes 294920 | tf_op jit(solution)/shard_map/ppermute | solution.py:226

commit v6 on v5

--- a/solution.py
+++ b/solution.py
@@ -23,7 +23,7 @@
     return lax.dot_general(a, b, ((contract[:1], contract[1:]), ((), ())), preferred_element_type=F32)
 
 
-def shipping(mask_ref, caps_ref, me, seq_count, tiles):
+def shipping(mask_ref, me, seq_count, tiles):
     odd = jnp.bitwise_and(me, 1)
     ones = mask_ref[1, 0]
     for t in range(1, tiles):
@@ -55,7 +55,7 @@
     return copies
 
 
-def stage_kernel(seq_count, tiles, mask_hbm, caps_hbm, q_hbm, g_hbm, cache_hbm, *refs):
+def stage_kernel(seq_count, captions, tiles, mask_hbm, caps_hbm, q_hbm, g_hbm, cache_hbm, *refs):
     y_ref, z_ref, q_ref, g_ref, cache_ref, flags_ref, caption_ref, mask_ref, caps_ref, sems = refs
     me = lax.axis_index("seq")
     copies = fetch(
@@ -70,7 +70,7 @@
     )
     for c in copies[:4]:
         c.wait()
-    mine, *picked = shipping(mask_ref, caps_ref, me, seq_count, tiles)
+    mine, *picked = shipping(mask_ref, me, seq_count, tiles)
     for tile, out in zip(picked, (y_ref, z_ref), strict=True):
         keep = (mask_ref[mine, tile] == 0).astype(F32).astype(BF16)
         at = pl.ds(pl.multiple_of(tile * TILE, TILE), TILE)
@@ -81,6 +81,12 @@
         flags_ref[t : t + 1, :] = jnp.full(lanes, mask_ref[1, t].astype(F32), F32)
         flags_ref[tiles + t : tiles + t + 1, :] = jnp.full(lanes, mask_ref[mine, t].astype(F32), F32)
     flags_ref[2 * tiles : 2 * tiles + 1, :] = jnp.full(lanes, mine.astype(F32), F32)
+    along = lax.rem(me + jnp.where(jnp.bitwise_and(me, 1) == 0, 2, seq_count - 2), seq_count)
+    expects = jnp.int32(0)
+    for d in (jnp.bitwise_xor(me, 1), along):
+        expects += jnp.where(jnp.logical_and(caps_ref[0, d] < captions, caps_ref[1, d] < captions), 1, 0)
+    last = flags_ref.shape[0] - 1
+    flags_ref[last : last + 1, :] = jnp.full(lanes, expects.astype(F32), F32)
     caption_ref[...] = jnp.full(caption_ref.shape, caps_ref[mine, me].astype(F32), F32).astype(BF16)
     copies[4].wait()
 
@@ -133,22 +139,25 @@
         copy.wait()
 
 
-def gather_parts(heads, blocks, y_ref, z_ref, main_ref, part_ref, both_ref):
+def gather_parts(heads, blocks, main_ref, part_ref, both_ref, received=None):
     me, core = lax.axis_index("seq"), jnp.bitwise_and(lax.axis_index("head"), 1)
     block_rows, width = L // blocks, heads * DH
     places = []
     for s in range(blocks):
         rel = jnp.bitwise_xor(jnp.bitwise_xor(me, s), core)
         pair, quarter = jnp.right_shift(rel, 1), blocks // 4
-        place = jnp.where(pair >= quarter, pair - quarter, 2 * quarter - 1 - pair)
+        place = jnp.where(pair >= quarter, 2 * (pair - quarter), 2 * (quarter - 1 - pair) + 1)
         place += jnp.bitwise_and(rel, 1) * (blocks // 2)
         places.append(pl.ds(pl.multiple_of(place * block_rows, block_rows), block_rows))
     for h in range(heads):
         cols = slice(h * DH, (h + 1) * DH)
-        query, grad = y_ref[0, :, cols] + z_ref[0, :, cols], y_ref[1, :, cols] + z_ref[1, :, cols]
-        attention_lo, score_lo = backward(main_ref[0, :, cols], main_ref[1, :, cols], query, grad)
-        dk = ((part_ref[0, :, cols] + dot(score_lo, query, (1, 0))) * INV_ROOT).astype(BF16)
-        dv = (part_ref[1, :, cols] + dot(attention_lo, grad, (1, 0))).astype(BF16)
+        dk, dv = part_ref[0, :, cols], part_ref[1, :, cols]
+        if received is not None:
+            y_ref, z_ref = received
+            query, grad = y_ref[0, :, cols] + z_ref[0, :, cols], y_ref[1, :, cols] + z_ref[1, :, cols]
+            attention_lo, score_lo = backward(main_ref[0, :, cols], main_ref[1, :, cols], query, grad)
+            dk, dv = dk + dot(score_lo, query, (1, 0)), dv + dot(attention_lo, grad, (1, 0))
+        dk, dv = (dk * INV_ROOT).astype(BF16), dv.astype(BF16)
         for s, rows in enumerate(places):
             both_ref[rows, h * DH : (h + 1) * DH] = dk[s * block_rows : (s + 1) * block_rows]
             both_ref[rows, width + h * DH : width + (h + 1) * DH] = dv[s * block_rows : (s + 1) * block_rows]
@@ -164,9 +173,32 @@
     sent_ref[...] = text[half:].reshape(sent_ref.shape)
 
 
-def first_text_kernel(heads, blocks, y_ref, z_ref, main_ref, part_ref, weight_ref, both_ref, kept_ref, sent_ref):
-    gather_parts(heads, blocks, y_ref, z_ref, main_ref, part_ref, both_ref)
-    project(both_ref, weight_ref, 1, kept_ref, sent_ref)
+def expects(flags_ref):
+    last = flags_ref.shape[0] - 1
+    return jnp.max(flags_ref[last : last + 1, :]) > 0.0
+
+
+def early_text_kernel(heads, blocks, flags_ref, part_ref, weight_ref, both_ref, kept_ref, sent_ref):
+    @pl.when(jnp.logical_not(expects(flags_ref)))
+    def _():
+        gather_parts(heads, blocks, None, part_ref, both_ref)
+        project(both_ref, weight_ref, 1, kept_ref, sent_ref)
+
+
+def first_text_kernel(heads, blocks, flags_ref, z_ref, y_ref, main_ref, part_ref, weight_ref, *refs):
+    early, outs = refs[:3], refs[3:]
+    come = expects(flags_ref)
+
+    @pl.when(come)
+    def _():
+        both_ref, kept_ref, sent_ref = outs
+        gather_parts(heads, blocks, main_ref, part_ref, both_ref, (y_ref, z_ref))
+        project(both_ref, weight_ref, 1, kept_ref, sent_ref)
+
+    @pl.when(jnp.logical_not(come))
+    def _():
+        for a, b in zip(early, outs, strict=True):
+            b[...] = a[...]
 
 
 def second_text_kernel(both_ref, weight_ref, kept_ref, sent_ref):
@@ -271,7 +303,7 @@
         return jax.ShapeDtypeStruct(shape, dtype)
 
     to_y, to_z, q_here, g_here, cache_first, flags, caption = call(
-        functools.partial(stage_kernel, seq_count, tiles),
+        functools.partial(stage_kernel, seq_count, captions, tiles),
         "stage",
         (
             like(2, TILE, width),
@@ -279,7 +311,7 @@
             like(rows_here, width),
             like(rows_here, width),
             like(2, slots, L, DH),
-            like(8 * (-(-(2 * tiles + 1) // 8)), 128, dtype=F32),
+            like(8 * (-(-(2 * tiles + 2) // 8)), 128, dtype=F32),
             like(16, 128),
         ),
         held_back[:5],
@@ -316,12 +348,22 @@
         out_specs=(hbm, vmem, vmem, vmem),
     )
     half = like(seq_count // 2, block_rows, 2 * width)
+    texts = (like(L, 2 * width), half, half)
+    early = call(
+        functools.partial(early_text_kernel, heads, seq_count),
+        "early_text",
+        texts,
+        (flags, part, weight),
+        [vmem] * 3,
+        limit=KERNEL_LIMIT,
+        hint_us=1.0,
+    )
     both, kept, sent = call(
         functools.partial(first_text_kernel, heads, seq_count),
         "first_text",
-        (like(L, 2 * width), half, half),
-        (from_y, from_z, main, part, weight),
-        [vmem] * 5,
+        texts,
+        (flags, from_z, from_y, main, part, weight, *early),
+        [vmem] * 9,
         limit=KERNEL_LIMIT,
         hint_us=2.0,
     )
@@ -338,7 +380,7 @@
     far = call(pair_kernel, "pair", (block,) * (seq_count // 2), (kept, swap(sent, "head", 1)), [vmem] * 2)
     came_own = swap(sent_own, "head", 1)
     quarter = seq_count // 4
-    bases = [2 * (quarter + i) for i in range(quarter)] + [2 * (quarter - 1 - i) for i in range(quarter)]
+    bases = [2 * b for i in range(quarter) for b in (quarter + i, quarter - 1 - i)]
     arrived, own = [], None
     for i, base in enumerate(bases):
         mine = call(

time: 36.5 us -> 34.8 us (0.953)
  starting transfers between devices: 17.1 us -> 15.6 us
  Pallas kernels: 9.93 us -> 8.88 us
  waiting for transfers between devices: 8.56 us -> 9.37 us
    ppermute x8, starting transfers between devices: 7.9 us -> 4.81 us  [swap(): return lax.ppermute(array, axis, [(i, i ^ bit) for i in range(n)])]
    ppermute x1, starting transfers between devices: 3.6 us -> 5.1 us  [shards_pairs(): lax.ppermute(to_z, 'seq', [(s, (s + (2 if s & 1 else -2)) % seq_count) fo...]
    ppermute x8, waiting for transfers between devices: 4.21 us -> 5.36 us  [swap(): return lax.ppermute(array, axis, [(i, i ^ bit) for i in range(n)])]
    pallas_call x11 -> x12, Pallas kernels: 9.93 us -> 8.88 us  [call(): pl.pallas_call(kernel, out_shape=out_shape, in_specs=specs, out_specs=out...]
  transfers between devices with their start and end apart: 13 -> 13, of which waited for: 7 -> 8; matrix products, arithmetic and copies ran while one was open for 0% -> 0% of each run, Pallas kernels for 15% -> 19%
where the time goes in v6:
time: 34.8 us; the launch traced here: 34.6 us
  starting transfers between devices  15.6 us (45%)
  waiting for transfers between devices  9.37 us (27%)
  Pallas kernels  8.88 us (26%)
  between operations  0.74 us (2%)
    pallas_call x12, Pallas kernels, call(): pl.pallas_call(kernel, out_shape=out_shape, in_specs=specs, out_specs=out...  8.88 us
    ppermute x4, starting transfers between devices, send(): return lax.ppermute(block, ('seq', 'head'), pairs)  5.68 us
    ppermute x8, waiting for transfers between devices, swap(): return lax.ppermute(array, axis, [(i, i ^ bit) for i in range(n)])  5.36 us
    ppermute x1, starting transfers between devices, shards_pairs(): lax.ppermute(to_z, 'seq', [(s, (s + (2 if s & 1 else -2)) % seq_count) fo...  5.1 us
    ppermute x8, starting transfers between devices, swap(): return lax.ppermute(array, axis, [(i, i ^ bit) for i in range(n)])  4.81 us
    ppermute x4, waiting for transfers between devices, send(): return lax.ppermute(block, ('seq', 'head'), pairs)  4.01 us
  transfers between devices with their start and end apart: 13, of which 8 were waited for; matrix products, arithmetic and copies ran while one was open for 0% of the time, Pallas kernels for 19%

profile of v6, /device:TPU:0, one launch (start us, length us, event | category | flops | bytes accessed | tf_op | source)
XLA Modules:
  0.0 34.6 jit_solution(2572869261751471255)
XLA Ops:
  0.6 1.3 %stage.1 = (bf16[2,128,384]{2,1,0:T(8,128)(2,1)S(1)}, bf16[2,128,384]{2,1,0:T(8,128)(2,1)S(1)}, bf16[384,384]{1,0:T(8,128)(2,1)S(1)}, bf16[384,384]{1,0:T(8,128)...) custom-call(s32[2,3]{1,0:T(2,128)} %bitcast.2, ...), custom_call_target="tpu_custom_call" | custom-call | bytes 3600000 | tf_op jit(solution)/shard_map/stage/pallas_call | solution.py:274
  1.9 5.1 %collective-permute-start = (bf16[2,128,384]{2,1,0:T(8,128)(2,1)S(1)}, bf16[2,128,384]{2,1,0:T(8,128)(2,1)S(1)}, u32[]{:S(2)}, u32[]{:S(2)}) collective-permute-start(bf16[2,128,384]{2,1,0:T(8,128)(2,1)S(1)} %get-tuple-element.32), channel_id=1, source_target_pairs={{0,24},{4,12},{8,0},{12,20},{16,8},{20,28},{24,16},{28,4},{1,25},{... | collective-permute-start | bytes 589832 | tf_op jit(solution)/shard_map/ppermute | solution.py:327
  7.0 4.4 %own_tiles.1 = (bf16[384,384]{1,0:T(8,128)(2,1)}, f32[2,512,384]{2,1,0:T(8,128)S(1)}, bf16[2,512,384]{2,1,0:T(8,128)(2,1)S(1)}, bf16[1536,768]{1,0:T(8,128)(2,1)S(1)}) custom-call(f32[8,128]{1,0:T(8,128)S(1)} %get-tuple-element.27.flags_ref, bf16[384,384]{1,0:T(8,128)(2,1)S(1)} %get-tuple-element.28.q_ref, bf16[384,384]{1,0:T(8,128)(2,1)S(1)} %get-tuple-element.29.g_ref, ...), custom_call_target="tpu_custom_call" | custom-call | bytes 18000000 | tf_op jit(solution)/shard_map/own_tiles/pallas_call | solution.py:274
  11.4 1.0 %early_text.1 = (bf16[512,768]{1,0:T(8,128)(2,1)S(1)}, bf16[4,64,768]{2,1,0:T(8,128)(2,1)S(1)}, bf16[4,64,768]{2,1,0:T(8,128)(2,1)S(1)}) custom-call(f32[8,128]{1,0:T(8,128)S(1)} %get-tuple-element.27.flags_ref, f32[2,512,384]{2,1,0:T(8,128)S(1)} %get-tuple-element.35.part_ref, bf16[1536,768]{1,0:T(8,128)(2,1)S(1)} %get-tuple-element.36.weight_ref), custom_call_target="tpu_custom_call" | custom-call | bytes 3600000 | tf_op jit(solution)/shard_map/early_text/pallas_call | solution.py:274
  12.5 0.9 %collective-permute-done.1.y_ref = bf16[2,128,384]{2,1,0:T(8,128)(2,1)S(1)} collective-permute-done((bf16[2,128,384]{2,1,0:T(8,128)(2,1)S(1)}, bf16[2,128,384]{2,1,0:T(8,128)(2,1)S(1)}, u32[]{:S(2)}, u32[]{:S(2)}) %collective-permute-start.1) | collective-permute-done | bytes 196640 | tf_op jit(solution)/shard_map/ppermute | solution.py:258
  13.4 0.2 first_text.1
  13.7 0.8 %second_text.1 = (bf16[4,64,768]{2,1,0:T(8,128)(2,1)S(1)}, bf16[4,64,768]{2,1,0:T(8,128)(2,1)S(1)}) custom-call(bf16[512,768]{1,0:T(8,128)(2,1)S(1)} %get-tuple-element.40.both_ref, bf16[1536,768]{1,0:T(8,128)(2,1)S(1)} %get-tuple-element.36.weight_ref), custom_call_target="tpu_custom_call" | custom-call | bytes 3600000 | tf_op jit(solution)/shard_map/second_text/pallas_call | solution.py:274
  14.5 0.6 %collective-permute-start.2 = (bf16[4,64,768]{2,1,0:T(8,128)(2,1)S(1)}, bf16[4,64,768]{2,1,0:T(8,128)(2,1)S(1)}, u32[]{:S(2)}, u32[]{:S(2)}) collective-permute-start(bf16[4,64,768]{2,1,0:T(8,128)(2,1)S(1)} %get-tuple-element.42), channel_id=1, source_target_pairs={{0,1},{1,0},{2,3},{3,2},{4,5},{5,4},{6,7},{7,6},{8,9},{9,8},{10,11... | collective-permute-start | bytes 1179656 | tf_op jit(solution)/shard_map/ppermute | solution.py:258
  15.1 0.3 collective-permute-done.3.came_ref
  15.5 1.6 %collective-permute-start.10 = (bf16[64,768]{1,0:T(8,128)(2,1)S(1)}, bf16[64,768]{1,0:T(8,128)(2,1)S(1)}, u32[]{:S(2)}, u32[]{:S(2)}) collective-permute-start(bf16[64,768]{1,0:T(8,128)(2,1)S(1)} %get-tuple-element.49), channel_id=1, source_target_pairs={{0,2},{1,3},{2,0},{3,1},{4,6},{5,7},{6,4},{7,5},{8,10},{9,11},{10,... | collective-permute-start | bytes 294920 | tf_op jit(solution)/shard_map/ppermute | solution.py:258
  17.1 0.5 %collective-permute-start.8 = (bf16[64,768]{1,0:T(8,128)(2,1)S(1)}, bf16[64,768]{1,0:T(8,128)(2,1)S(1)}, u32[]{:S(2)}, u32[]{:S(2)}) collective-permute-start(bf16[64,768]{1,0:T(8,128)(2,1)S(1)} %get-tuple-element.48), channel_id=1, source_target_pairs={{0,2},{1,3},{2,0},{3,1},{4,6},{5,7},{6,4},{7,5},{8,10},{9,11},{10,... | collective-permute-start | bytes 294920 | tf_op jit(solution)/shard_map/ppermute | solution.py:258
  17.6 1.5 %collective-permute-start.6 = (bf16[64,768]{1,0:T(8,128)(2,1)S(1)}, bf16[64,768]{1,0:T(8,128)(2,1)S(1)}, u32[]{:S(2)}, u32[]{:S(2)}) collective-permute-start(bf16[64,768]{1,0:T(8,128)(2,1)S(1)} %get-tuple-element.47), channel_id=1, source_target_pairs={{0,2},{1,3},{2,0},{3,1},{4,6},{5,7},{6,4},{7,5},{8,10},{9,11},{10,... | collective-permute-start | bytes 294920 | tf_op jit(solution)/shard_map/ppermute | solution.py:258
  19.1 0.5 %collective-permute-start.4 = (bf16[64,768]{1,0:T(8,128)(2,1)S(1)}, bf16[64,768]{1,0:T(8,128)(2,1)S(1)}, u32[]{:S(2)}, u32[]{:S(2)}) collective-permute-start(bf16[64,768]{1,0:T(8,128)(2,1)S(1)} %get-tuple-element.45), channel_id=1, source_target_pairs={{0,2},{1,3},{2,0},{3,1},{4,6},{5,7},{6,4},{7,5},{8,10},{9,11},{10,... | collective-permute-start | bytes 294920 | tf_op jit(solution)/shard_map/ppermute | solution.py:258
  19.6 1.6 %collective-permute-done.10.crossed_ref = bf16[64,768]{1,0:T(8,128)(2,1)S(1)} collective-permute-done((bf16[64,768]{1,0:T(8,128)(2,1)S(1)}, bf16[64,768]{1,0:T(8,128)(2,1)S(1)}, u32[]{:S(2)}, u32[]{:S(2)}) %collective-permute-start.10) | collective-permute-done | bytes 98336 | tf_op jit(solution)/shard_map/ppermute | solution.py:258
  21.2 1.2 %collective-permute-start.11 = (bf16[25,16,128]{2,1,0:T(8,128)(2,1)S(1)}, bf16[25,16,128]{2,1,0:T(8,128)(2,1)S(1)}, u32[]{:S(2)}, u32[]{:S(2)}) collective-permute-start(bf16[25,16,128]{2,1,0:T(8,128)(2,1)S(1)} %cross.7), channel_id=1, source_target_pairs={{0,16},{1,21},{2,18},{3,23},{4,20},{5,17},{6,22},{7,19},{8,24},{9,... | collective-permute-start | bytes 307208 | tf_op jit(solution)/shard_map/ppermute | solution.py:269
  22.5 0.8 %collective-permute-done.8.crossed_ref = bf16[64,768]{1,0:T(8,128)(2,1)S(1)} collective-permute-done((bf16[64,768]{1,0:T(8,128)(2,1)S(1)}, bf16[64,768]{1,0:T(8,128)(2,1)S(1)}, u32[]{:S(2)}, u32[]{:S(2)}) %collective-permute-start.8) | collective-permute-done | bytes 98336 | tf_op jit(solution)/shard_map/ppermute | solution.py:258
  23.4 1.6 %collective-permute-start.9 = (bf16[25,16,128]{2,1,0:T(8,128)(2,1)S(1)}, bf16[25,16,128]{2,1,0:T(8,128)(2,1)S(1)}, u32[]{:S(2)}, u32[]{:S(2)}) collective-permute-start(bf16[25,16,128]{2,1,0:T(8,128)(2,1)S(1)} %cross.6), channel_id=1, source_target_pairs={{0,8},{1,13},{2,10},{3,15},{4,12},{5,9},{6,14},{7,11},{8,0},{9,5},... | collective-permute-start | bytes 307208 | tf_op jit(solution)/shard_map/ppermute | solution.py:269
  25.0 0.4 %collective-permute-done.6.crossed_ref = bf16[64,768]{1,0:T(8,128)(2,1)S(1)} collective-permute-done((bf16[64,768]{1,0:T(8,128)(2,1)S(1)}, bf16[64,768]{1,0:T(8,128)(2,1)S(1)}, u32[]{:S(2)}, u32[]{:S(2)}) %collective-permute-start.6) | collective-permute-done | bytes 98336 | tf_op jit(solution)/shard_map/ppermute | solution.py:258
  25.5 2.1 %collective-permute-start.7 = (bf16[25,16,128]{2,1,0:T(8,128)(2,1)S(1)}, bf16[25,16,128]{2,1,0:T(8,128)(2,1)S(1)}, u32[]{:S(2)}, u32[]{:S(2)}) collective-permute-start(bf16[25,16,128]{2,1,0:T(8,128)(2,1)S(1)} %cross.5), channel_id=1, source_target_pairs={{0,24},{1,29},{2,26},{3,31},{4,28},{5,25},{6,30},{7,27},{8,16},{9,... | collective-permute-start | bytes 307208 | tf_op jit(solution)/shard_map/ppermute | solution.py:269
  27.7 0.7 %collective-permute-start.5 = (bf16[25,16,128]{2,1,0:T(8,128)(2,1)S(1)}, bf16[25,16,128]{2,1,0:T(8,128)(2,1)S(1)}, u32[]{:S(2)}, u32[]{:S(2)}) collective-permute-start(bf16[25,16,128]{2,1,0:T(8,128)(2,1)S(1)} %cross.4.refs_4_), channel_id=1, source_target_pairs={{1,5},{3,7},{5,1},{7,3},{9,13},{11,15},{13,9},{15,11},{17,21},{19,... | collective-permute-start | bytes 307208 | tf_op jit(solution)/shard_map/ppermute | solution.py:269
  28.4 0.4 %collective-permute-done.9.refs_2_ = bf16[25,16,128]{2,1,0:T(8,128)(2,1)S(1)} collective-permute-done((bf16[25,16,128]{2,1,0:T(8,128)(2,1)S(1)}, bf16[25,16,128]{2,1,0:T(8,128)(2,1)S(1)}, u32[]{:S(2)}, u32[]{:S(2)}) %collective-permute-start.9) | collective-permute-done | bytes 102432 | tf_op jit(solution)/shard_map/ppermute | solution.py:269
  28.7 3.6 %collective-permute-done.7.refs_1_ = bf16[25,16,128]{2,1,0:T(8,128)(2,1)S(1)} collective-permute-done((bf16[25,16,128]{2,1,0:T(8,128)(2,1)S(1)}, bf16[25,16,128]{2,1,0:T(8,128)(2,1)S(1)}, u32[]{:S(2)}, u32[]{:S(2)}) %collective-permute-start.7) | collective-permute-done | bytes 102432 | tf_op jit(solution)/shard_map/ppermute | solution.py:269
  32.6 1.3 %collective-permute-done.12.came_ref = bf16[2,64,384]{2,1,0:T(8,128)(2,1)S(1)} collective-permute-done((bf16[2,64,384]{2,1,0:T(8,128)(2,1)S(1)}, bf16[2,64,384]{2,1,0:T(8,128)(2,1)S(1)}, u32[]{:S(2)}, u32[]{:S(2)}) %collective-permute-start.12) | collective-permute-done | bytes 98336 | tf_op jit(solution)/shard_map/ppermute | solution.py:258
  33.9 0.7 %final.1 = bf16[2,64,384]{2,1,0:T(8,128)(2,1)} custom-call(f32[2,64,384]{2,1,0:T(8,128)S(1)} %get-tuple-element.50.kept_ref, bf16[2,64,384]{2,1,0:T(8,128)(2,1)S(1)} %collective-permute-done.12.came_ref), custom_call_target="tpu_custom_call" | custom-call | bytes 3600000 | tf_op jit(solution)/shard_map/final/pallas_call | solution.py:274
  (14 shorter events, 0.6 us)
Async XLA Ops:
  1.9 10.5 %collective-permute-start = (bf16[2,128,384]{2,1,0:T(8,128)(2,1)S(1)}, bf16[2,128,384]{2,1,0:T(8,128)(2,1)S(1)}, u32[]{:S(2)}, u32[]{:S(2)}) collective-permute-start(bf16[2,128,384]{2,1,0:T(8,128)(2,1)S(1)} %get-tuple-element.32), channel_id=1, source_target_pairs={{0,24},{4,12},{8,0},{12,20},{16,8},{20,28},{24,16},{28,4},{1,25},{... | collective-permute-start | bytes 589832 | tf_op jit(solution)/shard_map/ppermute | solution.py:327
  7.0 6.4 %collective-permute-start.1 = (bf16[2,128,384]{2,1,0:T(8,128)(2,1)S(1)}, bf16[2,128,384]{2,1,0:T(8,128)(2,1)S(1)}, u32[]{:S(2)}, u32[]{:S(2)}) collective-permute-start(bf16[2,128,384]{2,1,0:T(8,128)(2,1)S(1)} %get-tuple-element.33), channel_id=1, source_target_pairs={{0,4},{4,0},{8,12},{12,8},{16,20},{20,16},{24,28},{28,24},{1,5},{5... | collective-permute-start | bytes 589832 | tf_op jit(solution)/shard_map/ppermute | solution.py:258
  13.6 1.8 %collective-permute-start.3 = (bf16[4,64,768]{2,1,0:T(8,128)(2,1)S(1)}, bf16[4,64,768]{2,1,0:T(8,128)(2,1)S(1)}, u32[]{:S(2)}, u32[]{:S(2)}) collective-permute-start(bf16[4,64,768]{2,1,0:T(8,128)(2,1)S(1)} %get-tuple-element.44), channel_id=1, source_target_pairs={{0,1},{1,0},{2,3},{3,2},{4,5},{5,4},{6,7},{7,6},{8,9},{9,8},{10,11... | collective-permute-start | bytes 1179656 | tf_op jit(solution)/shard_map/ppermute | solution.py:258
  14.5 5.1 %collective-permute-start.2 = (bf16[4,64,768]{2,1,0:T(8,128)(2,1)S(1)}, bf16[4,64,768]{2,1,0:T(8,128)(2,1)S(1)}, u32[]{:S(2)}, u32[]{:S(2)}) collective-permute-start(bf16[4,64,768]{2,1,0:T(8,128)(2,1)S(1)} %get-tuple-element.42), channel_id=1, source_target_pairs={{0,1},{1,0},{2,3},{3,2},{4,5},{5,4},{6,7},{7,6},{8,9},{9,8},{10,11... | collective-permute-start | bytes 1179656 | tf_op jit(solution)/shard_map/ppermute | solution.py:258
  15.5 5.7 %collective-permute-start.10 = (bf16[64,768]{1,0:T(8,128)(2,1)S(1)}, bf16[64,768]{1,0:T(8,128)(2,1)S(1)}, u32[]{:S(2)}, u32[]{:S(2)}) collective-permute-start(bf16[64,768]{1,0:T(8,128)(2,1)S(1)} %get-tuple-element.49), channel_id=1, source_target_pairs={{0,2},{1,3},{2,0},{3,1},{4,6},{5,7},{6,4},{7,5},{8,10},{9,11},{10,... | collective-permute-start | bytes 294920 | tf_op jit(solution)/shard_map/ppermute | solution.py:258
  17.1 6.2 %collective-permute-start.8 = (bf16[64,768]{1,0:T(8,128)(2,1)S(1)}, bf16[64,768]{1,0:T(8,128)(2,1)S(1)}, u32[]{:S(2)}, u32[]{:S(2)}) collective-permute-start(bf16[64,768]{1,0:T(8,128)(2,1)S(1)} %get-tuple-element.48), channel_id=1, source_target_pairs={{0,2},{1,3},{2,0},{3,1},{4,6},{5,7},{6,4},{7,5},{8,10},{9,11},{10,... | collective-permute-start | bytes 294920 | tf_op jit(solution)/shard_map/ppermute | solution.py:258
  17.6 7.8 %collective-permute-start.6 = (bf16[64,768]{1,0:T(8,128)(2,1)S(1)}, bf16[64,768]{1,0:T(8,128)(2,1)S(1)}, u32[]{:S(2)}, u32[]{:S(2)}) collective-permute-start(bf16[64,768]{1,0:T(8,128)(2,1)S(1)} %get-tuple-element.47), channel_id=1, source_target_pairs={{0,2},{1,3},{2,0},{3,1},{4,6},{5,7},{6,4},{7,5},{8,10},{9,11},{10,... | collective-permute-start | bytes 294920 | tf_op jit(solution)/shard_map/ppermute | solution.py:258
  19.1 8.5 %collective-permute-start.4 = (bf16[64,768]{1,0:T(8,128)(2,1)S(1)}, bf16[64,768]{1,0:T(8,128)(2,1)S(1)}, u32[]{:S(2)}, u32[]{:S(2)}) collective-permute-start(bf16[64,768]{1,0:T(8,128)(2,1)S(1)} %get-tuple-element.45), channel_id=1, source_target_pairs={{0,2},{1,3},{2,0},{3,1},{4,6},{5,7},{6,4},{7,5},{8,10},{9,11},{10,... | collective-permute-start | bytes 294920 | tf_op jit(solution)/shard_map/ppermute | solution.py:258
  21.2 7.1 %collective-permute-start.11 = (bf16[25,16,128]{2,1,0:T(8,128)(2,1)S(1)}, bf16[25,16,128]{2,1,0:T(8,128)(2,1)S(1)}, u32[]{:S(2)}, u32[]{:S(2)}) collective-permute-start(bf16[25,16,128]{2,1,0:T(8,128)(2,1)S(1)} %cross.7), channel_id=1, source_target_pairs={{0,16},{1,21},{2,18},{3,23},{4,20},{5,17},{6,22},{7,19},{8,24},{9,... | collective-permute-start | bytes 307208 | tf_op jit(solution)/shard_map/ppermute | solution.py:269
  23.4 5.4 %collective-permute-start.9 = (bf16[25,16,128]{2,1,0:T(8,128)(2,1)S(1)}, bf16[25,16,128]{2,1,0:T(8,128)(2,1)S(1)}, u32[]{:S(2)}, u32[]{:S(2)}) collective-permute-start(bf16[25,16,128]{2,1,0:T(8,128)(2,1)S(1)} %cross.6), channel_id=1, source_target_pairs={{0,8},{1,13},{2,10},{3,15},{4,12},{5,9},{6,14},{7,11},{8,0},{9,5},... | collective-permute-start | bytes 307208 | tf_op jit(solution)/shard_map/ppermute | solution.py:269
  25.5 6.9 %collective-permute-start.7 = (bf16[25,16,128]{2,1,0:T(8,128)(2,1)S(1)}, bf16[25,16,128]{2,1,0:T(8,128)(2,1)S(1)}, u32[]{:S(2)}, u32[]{:S(2)}) collective-permute-start(bf16[25,16,128]{2,1,0:T(8,128)(2,1)S(1)} %cross.5), channel_id=1, source_target_pairs={{0,24},{1,29},{2,26},{3,31},{4,28},{5,25},{6,30},{7,27},{8,16},{9,... | collective-permute-start | bytes 307208 | tf_op jit(solution)/shard_map/ppermute | solution.py:269
  27.7 4.7 %collective-permute-start.5 = (bf16[25,16,128]{2,1,0:T(8,128)(2,1)S(1)}, bf16[25,16,128]{2,1,0:T(8,128)(2,1)S(1)}, u32[]{:S(2)}, u32[]{:S(2)}) collective-permute-start(bf16[25,16,128]{2,1,0:T(8,128)(2,1)S(1)} %cross.4.refs_4_), channel_id=1, source_target_pairs={{1,5},{3,7},{5,1},{7,3},{9,13},{11,15},{13,9},{15,11},{17,21},{19,... | collective-permute-start | bytes 307208 | tf_op jit(solution)/shard_map/ppermute | solution.py:269
  32.5 1.4 %collective-permute-start.12 = (bf16[2,64,384]{2,1,0:T(8,128)(2,1)S(1)}, bf16[2,64,384]{2,1,0:T(8,128)(2,1)S(1)}, u32[]{:S(2)}, u32[]{:S(2)}) collective-permute-start(bf16[2,64,384]{2,1,0:T(8,128)(2,1)S(1)} %get-tuple-element.51), channel_id=1, source_target_pairs={{0,1},{1,0},{2,3},{3,2},{4,5},{5,4},{6,7},{7,6},{8,9},{9,8},{10,11... | collective-permute-start | bytes 294920 | tf_op jit(solution)/shard_map/ppermute | solution.py:258

commit v7 on v6

--- a/solution.py
+++ b/solution.py
@@ -103,38 +103,61 @@
     width = heads * DH
     pairs += [(wk_hbm, weight_ref.at[:, pl.ds(0, width)]), (wv_hbm, weight_ref.at[:, pl.ds(width, width)])]
     copies = fetch(pairs, sems)
-    slots = [flags_ref[t : t + 1, :] for t in range(tiles)]
-    keeps = [flags_ref[tiles + t : tiles + t + 1, :] for t in range(tiles)]
     mine = flags_ref[2 * tiles : 2 * tiles + 1, :]
-    stores = []
-    for h in range(heads):
-        cols = slice(h * DH, (h + 1) * DH)
-        if h:
-            copies[h - 1].wait()
-        cache = first_ref if h == 0 else cache_buf.at[h - 1]
-        keys, values = (cache[0, 0], cache[0, 1]), (cache[1, 0], cache[1, 1])
-        probs, grads, queries, outs = [], [], [], []
-        for t in range(tiles):
-            rows = slice(t * TILE, (t + 1) * TILE)
-            query, grad = q_ref[rows, cols], g_ref[rows, cols]
-            attention_lo, score_lo = backward(pick(slots[t], keys), pick(slots[t], values), query, grad)
-            probs.append(attention_lo)
-            grads.append(score_lo)
-            queries.append(query * keeps[t].astype(BF16))
-            outs.append(grad * keeps[t].astype(BF16))
-        score_grads = jnp.concatenate(grads, axis=1)
-        dq = [dot(key.T, score_grads, (1, 0)) * INV_ROOT for key in keys]
-        for t in range(tiles):
-            rows = slice(t * TILE, (t + 1) * TILE)
-            dq_t = jnp.where(slots[t] == 1.0, dq[1][:, rows], dq[0][:, rows])
-            dq_buf[h, rows, :] = dq_t.astype(BF16).T
-        store = pltpu.make_async_copy(dq_buf.at[h], dq_hbm.at[:, pl.ds(h * DH, DH)], out_sems.at[h])
-        store.start()
-        stores.append(store)
-        part_ref[0, :, cols] = dot(score_grads, jnp.concatenate(queries, axis=0), (1, 0))
-        part_ref[1, :, cols] = dot(jnp.concatenate(probs, axis=1), jnp.concatenate(outs, axis=0), (1, 0))
-        main_ref[0, :, cols] = pick(mine, keys)
-        main_ref[1, :, cols] = pick(mine, values)
+    slot = (jnp.max(mine) > 0.0).astype(jnp.int32)
+    one_caption = jnp.min(flags_ref[tiles : 2 * tiles, :]) > 0.0
+    stores = [
+        pltpu.make_async_copy(dq_buf.at[h], dq_hbm.at[:, pl.ds(h * DH, DH)], out_sems.at[h]) for h in range(heads)
+    ]
+
+    @pl.when(one_caption)
+    def _():
+        for h in range(heads):
+            cols = slice(h * DH, (h + 1) * DH)
+            if h:
+                copies[h - 1].wait()
+            cache = first_ref if h == 0 else cache_buf.at[h - 1]
+            key, value = cache[0, slot], cache[1, slot]
+            query, grad = q_ref[:, cols], g_ref[:, cols]
+            attention_lo, score_lo = backward(key, value, query, grad)
+            dq_buf[h] = (dot(key.T, score_lo, (1, 0)) * INV_ROOT).astype(BF16).T
+            stores[h].start()
+            part_ref[0, :, cols] = dot(score_lo, query, (1, 0))
+            part_ref[1, :, cols] = dot(attention_lo, grad, (1, 0))
+            main_ref[0, :, cols] = key
+            main_ref[1, :, cols] = value
+
+    @pl.when(jnp.logical_not(one_caption))
+    def _():
+        slots = [flags_ref[t : t + 1, :] for t in range(tiles)]
+        keeps = [flags_ref[tiles + t : tiles + t + 1, :] for t in range(tiles)]
+        for h in range(heads):
+            cols = slice(h * DH, (h + 1) * DH)
+            if h:
+                copies[h - 1].wait()
+            cache = first_ref if h == 0 else cache_buf.at[h - 1]
+            keys, values = (cache[0, 0], cache[0, 1]), (cache[1, 0], cache[1, 1])
+            probs, grads, queries, outs = [], [], [], []
+            for t in range(tiles):
+                rows = slice(t * TILE, (t + 1) * TILE)
+                query, grad = q_ref[rows, cols], g_ref[rows, cols]
+                attention_lo, score_lo = backward(pick(slots[t], keys), pick(slots[t], values), query, grad)
+                probs.append(attention_lo)
+                grads.append(score_lo)
+                queries.append(query * keeps[t].astype(BF16))
+                outs.append(grad * keeps[t].astype(BF16))
+            score_grads = jnp.concatenate(grads, axis=1)
+            dq = [dot(key.T, score_grads, (1, 0)) * INV_ROOT for key in keys]
+            for t in range(tiles):
+                rows = slice(t * TILE, (t + 1) * TILE)
+                dq_t = jnp.where(slots[t] == 1.0, dq[1][:, rows], dq[0][:, rows])
+                dq_buf[h, rows, :] = dq_t.astype(BF16).T
+            stores[h].start()
+            part_ref[0, :, cols] = dot(score_grads, jnp.concatenate(queries, axis=0), (1, 0))
+            part_ref[1, :, cols] = dot(jnp.concatenate(probs, axis=1), jnp.concatenate(outs, axis=0), (1, 0))
+            main_ref[0, :, cols] = pick(mine, keys)
+            main_ref[1, :, cols] = pick(mine, values)
+
     for copy in stores + copies[heads - 1 :]:
         copy.wait()
 
@@ -145,8 +168,7 @@
     places = []
     for s in range(blocks):
         rel = jnp.bitwise_xor(jnp.bitwise_xor(me, s), core)
-        pair, quarter = jnp.right_shift(rel, 1), blocks // 4
-        place = jnp.where(pair >= quarter, 2 * (pair - quarter), 2 * (quarter - 1 - pair) + 1)
+        place = blocks // 2 - 1 - jnp.right_shift(rel, 1)
         place += jnp.bitwise_and(rel, 1) * (blocks // 2)
         places.append(pl.ds(pl.multiple_of(place * block_rows, block_rows), block_rows))
     for h in range(heads):
@@ -379,8 +401,7 @@
     block = like(block_rows, 2 * width)
     far = call(pair_kernel, "pair", (block,) * (seq_count // 2), (kept, swap(sent, "head", 1)), [vmem] * 2)
     came_own = swap(sent_own, "head", 1)
-    quarter = seq_count // 4
-    bases = [2 * b for i in range(quarter) for b in (quarter + i, quarter - 1 - i)]
+    bases = [2 * (seq_count // 2 - 1 - i) for i in range(seq_count // 2)]
     arrived, own = [], None
     for i, base in enumerate(bases):
         mine = call(

time: 34.8 us -> 34.5 us (level)
  Pallas kernels: 8.88 us -> 8.5 us
    pallas_call x12, Pallas kernels: 8.88 us -> 8.5 us  [call(): pl.pallas_call(kernel, out_shape=out_shape, in_specs=specs, out_specs=out...]
  transfers between devices with their start and end apart: 13 -> 13, of which waited for: 8 -> 7; matrix products, arithmetic and copies ran while one was open for 0% -> 0% of each run, Pallas kernels for 19% -> 18%
where the time goes in v7:
time: 34.5 us; the launch traced here: 34.3 us
  starting transfers between devices  15.6 us (45%)
  waiting for transfers between devices  9.5 us (28%)
  Pallas kernels  8.5 us (25%)
  between operations  0.72 us (2%)
    pallas_call x12, Pallas kernels, call(): pl.pallas_call(kernel, out_shape=out_shape, in_specs=specs, out_specs=out...  8.5 us
    ppermute x4, starting transfers between devices, send(): return lax.ppermute(block, ('seq', 'head'), pairs)  5.67 us
    ppermute x8, waiting for transfers between devices, swap(): return lax.ppermute(array, axis, [(i, i ^ bit) for i in range(n)])  5.18 us
    ppermute x1, starting transfers between devices, shards_pairs(): lax.ppermute(to_z, 'seq', [(s, (s + (2 if s & 1 else -2)) % seq_count) fo...  5.1 us
    ppermute x8, starting transfers between devices, swap(): return lax.ppermute(array, axis, [(i, i ^ bit) for i in range(n)])  4.86 us
    ppermute x4, waiting for transfers between devices, send(): return lax.ppermute(block, ('seq', 'head'), pairs)  4.31 us
  transfers between devices with their start and end apart: 13, of which 7 were waited for; matrix products, arithmetic and copies ran while one was open for 0% of the time, Pallas kernels for 18%

profile of v7, /device:TPU:0, one launch (start us, length us, event | category | flops | bytes accessed | tf_op | source)
XLA Modules:
  0.0 34.3 jit_solution(12918609248802072116)
XLA Ops:
  0.6 1.3 %stage.1 = (bf16[2,128,384]{2,1,0:T(8,128)(2,1)S(1)}, bf16[2,128,384]{2,1,0:T(8,128)(2,1)S(1)}, bf16[384,384]{1,0:T(8,128)(2,1)S(1)}, bf16[384,384]{1,0:T(8,128)...) custom-call(s32[2,3]{1,0:T(2,128)} %bitcast.2, ...), custom_call_target="tpu_custom_call" | custom-call | bytes 3600000 | tf_op jit(solution)/shard_map/stage/pallas_call | solution.py:296
  1.9 5.1 %collective-permute-start = (bf16[2,128,384]{2,1,0:T(8,128)(2,1)S(1)}, bf16[2,128,384]{2,1,0:T(8,128)(2,1)S(1)}, u32[]{:S(2)}, u32[]{:S(2)}) collective-permute-start(bf16[2,128,384]{2,1,0:T(8,128)(2,1)S(1)} %get-tuple-element.32), channel_id=1, source_target_pairs={{0,24},{4,12},{8,0},{12,20},{16,8},{20,28},{24,16},{28,4},{1,25},{... | collective-permute-start | bytes 589832 | tf_op jit(solution)/shard_map/ppermute | solution.py:349
  7.0 4.0 %own_tiles.1 = (bf16[384,384]{1,0:T(8,128)(2,1)}, f32[2,512,384]{2,1,0:T(8,128)S(1)}, bf16[2,512,384]{2,1,0:T(8,128)(2,1)S(1)}, bf16[1536,768]{1,0:T(8,128)(2,1)S(1)}) custom-call(f32[8,128]{1,0:T(8,128)S(1)} %get-tuple-element.27.flags_ref, bf16[384,384]{1,0:T(8,128)(2,1)S(1)} %get-tuple-element.28.q_ref, bf16[384,384]{1,0:T(8,128)(2,1)S(1)} %get-tuple-element.29.g_ref, ...), custom_call_target="tpu_custom_call" | custom-call | bytes 18000000 | tf_op jit(solution)/shard_map/own_tiles/pallas_call | solution.py:296
  11.0 1.0 %early_text.1 = (bf16[512,768]{1,0:T(8,128)(2,1)S(1)}, bf16[4,64,768]{2,1,0:T(8,128)(2,1)S(1)}, bf16[4,64,768]{2,1,0:T(8,128)(2,1)S(1)}) custom-call(f32[8,128]{1,0:T(8,128)S(1)} %get-tuple-element.27.flags_ref, f32[2,512,384]{2,1,0:T(8,128)S(1)} %get-tuple-element.35.part_ref, bf16[1536,768]{1,0:T(8,128)(2,1)S(1)} %get-tuple-element.36.weight_ref), custom_call_target="tpu_custom_call" | custom-call | bytes 3600000 | tf_op jit(solution)/shard_map/early_text/pallas_call | solution.py:296
  12.1 1.3 %collective-permute-done.1.y_ref = bf16[2,128,384]{2,1,0:T(8,128)(2,1)S(1)} collective-permute-done((bf16[2,128,384]{2,1,0:T(8,128)(2,1)S(1)}, bf16[2,128,384]{2,1,0:T(8,128)(2,1)S(1)}, u32[]{:S(2)}, u32[]{:S(2)}) %collective-permute-start.1) | collective-permute-done | bytes 196640 | tf_op jit(solution)/shard_map/ppermute | solution.py:280
  13.4 0.2 first_text.1
  13.7 0.8 %second_text.1 = (bf16[4,64,768]{2,1,0:T(8,128)(2,1)S(1)}, bf16[4,64,768]{2,1,0:T(8,128)(2,1)S(1)}) custom-call(bf16[512,768]{1,0:T(8,128)(2,1)S(1)} %get-tuple-element.40.both_ref, bf16[1536,768]{1,0:T(8,128)(2,1)S(1)} %get-tuple-element.36.weight_ref), custom_call_target="tpu_custom_call" | custom-call | bytes 3600000 | tf_op jit(solution)/shard_map/second_text/pallas_call | solution.py:296
  14.5 0.6 %collective-permute-start.2 = (bf16[4,64,768]{2,1,0:T(8,128)(2,1)S(1)}, bf16[4,64,768]{2,1,0:T(8,128)(2,1)S(1)}, u32[]{:S(2)}, u32[]{:S(2)}) collective-permute-start(bf16[4,64,768]{2,1,0:T(8,128)(2,1)S(1)} %get-tuple-element.42), channel_id=1, source_target_pairs={{0,1},{1,0},{2,3},{3,2},{4,5},{5,4},{6,7},{7,6},{8,9},{9,8},{10,11... | collective-permute-start | bytes 1179656 | tf_op jit(solution)/shard_map/ppermute | solution.py:280
  15.1 0.3 collective-permute-done.3.came_ref
  15.5 1.6 %collective-permute-start.10 = (bf16[64,768]{1,0:T(8,128)(2,1)S(1)}, bf16[64,768]{1,0:T(8,128)(2,1)S(1)}, u32[]{:S(2)}, u32[]{:S(2)}) collective-permute-start(bf16[64,768]{1,0:T(8,128)(2,1)S(1)} %get-tuple-element.49), channel_id=1, source_target_pairs={{0,2},{1,3},{2,0},{3,1},{4,6},{5,7},{6,4},{7,5},{8,10},{9,11},{10,... | collective-permute-start | bytes 294920 | tf_op jit(solution)/shard_map/ppermute | solution.py:280
  17.1 0.5 %collective-permute-start.8 = (bf16[64,768]{1,0:T(8,128)(2,1)S(1)}, bf16[64,768]{1,0:T(8,128)(2,1)S(1)}, u32[]{:S(2)}, u32[]{:S(2)}) collective-permute-start(bf16[64,768]{1,0:T(8,128)(2,1)S(1)} %get-tuple-element.48), channel_id=1, source_target_pairs={{0,2},{1,3},{2,0},{3,1},{4,6},{5,7},{6,4},{7,5},{8,10},{9,11},{10,... | collective-permute-start | bytes 294920 | tf_op jit(solution)/shard_map/ppermute | solution.py:280
  17.6 1.5 %collective-permute-start.6 = (bf16[64,768]{1,0:T(8,128)(2,1)S(1)}, bf16[64,768]{1,0:T(8,128)(2,1)S(1)}, u32[]{:S(2)}, u32[]{:S(2)}) collective-permute-start(bf16[64,768]{1,0:T(8,128)(2,1)S(1)} %get-tuple-element.47), channel_id=1, source_target_pairs={{0,2},{1,3},{2,0},{3,1},{4,6},{5,7},{6,4},{7,5},{8,10},{9,11},{10,... | collective-permute-start | bytes 294920 | tf_op jit(solution)/shard_map/ppermute | solution.py:280
  19.1 0.5 %collective-permute-start.4 = (bf16[64,768]{1,0:T(8,128)(2,1)S(1)}, bf16[64,768]{1,0:T(8,128)(2,1)S(1)}, u32[]{:S(2)}, u32[]{:S(2)}) collective-permute-start(bf16[64,768]{1,0:T(8,128)(2,1)S(1)} %get-tuple-element.45), channel_id=1, source_target_pairs={{0,2},{1,3},{2,0},{3,1},{4,6},{5,7},{6,4},{7,5},{8,10},{9,11},{10,... | collective-permute-start | bytes 294920 | tf_op jit(solution)/shard_map/ppermute | solution.py:280
  19.6 1.6 %collective-permute-done.10.crossed_ref = bf16[64,768]{1,0:T(8,128)(2,1)S(1)} collective-permute-done((bf16[64,768]{1,0:T(8,128)(2,1)S(1)}, bf16[64,768]{1,0:T(8,128)(2,1)S(1)}, u32[]{:S(2)}, u32[]{:S(2)}) %collective-permute-start.10) | collective-permute-done | bytes 98336 | tf_op jit(solution)/shard_map/ppermute | solution.py:280
  21.2 2.1 %collective-permute-start.11 = (bf16[25,16,128]{2,1,0:T(8,128)(2,1)S(1)}, bf16[25,16,128]{2,1,0:T(8,128)(2,1)S(1)}, u32[]{:S(2)}, u32[]{:S(2)}) collective-permute-start(bf16[25,16,128]{2,1,0:T(8,128)(2,1)S(1)} %cross.7), channel_id=1, source_target_pairs={{0,24},{1,29},{2,26},{3,31},{4,28},{5,25},{6,30},{7,27},{8,16},{9,... | collective-permute-start | bytes 307208 | tf_op jit(solution)/shard_map/ppermute | solution.py:291
  23.5 1.2 %collective-permute-start.9 = (bf16[25,16,128]{2,1,0:T(8,128)(2,1)S(1)}, bf16[25,16,128]{2,1,0:T(8,128)(2,1)S(1)}, u32[]{:S(2)}, u32[]{:S(2)}) collective-permute-start(bf16[25,16,128]{2,1,0:T(8,128)(2,1)S(1)} %cross.6), channel_id=1, source_target_pairs={{0,16},{1,21},{2,18},{3,23},{4,20},{5,17},{6,22},{7,19},{8,24},{9,... | collective-permute-start | bytes 307208 | tf_op jit(solution)/shard_map/ppermute | solution.py:291
  24.7 0.7 %collective-permute-done.6.crossed_ref = bf16[64,768]{1,0:T(8,128)(2,1)S(1)} collective-permute-done((bf16[64,768]{1,0:T(8,128)(2,1)S(1)}, bf16[64,768]{1,0:T(8,128)(2,1)S(1)}, u32[]{:S(2)}, u32[]{:S(2)}) %collective-permute-start.6) | collective-permute-done | bytes 98336 | tf_op jit(solution)/shard_map/ppermute | solution.py:280
  25.5 1.6 %collective-permute-start.7 = (bf16[25,16,128]{2,1,0:T(8,128)(2,1)S(1)}, bf16[25,16,128]{2,1,0:T(8,128)(2,1)S(1)}, u32[]{:S(2)}, u32[]{:S(2)}) collective-permute-start(bf16[25,16,128]{2,1,0:T(8,128)(2,1)S(1)} %cross.5), channel_id=1, source_target_pairs={{0,8},{1,13},{2,10},{3,15},{4,12},{5,9},{6,14},{7,11},{8,0},{9,5},... | collective-permute-start | bytes 307208 | tf_op jit(solution)/shard_map/ppermute | solution.py:291
  27.1 0.7 %collective-permute-start.5 = (bf16[25,16,128]{2,1,0:T(8,128)(2,1)S(1)}, bf16[25,16,128]{2,1,0:T(8,128)(2,1)S(1)}, u32[]{:S(2)}, u32[]{:S(2)}) collective-permute-start(bf16[25,16,128]{2,1,0:T(8,128)(2,1)S(1)} %cross.4.refs_4_), channel_id=1, source_target_pairs={{1,5},{3,7},{5,1},{7,3},{9,13},{11,15},{13,9},{15,11},{17,21},{19,... | collective-permute-start | bytes 307208 | tf_op jit(solution)/shard_map/ppermute | solution.py:291
  27.9 4.3 %collective-permute-done.9.refs_2_ = bf16[25,16,128]{2,1,0:T(8,128)(2,1)S(1)} collective-permute-done((bf16[25,16,128]{2,1,0:T(8,128)(2,1)S(1)}, bf16[25,16,128]{2,1,0:T(8,128)(2,1)S(1)}, u32[]{:S(2)}, u32[]{:S(2)}) %collective-permute-start.9) | collective-permute-done | bytes 102432 | tf_op jit(solution)/shard_map/ppermute | solution.py:291
  32.1 0.2 captions.1
  32.3 0.1 collective-permute-start.12
  32.4 1.2 %collective-permute-done.12.came_ref = bf16[2,64,384]{2,1,0:T(8,128)(2,1)S(1)} collective-permute-done((bf16[2,64,384]{2,1,0:T(8,128)(2,1)S(1)}, bf16[2,64,384]{2,1,0:T(8,128)(2,1)S(1)}, u32[]{:S(2)}, u32[]{:S(2)}) %collective-permute-start.12) | collective-permute-done | bytes 98336 | tf_op jit(solution)/shard_map/ppermute | solution.py:280
  33.7 0.7 %final.1 = bf16[2,64,384]{2,1,0:T(8,128)(2,1)} custom-call(f32[2,64,384]{2,1,0:T(8,128)S(1)} %get-tuple-element.50.kept_ref, bf16[2,64,384]{2,1,0:T(8,128)(2,1)S(1)} %collective-permute-done.12.came_ref), custom_call_target="tpu_custom_call" | custom-call | bytes 3600000 | tf_op jit(solution)/shard_map/final/pallas_call | solution.py:296
  (14 shorter events, 0.4 us)
Async XLA Ops:
  1.9 10.2 %collective-permute-start = (bf16[2,128,384]{2,1,0:T(8,128)(2,1)S(1)}, bf16[2,128,384]{2,1,0:T(8,128)(2,1)S(1)}, u32[]{:S(2)}, u32[]{:S(2)}) collective-permute-start(bf16[2,128,384]{2,1,0:T(8,128)(2,1)S(1)} %get-tuple-element.32), channel_id=1, source_target_pairs={{0,24},{4,12},{8,0},{12,20},{16,8},{20,28},{24,16},{28,4},{1,25},{... | collective-permute-start | bytes 589832 | tf_op jit(solution)/shard_map/ppermute | solution.py:349
  7.0 6.4 %collective-permute-start.1 = (bf16[2,128,384]{2,1,0:T(8,128)(2,1)S(1)}, bf16[2,128,384]{2,1,0:T(8,128)(2,1)S(1)}, u32[]{:S(2)}, u32[]{:S(2)}) collective-permute-start(bf16[2,128,384]{2,1,0:T(8,128)(2,1)S(1)} %get-tuple-element.33), channel_id=1, source_target_pairs={{0,4},{4,0},{8,12},{12,8},{16,20},{20,16},{24,28},{28,24},{1,5},{5... | collective-permute-start | bytes 589832 | tf_op jit(solution)/shard_map/ppermute | solution.py:280
  13.6 1.8 %collective-permute-start.3 = (bf16[4,64,768]{2,1,0:T(8,128)(2,1)S(1)}, bf16[4,64,768]{2,1,0:T(8,128)(2,1)S(1)}, u32[]{:S(2)}, u32[]{:S(2)}) collective-permute-start(bf16[4,64,768]{2,1,0:T(8,128)(2,1)S(1)} %get-tuple-element.44), channel_id=1, source_target_pairs={{0,1},{1,0},{2,3},{3,2},{4,5},{5,4},{6,7},{7,6},{8,9},{9,8},{10,11... | collective-permute-start | bytes 1179656 | tf_op jit(solution)/shard_map/ppermute | solution.py:280
  14.5 5.1 %collective-permute-start.2 = (bf16[4,64,768]{2,1,0:T(8,128)(2,1)S(1)}, bf16[4,64,768]{2,1,0:T(8,128)(2,1)S(1)}, u32[]{:S(2)}, u32[]{:S(2)}) collective-permute-start(bf16[4,64,768]{2,1,0:T(8,128)(2,1)S(1)} %get-tuple-element.42), channel_id=1, source_target_pairs={{0,1},{1,0},{2,3},{3,2},{4,5},{5,4},{6,7},{7,6},{8,9},{9,8},{10,11... | collective-permute-start | bytes 1179656 | tf_op jit(solution)/shard_map/ppermute | solution.py:280
  15.5 5.7 %collective-permute-start.10 = (bf16[64,768]{1,0:T(8,128)(2,1)S(1)}, bf16[64,768]{1,0:T(8,128)(2,1)S(1)}, u32[]{:S(2)}, u32[]{:S(2)}) collective-permute-start(bf16[64,768]{1,0:T(8,128)(2,1)S(1)} %get-tuple-element.49), channel_id=1, source_target_pairs={{0,2},{1,3},{2,0},{3,1},{4,6},{5,7},{6,4},{7,5},{8,10},{9,11},{10,... | collective-permute-start | bytes 294920 | tf_op jit(solution)/shard_map/ppermute | solution.py:280
  17.1 6.3 %collective-permute-start.8 = (bf16[64,768]{1,0:T(8,128)(2,1)S(1)}, bf16[64,768]{1,0:T(8,128)(2,1)S(1)}, u32[]{:S(2)}, u32[]{:S(2)}) collective-permute-start(bf16[64,768]{1,0:T(8,128)(2,1)S(1)} %get-tuple-element.48), channel_id=1, source_target_pairs={{0,2},{1,3},{2,0},{3,1},{4,6},{5,7},{6,4},{7,5},{8,10},{9,11},{10,... | collective-permute-start | bytes 294920 | tf_op jit(solution)/shard_map/ppermute | solution.py:280
  17.6 7.8 %collective-permute-start.6 = (bf16[64,768]{1,0:T(8,128)(2,1)S(1)}, bf16[64,768]{1,0:T(8,128)(2,1)S(1)}, u32[]{:S(2)}, u32[]{:S(2)}) collective-permute-start(bf16[64,768]{1,0:T(8,128)(2,1)S(1)} %get-tuple-element.47), channel_id=1, source_target_pairs={{0,2},{1,3},{2,0},{3,1},{4,6},{5,7},{6,4},{7,5},{8,10},{9,11},{10,... | collective-permute-start | bytes 294920 | tf_op jit(solution)/shard_map/ppermute | solution.py:280
  19.1 8.0 %collective-permute-start.4 = (bf16[64,768]{1,0:T(8,128)(2,1)S(1)}, bf16[64,768]{1,0:T(8,128)(2,1)S(1)}, u32[]{:S(2)}, u32[]{:S(2)}) collective-permute-start(bf16[64,768]{1,0:T(8,128)(2,1)S(1)} %get-tuple-element.45), channel_id=1, source_target_pairs={{0,2},{1,3},{2,0},{3,1},{4,6},{5,7},{6,4},{7,5},{8,10},{9,11},{10,... | collective-permute-start | bytes 294920 | tf_op jit(solution)/shard_map/ppermute | solution.py:280
  21.2 6.6 %collective-permute-start.11 = (bf16[25,16,128]{2,1,0:T(8,128)(2,1)S(1)}, bf16[25,16,128]{2,1,0:T(8,128)(2,1)S(1)}, u32[]{:S(2)}, u32[]{:S(2)}) collective-permute-start(bf16[25,16,128]{2,1,0:T(8,128)(2,1)S(1)} %cross.7), channel_id=1, source_target_pairs={{0,24},{1,29},{2,26},{3,31},{4,28},{5,25},{6,30},{7,27},{8,16},{9,... | collective-permute-start | bytes 307208 | tf_op jit(solution)/shard_map/ppermute | solution.py:291
  23.5 8.7 %collective-permute-start.9 = (bf16[25,16,128]{2,1,0:T(8,128)(2,1)S(1)}, bf16[25,16,128]{2,1,0:T(8,128)(2,1)S(1)}, u32[]{:S(2)}, u32[]{:S(2)}) collective-permute-start(bf16[25,16,128]{2,1,0:T(8,128)(2,1)S(1)} %cross.6), channel_id=1, source_target_pairs={{0,16},{1,21},{2,18},{3,23},{4,20},{5,17},{6,22},{7,19},{8,24},{9,... | collective-permute-start | bytes 307208 | tf_op jit(solution)/shard_map/ppermute | solution.py:291
  25.5 6.7 %collective-permute-start.7 = (bf16[25,16,128]{2,1,0:T(8,128)(2,1)S(1)}, bf16[25,16,128]{2,1,0:T(8,128)(2,1)S(1)}, u32[]{:S(2)}, u32[]{:S(2)}) collective-permute-start(bf16[25,16,128]{2,1,0:T(8,128)(2,1)S(1)} %cross.5), channel_id=1, source_target_pairs={{0,8},{1,13},{2,10},{3,15},{4,12},{5,9},{6,14},{7,11},{8,0},{9,5},... | collective-permute-start | bytes 307208 | tf_op jit(solution)/shard_map/ppermute | solution.py:291
  27.1 5.0 %collective-permute-start.5 = (bf16[25,16,128]{2,1,0:T(8,128)(2,1)S(1)}, bf16[25,16,128]{2,1,0:T(8,128)(2,1)S(1)}, u32[]{:S(2)}, u32[]{:S(2)}) collective-permute-start(bf16[25,16,128]{2,1,0:T(8,128)(2,1)S(1)} %cross.4.refs_4_), channel_id=1, source_target_pairs={{1,5},{3,7},{5,1},{7,3},{9,13},{11,15},{13,9},{15,11},{17,21},{19,... | collective-permute-start | bytes 307208 | tf_op jit(solution)/shard_map/ppermute | solution.py:291
  32.3 1.4 %collective-permute-start.12 = (bf16[2,64,384]{2,1,0:T(8,128)(2,1)S(1)}, bf16[2,64,384]{2,1,0:T(8,128)(2,1)S(1)}, u32[]{:S(2)}, u32[]{:S(2)}) collective-permute-start(bf16[2,64,384]{2,1,0:T(8,128)(2,1)S(1)} %get-tuple-element.51), channel_id=1, source_target_pairs={{0,1},{1,0},{2,3},{3,2},{4,5},{5,4},{6,7},{7,6},{8,9},{9,8},{10,11... | collective-permute-start | bytes 294920 | tf_op jit(solution)/shard_map/ppermute | solution.py:280

commit v8 on v7

--- a/solution.py
+++ b/solution.py
@@ -185,14 +185,11 @@
             both_ref[rows, width + h * DH : width + (h + 1) * DH] = dv[s * block_rows : (s + 1) * block_rows]
 
 
-def project(both_ref, weight_ref, rel, kept_ref, sent_ref):
-    features = kept_ref.shape[2]
+def project(both, weight_ref, rel, out_ref):
+    features = out_ref.shape[2]
     chip = jnp.right_shift(lax.axis_index("head"), 1)
     rows = pl.ds(pl.multiple_of(jnp.bitwise_xor(chip, rel) * features, features), features)
-    text = dot(both_ref[...], weight_ref[rows, :], (1, 1)).astype(BF16)
-    half = text.shape[0] // 2
-    kept_ref[...] = text[:half].reshape(kept_ref.shape)
-    sent_ref[...] = text[half:].reshape(sent_ref.shape)
+    out_ref[...] = dot(both, weight_ref[rows, :], (1, 1)).astype(BF16).reshape(out_ref.shape)
 
 
 def expects(flags_ref):
@@ -200,22 +197,22 @@
     return jnp.max(flags_ref[last : last + 1, :]) > 0.0
 
 
-def early_text_kernel(heads, blocks, flags_ref, part_ref, weight_ref, both_ref, kept_ref, sent_ref):
+def early_text_kernel(heads, blocks, flags_ref, part_ref, weight_ref, both_ref, sent_ref):
     @pl.when(jnp.logical_not(expects(flags_ref)))
     def _():
         gather_parts(heads, blocks, None, part_ref, both_ref)
-        project(both_ref, weight_ref, 1, kept_ref, sent_ref)
+        project(both_ref[L // 2 :, :], weight_ref, 1, sent_ref)
 
 
 def first_text_kernel(heads, blocks, flags_ref, z_ref, y_ref, main_ref, part_ref, weight_ref, *refs):
-    early, outs = refs[:3], refs[3:]
+    early, outs = refs[:2], refs[2:]
     come = expects(flags_ref)
 
     @pl.when(come)
     def _():
-        both_ref, kept_ref, sent_ref = outs
+        both_ref, sent_ref = outs
         gather_parts(heads, blocks, main_ref, part_ref, both_ref, (y_ref, z_ref))
-        project(both_ref, weight_ref, 1, kept_ref, sent_ref)
+        project(both_ref[L // 2 :, :], weight_ref, 1, sent_ref)
 
     @pl.when(jnp.logical_not(come))
     def _():
@@ -223,8 +220,10 @@
             b[...] = a[...]
 
 
-def second_text_kernel(both_ref, weight_ref, kept_ref, sent_ref):
-    project(both_ref, weight_ref, 0, kept_ref, sent_ref)
+def second_text_kernel(both_ref, weight_ref, sent_own_ref, kept_ref, kept_own_ref):
+    project(both_ref[L // 2 :, :], weight_ref, 0, sent_own_ref)
+    project(both_ref[: L // 2, :], weight_ref, 1, kept_ref)
+    project(both_ref[: L // 2, :], weight_ref, 0, kept_own_ref)
 
 
 def pair_kernel(kept_ref, came_ref, *outs):
@@ -370,7 +369,7 @@
         out_specs=(hbm, vmem, vmem, vmem),
     )
     half = like(seq_count // 2, block_rows, 2 * width)
-    texts = (like(L, 2 * width), half, half)
+    texts = (like(L, 2 * width), half)
     early = call(
         functools.partial(early_text_kernel, heads, seq_count),
         "early_text",
@@ -380,19 +379,19 @@
         limit=KERNEL_LIMIT,
         hint_us=1.0,
     )
-    both, kept, sent = call(
+    both, sent = call(
         functools.partial(first_text_kernel, heads, seq_count),
         "first_text",
         texts,
         (flags, from_z, from_y, main, part, weight, *early),
-        [vmem] * 9,
+        [vmem] * 8,
         limit=KERNEL_LIMIT,
         hint_us=2.0,
     )
-    kept_own, sent_own = call(
+    sent_own, kept, kept_own = call(
         second_text_kernel,
         "second_text",
-        (half, half),
+        (half, half, half),
         (both, weight),
         [vmem] * 2,
         limit=KERNEL_LIMIT,

time: 34.5 us -> 34.4 us (level)
  starting transfers between devices: 15.6 us -> 15.1 us
  waiting for transfers between devices: 9.5 us -> 9.9 us
    ppermute x4, starting transfers between devices: 5.67 us -> 5.07 us  [send(): return lax.ppermute(block, ('seq', 'head'), pairs)]
  transfers between devices with their start and end apart: 13 -> 13, of which waited for: 7 -> 6; matrix products, arithmetic and copies ran while one was open for 0% -> 0% of each run, Pallas kernels for 18% -> 18%
where the time goes in v8:
time: 34.4 us; the launch traced here: 34.2 us
  starting transfers between devices  15.1 us (44%)
  waiting for transfers between devices  9.9 us (29%)
  Pallas kernels  8.49 us (25%)
  between operations  0.72 us (2%)
    pallas_call x12, Pallas kernels, call(): pl.pallas_call(kernel, out_shape=out_shape, in_specs=specs, out_specs=out...  8.49 us
    ppermute x8, waiting for transfers between devices, swap(): return lax.ppermute(array, axis, [(i, i ^ bit) for i in range(n)])  5.42 us
    ppermute x1, starting transfers between devices, shards_pairs(): lax.ppermute(to_z, 'seq', [(s, (s + (2 if s & 1 else -2)) % seq_count) fo...  5.1 us
    ppermute x4, starting transfers between devices, send(): return lax.ppermute(block, ('seq', 'head'), pairs)  5.07 us
    ppermute x8, starting transfers between devices, swap(): return lax.ppermute(array, axis, [(i, i ^ bit) for i in range(n)])  4.91 us
    ppermute x4, waiting for transfers between devices, send(): return lax.ppermute(block, ('seq', 'head'), pairs)  4.47 us
  transfers between devices with their start and end apart: 13, of which 6 were waited for; matrix products, arithmetic and copies ran while one was open for 0% of the time, Pallas kernels for 18%

profile of v8, /device:TPU:0, one launch (start us, length us, event | category | flops | bytes accessed | tf_op | source)
XLA Modules:
  0.0 34.2 jit_solution(3709768545729492647)
XLA Ops:
  0.6 1.3 %stage.1 = (bf16[2,128,384]{2,1,0:T(8,128)(2,1)S(1)}, bf16[2,128,384]{2,1,0:T(8,128)(2,1)S(1)}, bf16[384,384]{1,0:T(8,128)(2,1)S(1)}, bf16[384,384]{1,0:T(8,128)...) custom-call(s32[2,3]{1,0:T(2,128)} %bitcast.2, ...), custom_call_target="tpu_custom_call" | custom-call | bytes 3600000 | tf_op jit(solution)/shard_map/stage/pallas_call | solution.py:295
  1.9 5.1 %collective-permute-start = (bf16[2,128,384]{2,1,0:T(8,128)(2,1)S(1)}, bf16[2,128,384]{2,1,0:T(8,128)(2,1)S(1)}, u32[]{:S(2)}, u32[]{:S(2)}) collective-permute-start(bf16[2,128,384]{2,1,0:T(8,128)(2,1)S(1)} %get-tuple-element.31), channel_id=1, source_target_pairs={{0,24},{4,12},{8,0},{12,20},{16,8},{20,28},{24,16},{28,4},{1,25},{... | collective-permute-start | bytes 589832 | tf_op jit(solution)/shard_map/ppermute | solution.py:348
  7.0 4.0 %own_tiles.1 = (bf16[384,384]{1,0:T(8,128)(2,1)}, f32[2,512,384]{2,1,0:T(8,128)S(1)}, bf16[2,512,384]{2,1,0:T(8,128)(2,1)S(1)}, bf16[1536,768]{1,0:T(8,128)(2,1)S(1)}) custom-call(f32[8,128]{1,0:T(8,128)S(1)} %get-tuple-element.26.flags_ref, bf16[384,384]{1,0:T(8,128)(2,1)S(1)} %get-tuple-element.27.q_ref, bf16[384,384]{1,0:T(8,128)(2,1)S(1)} %get-tuple-element.28.g_ref, ...), custom_call_target="tpu_custom_call" | custom-call | bytes 18000000 | tf_op jit(solution)/shard_map/own_tiles/pallas_call | solution.py:295
  11.0 0.7 %early_text.1 = (bf16[512,768]{1,0:T(8,128)(2,1)S(1)}, bf16[4,64,768]{2,1,0:T(8,128)(2,1)S(1)}) custom-call(f32[8,128]{1,0:T(8,128)S(1)} %get-tuple-element.26.flags_ref, f32[2,512,384]{2,1,0:T(8,128)S(1)} %get-tuple-element.34.part_ref, bf16[1536,768]{1,0:T(8,128)(2,1)S(1)} %get-tuple-element.35.weight_ref), custom_call_target="tpu_custom_call" | custom-call | bytes 3600000 | tf_op jit(solution)/shard_map/early_text/pallas_call | solution.py:295
  11.8 1.6 %collective-permute-done.1.y_ref = bf16[2,128,384]{2,1,0:T(8,128)(2,1)S(1)} collective-permute-done((bf16[2,128,384]{2,1,0:T(8,128)(2,1)S(1)}, bf16[2,128,384]{2,1,0:T(8,128)(2,1)S(1)}, u32[]{:S(2)}, u32[]{:S(2)}) %collective-permute-start.1) | collective-permute-done | bytes 196640 | tf_op jit(solution)/shard_map/ppermute | solution.py:279
  13.4 0.2 first_text.1
  13.7 1.1 %second_text.1 = (bf16[4,64,768]{2,1,0:T(8,128)(2,1)S(1)}, bf16[4,64,768]{2,1,0:T(8,128)(2,1)S(1)}, bf16[4,64,768]{2,1,0:T(8,128)(2,1)S(1)}) custom-call(bf16[512,768]{1,0:T(8,128)(2,1)S(1)} %get-tuple-element.38.both_ref, bf16[1536,768]{1,0:T(8,128)(2,1)S(1)} %get-tuple-element.35.weight_ref), custom_call_target="tpu_custom_call" | custom-call | bytes 3600000 | tf_op jit(solution)/shard_map/second_text/pallas_call | solution.py:295
  14.8 0.6 %collective-permute-start.2 = (bf16[4,64,768]{2,1,0:T(8,128)(2,1)S(1)}, bf16[4,64,768]{2,1,0:T(8,128)(2,1)S(1)}, u32[]{:S(2)}, u32[]{:S(2)}) collective-permute-start(bf16[4,64,768]{2,1,0:T(8,128)(2,1)S(1)} %get-tuple-element.40), channel_id=1, source_target_pairs={{0,1},{1,0},{2,3},{3,2},{4,5},{5,4},{6,7},{7,6},{8,9},{9,8},{10,11... | collective-permute-start | bytes 1179656 | tf_op jit(solution)/shard_map/ppermute | solution.py:279
  15.5 1.6 %collective-permute-start.10 = (bf16[64,768]{1,0:T(8,128)(2,1)S(1)}, bf16[64,768]{1,0:T(8,128)(2,1)S(1)}, u32[]{:S(2)}, u32[]{:S(2)}) collective-permute-start(bf16[64,768]{1,0:T(8,128)(2,1)S(1)} %get-tuple-element.47), channel_id=1, source_target_pairs={{0,2},{1,3},{2,0},{3,1},{4,6},{5,7},{6,4},{7,5},{8,10},{9,11},{10,... | collective-permute-start | bytes 294920 | tf_op jit(solution)/shard_map/ppermute | solution.py:279
  17.1 0.5 %collective-permute-start.8 = (bf16[64,768]{1,0:T(8,128)(2,1)S(1)}, bf16[64,768]{1,0:T(8,128)(2,1)S(1)}, u32[]{:S(2)}, u32[]{:S(2)}) collective-permute-start(bf16[64,768]{1,0:T(8,128)(2,1)S(1)} %get-tuple-element.46), channel_id=1, source_target_pairs={{0,2},{1,3},{2,0},{3,1},{4,6},{5,7},{6,4},{7,5},{8,10},{9,11},{10,... | collective-permute-start | bytes 294920 | tf_op jit(solution)/shard_map/ppermute | solution.py:279
  17.6 1.5 %collective-permute-start.6 = (bf16[64,768]{1,0:T(8,128)(2,1)S(1)}, bf16[64,768]{1,0:T(8,128)(2,1)S(1)}, u32[]{:S(2)}, u32[]{:S(2)}) collective-permute-start(bf16[64,768]{1,0:T(8,128)(2,1)S(1)} %get-tuple-element.45), channel_id=1, source_target_pairs={{0,2},{1,3},{2,0},{3,1},{4,6},{5,7},{6,4},{7,5},{8,10},{9,11},{10,... | collective-permute-start | bytes 294920 | tf_op jit(solution)/shard_map/ppermute | solution.py:279
  19.1 0.5 %collective-permute-start.4 = (bf16[64,768]{1,0:T(8,128)(2,1)S(1)}, bf16[64,768]{1,0:T(8,128)(2,1)S(1)}, u32[]{:S(2)}, u32[]{:S(2)}) collective-permute-start(bf16[64,768]{1,0:T(8,128)(2,1)S(1)} %get-tuple-element.43), channel_id=1, source_target_pairs={{0,2},{1,3},{2,0},{3,1},{4,6},{5,7},{6,4},{7,5},{8,10},{9,11},{10,... | collective-permute-start | bytes 294920 | tf_op jit(solution)/shard_map/ppermute | solution.py:279
  19.6 1.6 %collective-permute-done.10.crossed_ref = bf16[64,768]{1,0:T(8,128)(2,1)S(1)} collective-permute-done((bf16[64,768]{1,0:T(8,128)(2,1)S(1)}, bf16[64,768]{1,0:T(8,128)(2,1)S(1)}, u32[]{:S(2)}, u32[]{:S(2)}) %collective-permute-start.10) | collective-permute-done | bytes 98336 | tf_op jit(solution)/shard_map/ppermute | solution.py:279
  21.2 2.1 %collective-permute-start.11 = (bf16[25,16,128]{2,1,0:T(8,128)(2,1)S(1)}, bf16[25,16,128]{2,1,0:T(8,128)(2,1)S(1)}, u32[]{:S(2)}, u32[]{:S(2)}) collective-permute-start(bf16[25,16,128]{2,1,0:T(8,128)(2,1)S(1)} %cross.7), channel_id=1, source_target_pairs={{0,24},{1,29},{2,26},{3,31},{4,28},{5,25},{6,30},{7,27},{8,16},{9,... | collective-permute-start | bytes 307208 | tf_op jit(solution)/shard_map/ppermute | solution.py:290
  23.4 0.9 %collective-permute-start.9 = (bf16[25,16,128]{2,1,0:T(8,128)(2,1)S(1)}, bf16[25,16,128]{2,1,0:T(8,128)(2,1)S(1)}, u32[]{:S(2)}, u32[]{:S(2)}) collective-permute-start(bf16[25,16,128]{2,1,0:T(8,128)(2,1)S(1)} %cross.6), channel_id=1, source_target_pairs={{0,16},{1,21},{2,18},{3,23},{4,20},{5,17},{6,22},{7,19},{8,24},{9,... | collective-permute-start | bytes 307208 | tf_op jit(solution)/shard_map/ppermute | solution.py:290
  24.4 1.0 %collective-permute-done.6.crossed_ref = bf16[64,768]{1,0:T(8,128)(2,1)S(1)} collective-permute-done((bf16[64,768]{1,0:T(8,128)(2,1)S(1)}, bf16[64,768]{1,0:T(8,128)(2,1)S(1)}, u32[]{:S(2)}, u32[]{:S(2)}) %collective-permute-start.6) | collective-permute-done | bytes 98336 | tf_op jit(solution)/shard_map/ppermute | solution.py:279
  25.4 1.3 %collective-permute-start.7 = (bf16[25,16,128]{2,1,0:T(8,128)(2,1)S(1)}, bf16[25,16,128]{2,1,0:T(8,128)(2,1)S(1)}, u32[]{:S(2)}, u32[]{:S(2)}) collective-permute-start(bf16[25,16,128]{2,1,0:T(8,128)(2,1)S(1)} %cross.5), channel_id=1, source_target_pairs={{0,8},{1,13},{2,10},{3,15},{4,12},{5,9},{6,14},{7,11},{8,0},{9,5},... | collective-permute-start | bytes 307208 | tf_op jit(solution)/shard_map/ppermute | solution.py:290
  26.8 0.7 %collective-permute-start.5 = (bf16[25,16,128]{2,1,0:T(8,128)(2,1)S(1)}, bf16[25,16,128]{2,1,0:T(8,128)(2,1)S(1)}, u32[]{:S(2)}, u32[]{:S(2)}) collective-permute-start(bf16[25,16,128]{2,1,0:T(8,128)(2,1)S(1)} %cross.4.refs_4_), channel_id=1, source_target_pairs={{1,5},{3,7},{5,1},{7,3},{9,13},{11,15},{13,9},{15,11},{17,21},{19,... | collective-permute-start | bytes 307208 | tf_op jit(solution)/shard_map/ppermute | solution.py:290
  27.5 0.4 %collective-permute-done.11.refs_3_ = bf16[25,16,128]{2,1,0:T(8,128)(2,1)S(1)} collective-permute-done((bf16[25,16,128]{2,1,0:T(8,128)(2,1)S(1)}, bf16[25,16,128]{2,1,0:T(8,128)(2,1)S(1)}, u32[]{:S(2)}, u32[]{:S(2)}) %collective-permute-start.11) | collective-permute-done | bytes 102432 | tf_op jit(solution)/shard_map/ppermute | solution.py:290
  27.9 4.1 %collective-permute-done.9.refs_2_ = bf16[25,16,128]{2,1,0:T(8,128)(2,1)S(1)} collective-permute-done((bf16[25,16,128]{2,1,0:T(8,128)(2,1)S(1)}, bf16[25,16,128]{2,1,0:T(8,128)(2,1)S(1)}, u32[]{:S(2)}, u32[]{:S(2)}) %collective-permute-start.9) | collective-permute-done | bytes 102432 | tf_op jit(solution)/shard_map/ppermute | solution.py:290
  32.0 0.2 captions.1
  32.2 0.2 collective-permute-start.12
  32.3 1.2 %collective-permute-done.12.came_ref = bf16[2,64,384]{2,1,0:T(8,128)(2,1)S(1)} collective-permute-done((bf16[2,64,384]{2,1,0:T(8,128)(2,1)S(1)}, bf16[2,64,384]{2,1,0:T(8,128)(2,1)S(1)}, u32[]{:S(2)}, u32[]{:S(2)}) %collective-permute-start.12) | collective-permute-done | bytes 98336 | tf_op jit(solution)/shard_map/ppermute | solution.py:279
  33.5 0.7 %final.1 = bf16[2,64,384]{2,1,0:T(8,128)(2,1)} custom-call(f32[2,64,384]{2,1,0:T(8,128)S(1)} %get-tuple-element.48.kept_ref, bf16[2,64,384]{2,1,0:T(8,128)(2,1)S(1)} %collective-permute-done.12.came_ref), custom_call_target="tpu_custom_call" | custom-call | bytes 3600000 | tf_op jit(solution)/shard_map/final/pallas_call | solution.py:295
  (14 shorter events, 0.4 us)
Async XLA Ops:
  1.9 9.9 %collective-permute-start = (bf16[2,128,384]{2,1,0:T(8,128)(2,1)S(1)}, bf16[2,128,384]{2,1,0:T(8,128)(2,1)S(1)}, u32[]{:S(2)}, u32[]{:S(2)}) collective-permute-start(bf16[2,128,384]{2,1,0:T(8,128)(2,1)S(1)} %get-tuple-element.31), channel_id=1, source_target_pairs={{0,24},{4,12},{8,0},{12,20},{16,8},{20,28},{24,16},{28,4},{1,25},{... | collective-permute-start | bytes 589832 | tf_op jit(solution)/shard_map/ppermute | solution.py:348
  7.0 6.4 %collective-permute-start.1 = (bf16[2,128,384]{2,1,0:T(8,128)(2,1)S(1)}, bf16[2,128,384]{2,1,0:T(8,128)(2,1)S(1)}, u32[]{:S(2)}, u32[]{:S(2)}) collective-permute-start(bf16[2,128,384]{2,1,0:T(8,128)(2,1)S(1)} %get-tuple-element.32), channel_id=1, source_target_pairs={{0,4},{4,0},{8,12},{12,8},{16,20},{20,16},{24,28},{28,24},{1,5},{5... | collective-permute-start | bytes 589832 | tf_op jit(solution)/shard_map/ppermute | solution.py:279
  13.6 1.8 %collective-permute-start.3 = (bf16[4,64,768]{2,1,0:T(8,128)(2,1)S(1)}, bf16[4,64,768]{2,1,0:T(8,128)(2,1)S(1)}, u32[]{:S(2)}, u32[]{:S(2)}) collective-permute-start(bf16[4,64,768]{2,1,0:T(8,128)(2,1)S(1)} %get-tuple-element.42), channel_id=1, source_target_pairs={{0,1},{1,0},{2,3},{3,2},{4,5},{5,4},{6,7},{7,6},{8,9},{9,8},{10,11... | collective-permute-start | bytes 1179656 | tf_op jit(solution)/shard_map/ppermute | solution.py:279
  14.8 4.8 %collective-permute-start.2 = (bf16[4,64,768]{2,1,0:T(8,128)(2,1)S(1)}, bf16[4,64,768]{2,1,0:T(8,128)(2,1)S(1)}, u32[]{:S(2)}, u32[]{:S(2)}) collective-permute-start(bf16[4,64,768]{2,1,0:T(8,128)(2,1)S(1)} %get-tuple-element.40), channel_id=1, source_target_pairs={{0,1},{1,0},{2,3},{3,2},{4,5},{5,4},{6,7},{7,6},{8,9},{9,8},{10,11... | collective-permute-start | bytes 1179656 | tf_op jit(solution)/shard_map/ppermute | solution.py:279
  15.5 5.7 %collective-permute-start.10 = (bf16[64,768]{1,0:T(8,128)(2,1)S(1)}, bf16[64,768]{1,0:T(8,128)(2,1)S(1)}, u32[]{:S(2)}, u32[]{:S(2)}) collective-permute-start(bf16[64,768]{1,0:T(8,128)(2,1)S(1)} %get-tuple-element.47), channel_id=1, source_target_pairs={{0,2},{1,3},{2,0},{3,1},{4,6},{5,7},{6,4},{7,5},{8,10},{9,11},{10,... | collective-permute-start | bytes 294920 | tf_op jit(solution)/shard_map/ppermute | solution.py:279
  17.1 6.3 %collective-permute-start.8 = (bf16[64,768]{1,0:T(8,128)(2,1)S(1)}, bf16[64,768]{1,0:T(8,128)(2,1)S(1)}, u32[]{:S(2)}, u32[]{:S(2)}) collective-permute-start(bf16[64,768]{1,0:T(8,128)(2,1)S(1)} %get-tuple-element.46), channel_id=1, source_target_pairs={{0,2},{1,3},{2,0},{3,1},{4,6},{5,7},{6,4},{7,5},{8,10},{9,11},{10,... | collective-permute-start | bytes 294920 | tf_op jit(solution)/shard_map/ppermute | solution.py:279
  17.6 7.8 %collective-permute-start.6 = (bf16[64,768]{1,0:T(8,128)(2,1)S(1)}, bf16[64,768]{1,0:T(8,128)(2,1)S(1)}, u32[]{:S(2)}, u32[]{:S(2)}) collective-permute-start(bf16[64,768]{1,0:T(8,128)(2,1)S(1)} %get-tuple-element.45), channel_id=1, source_target_pairs={{0,2},{1,3},{2,0},{3,1},{4,6},{5,7},{6,4},{7,5},{8,10},{9,11},{10,... | collective-permute-start | bytes 294920 | tf_op jit(solution)/shard_map/ppermute | solution.py:279
  19.1 7.7 %collective-permute-start.4 = (bf16[64,768]{1,0:T(8,128)(2,1)S(1)}, bf16[64,768]{1,0:T(8,128)(2,1)S(1)}, u32[]{:S(2)}, u32[]{:S(2)}) collective-permute-start(bf16[64,768]{1,0:T(8,128)(2,1)S(1)} %get-tuple-element.43), channel_id=1, source_target_pairs={{0,2},{1,3},{2,0},{3,1},{4,6},{5,7},{6,4},{7,5},{8,10},{9,11},{10,... | collective-permute-start | bytes 294920 | tf_op jit(solution)/shard_map/ppermute | solution.py:279
  21.2 6.6 %collective-permute-start.11 = (bf16[25,16,128]{2,1,0:T(8,128)(2,1)S(1)}, bf16[25,16,128]{2,1,0:T(8,128)(2,1)S(1)}, u32[]{:S(2)}, u32[]{:S(2)}) collective-permute-start(bf16[25,16,128]{2,1,0:T(8,128)(2,1)S(1)} %cross.7), channel_id=1, source_target_pairs={{0,24},{1,29},{2,26},{3,31},{4,28},{5,25},{6,30},{7,27},{8,16},{9,... | collective-permute-start | bytes 307208 | tf_op jit(solution)/shard_map/ppermute | solution.py:290
  23.4 8.5 %collective-permute-start.9 = (bf16[25,16,128]{2,1,0:T(8,128)(2,1)S(1)}, bf16[25,16,128]{2,1,0:T(8,128)(2,1)S(1)}, u32[]{:S(2)}, u32[]{:S(2)}) collective-permute-start(bf16[25,16,128]{2,1,0:T(8,128)(2,1)S(1)} %cross.6), channel_id=1, source_target_pairs={{0,16},{1,21},{2,18},{3,23},{4,20},{5,17},{6,22},{7,19},{8,24},{9,... | collective-permute-start | bytes 307208 | tf_op jit(solution)/shard_map/ppermute | solution.py:290
  25.4 6.5 %collective-permute-start.7 = (bf16[25,16,128]{2,1,0:T(8,128)(2,1)S(1)}, bf16[25,16,128]{2,1,0:T(8,128)(2,1)S(1)}, u32[]{:S(2)}, u32[]{:S(2)}) collective-permute-start(bf16[25,16,128]{2,1,0:T(8,128)(2,1)S(1)} %cross.5), channel_id=1, source_target_pairs={{0,8},{1,13},{2,10},{3,15},{4,12},{5,9},{6,14},{7,11},{8,0},{9,5},... | collective-permute-start | bytes 307208 | tf_op jit(solution)/shard_map/ppermute | solution.py:290
  26.8 5.1 %collective-permute-start.5 = (bf16[25,16,128]{2,1,0:T(8,128)(2,1)S(1)}, bf16[25,16,128]{2,1,0:T(8,128)(2,1)S(1)}, u32[]{:S(2)}, u32[]{:S(2)}) collective-permute-start(bf16[25,16,128]{2,1,0:T(8,128)(2,1)S(1)} %cross.4.refs_4_), channel_id=1, source_target_pairs={{1,5},{3,7},{5,1},{7,3},{9,13},{11,15},{13,9},{15,11},{17,21},{19,... | collective-permute-start | bytes 307208 | tf_op jit(solution)/shard_map/ppermute | solution.py:290
  32.2 1.4 %collective-permute-start.12 = (bf16[2,64,384]{2,1,0:T(8,128)(2,1)S(1)}, bf16[2,64,384]{2,1,0:T(8,128)(2,1)S(1)}, u32[]{:S(2)}, u32[]{:S(2)}) collective-permute-start(bf16[2,64,384]{2,1,0:T(8,128)(2,1)S(1)} %get-tuple-element.49), channel_id=1, source_target_pairs={{0,1},{1,0},{2,3},{3,2},{4,5},{5,4},{6,7},{7,6},{8,9},{9,8},{10,11... | collective-permute-start | bytes 294920 | tf_op jit(solution)/shard_map/ppermute | solution.py:279

commit v9 on v8

--- a/solution.py
+++ b/solution.py
@@ -68,14 +68,9 @@
         ],
         sems,
     )
-    for c in copies[:4]:
+    for c in copies[:2]:
         c.wait()
     mine, *picked = shipping(mask_ref, me, seq_count, tiles)
-    for tile, out in zip(picked, (y_ref, z_ref), strict=True):
-        keep = (mask_ref[mine, tile] == 0).astype(F32).astype(BF16)
-        at = pl.ds(pl.multiple_of(tile * TILE, TILE), TILE)
-        out[0] = q_ref[at, :] * keep
-        out[1] = g_ref[at, :] * keep
     lanes = (1, flags_ref.shape[1])
     for t in range(tiles):
         flags_ref[t : t + 1, :] = jnp.full(lanes, mask_ref[1, t].astype(F32), F32)
@@ -88,6 +83,13 @@
     last = flags_ref.shape[0] - 1
     flags_ref[last : last + 1, :] = jnp.full(lanes, expects.astype(F32), F32)
     caption_ref[...] = jnp.full(caption_ref.shape, caps_ref[mine, me].astype(F32), F32).astype(BF16)
+    for c in copies[2:4]:
+        c.wait()
+    for tile, out in zip(picked, (y_ref, z_ref), strict=True):
+        keep = (mask_ref[mine, tile] == 0).astype(F32).astype(BF16)
+        at = pl.ds(pl.multiple_of(tile * TILE, TILE), TILE)
+        out[0] = q_ref[at, :] * keep
+        out[1] = g_ref[at, :] * keep
     copies[4].wait()
 
 

time: 34.4 us -> 34.4 us (level)
  no operation moved by 1% of the time
where the time goes in v9:
time: 34.4 us; the launch traced here: 34.2 us
  starting transfers between devices  15.1 us (44%)
  waiting for transfers between devices  9.9 us (29%)
  Pallas kernels  8.49 us (25%)
  between operations  0.72 us (2%)
    pallas_call x12, Pallas kernels, call(): pl.pallas_call(kernel, out_shape=out_shape, in_specs=specs, out_specs=out...  8.49 us
    ppermute x8, waiting for transfers between devices, swap(): return lax.ppermute(array, axis, [(i, i ^ bit) for i in range(n)])  5.42 us
    ppermute x1, starting transfers between devices, shards_pairs(): lax.ppermute(to_z, 'seq', [(s, (s + (2 if s & 1 else -2)) % seq_count) fo...  5.1 us
    ppermute x4, starting transfers between devices, send(): return lax.ppermute(block, ('seq', 'head'), pairs)  5.07 us
    ppermute x8, starting transfers between devices, swap(): return lax.ppermute(array, axis, [(i, i ^ bit) for i in range(n)])  4.91 us
    ppermute x4, waiting for transfers between devices, send(): return lax.ppermute(block, ('seq', 'head'), pairs)  4.47 us
  transfers between devices with their start and end apart: 13, of which 6 were waited for; matrix products, arithmetic and copies ran while one was open for 0% of the time, Pallas kernels for 18%

profile of v9, /device:TPU:0, one launch (start us, length us, event | category | flops | bytes accessed | tf_op | source)
XLA Modules:
  0.0 34.2 jit_solution(16721016321299556355)
XLA Ops:
  0.6 1.3 %stage.1 = (bf16[2,128,384]{2,1,0:T(8,128)(2,1)S(1)}, bf16[2,128,384]{2,1,0:T(8,128)(2,1)S(1)}, bf16[384,384]{1,0:T(8,128)(2,1)S(1)}, bf16[384,384]{1,0:T(8,128)...) custom-call(s32[2,3]{1,0:T(2,128)} %bitcast.2, ...), custom_call_target="tpu_custom_call" | custom-call | bytes 3600000 | tf_op jit(solution)/shard_map/stage/pallas_call | solution.py:297
  1.9 5.1 %collective-permute-start = (bf16[2,128,384]{2,1,0:T(8,128)(2,1)S(1)}, bf16[2,128,384]{2,1,0:T(8,128)(2,1)S(1)}, u32[]{:S(2)}, u32[]{:S(2)}) collective-permute-start(bf16[2,128,384]{2,1,0:T(8,128)(2,1)S(1)} %get-tuple-element.31), channel_id=1, source_target_pairs={{0,24},{4,12},{8,0},{12,20},{16,8},{20,28},{24,16},{28,4},{1,25},{... | collective-permute-start | bytes 589832 | tf_op jit(solution)/shard_map/ppermute | solution.py:350
  7.0 4.0 %own_tiles.1 = (bf16[384,384]{1,0:T(8,128)(2,1)}, f32[2,512,384]{2,1,0:T(8,128)S(1)}, bf16[2,512,384]{2,1,0:T(8,128)(2,1)S(1)}, bf16[1536,768]{1,0:T(8,128)(2,1)S(1)}) custom-call(f32[8,128]{1,0:T(8,128)S(1)} %get-tuple-element.26.flags_ref, bf16[384,384]{1,0:T(8,128)(2,1)S(1)} %get-tuple-element.27.q_ref, bf16[384,384]{1,0:T(8,128)(2,1)S(1)} %get-tuple-element.28.g_ref, ...), custom_call_target="tpu_custom_call" | custom-call | bytes 18000000 | tf_op jit(solution)/shard_map/own_tiles/pallas_call | solution.py:297
  11.0 0.7 %early_text.1 = (bf16[512,768]{1,0:T(8,128)(2,1)S(1)}, bf16[4,64,768]{2,1,0:T(8,128)(2,1)S(1)}) custom-call(f32[8,128]{1,0:T(8,128)S(1)} %get-tuple-element.26.flags_ref, f32[2,512,384]{2,1,0:T(8,128)S(1)} %get-tuple-element.34.part_ref, bf16[1536,768]{1,0:T(8,128)(2,1)S(1)} %get-tuple-element.35.weight_ref), custom_call_target="tpu_custom_call" | custom-call | bytes 3600000 | tf_op jit(solution)/shard_map/early_text/pallas_call | solution.py:297
  11.8 1.6 %collective-permute-done.1.y_ref = bf16[2,128,384]{2,1,0:T(8,128)(2,1)S(1)} collective-permute-done((bf16[2,128,384]{2,1,0:T(8,128)(2,1)S(1)}, bf16[2,128,384]{2,1,0:T(8,128)(2,1)S(1)}, u32[]{:S(2)}, u32[]{:S(2)}) %collective-permute-start.1) | collective-permute-done | bytes 196640 | tf_op jit(solution)/shard_map/ppermute | solution.py:281
  13.4 0.2 first_text.1
  13.7 1.1 %second_text.1 = (bf16[4,64,768]{2,1,0:T(8,128)(2,1)S(1)}, bf16[4,64,768]{2,1,0:T(8,128)(2,1)S(1)}, bf16[4,64,768]{2,1,0:T(8,128)(2,1)S(1)}) custom-call(bf16[512,768]{1,0:T(8,128)(2,1)S(1)} %get-tuple-element.38.both_ref, bf16[1536,768]{1,0:T(8,128)(2,1)S(1)} %get-tuple-element.35.weight_ref), custom_call_target="tpu_custom_call" | custom-call | bytes 3600000 | tf_op jit(solution)/shard_map/second_text/pallas_call | solution.py:297
  14.8 0.6 %collective-permute-start.2 = (bf16[4,64,768]{2,1,0:T(8,128)(2,1)S(1)}, bf16[4,64,768]{2,1,0:T(8,128)(2,1)S(1)}, u32[]{:S(2)}, u32[]{:S(2)}) collective-permute-start(bf16[4,64,768]{2,1,0:T(8,128)(2,1)S(1)} %get-tuple-element.40), channel_id=1, source_target_pairs={{0,1},{1,0},{2,3},{3,2},{4,5},{5,4},{6,7},{7,6},{8,9},{9,8},{10,11... | collective-permute-start | bytes 1179656 | tf_op jit(solution)/shard_map/ppermute | solution.py:281
  15.5 1.6 %collective-permute-start.10 = (bf16[64,768]{1,0:T(8,128)(2,1)S(1)}, bf16[64,768]{1,0:T(8,128)(2,1)S(1)}, u32[]{:S(2)}, u32[]{:S(2)}) collective-permute-start(bf16[64,768]{1,0:T(8,128)(2,1)S(1)} %get-tuple-element.47), channel_id=1, source_target_pairs={{0,2},{1,3},{2,0},{3,1},{4,6},{5,7},{6,4},{7,5},{8,10},{9,11},{10,... | collective-permute-start | bytes 294920 | tf_op jit(solution)/shard_map/ppermute | solution.py:281
  17.1 0.5 %collective-permute-start.8 = (bf16[64,768]{1,0:T(8,128)(2,1)S(1)}, bf16[64,768]{1,0:T(8,128)(2,1)S(1)}, u32[]{:S(2)}, u32[]{:S(2)}) collective-permute-start(bf16[64,768]{1,0:T(8,128)(2,1)S(1)} %get-tuple-element.46), channel_id=1, source_target_pairs={{0,2},{1,3},{2,0},{3,1},{4,6},{5,7},{6,4},{7,5},{8,10},{9,11},{10,... | collective-permute-start | bytes 294920 | tf_op jit(solution)/shard_map/ppermute | solution.py:281
  17.6 1.5 %collective-permute-start.6 = (bf16[64,768]{1,0:T(8,128)(2,1)S(1)}, bf16[64,768]{1,0:T(8,128)(2,1)S(1)}, u32[]{:S(2)}, u32[]{:S(2)}) collective-permute-start(bf16[64,768]{1,0:T(8,128)(2,1)S(1)} %get-tuple-element.45), channel_id=1, source_target_pairs={{0,2},{1,3},{2,0},{3,1},{4,6},{5,7},{6,4},{7,5},{8,10},{9,11},{10,... | collective-permute-start | bytes 294920 | tf_op jit(solution)/shard_map/ppermute | solution.py:281
  19.1 0.5 %collective-permute-start.4 = (bf16[64,768]{1,0:T(8,128)(2,1)S(1)}, bf16[64,768]{1,0:T(8,128)(2,1)S(1)}, u32[]{:S(2)}, u32[]{:S(2)}) collective-permute-start(bf16[64,768]{1,0:T(8,128)(2,1)S(1)} %get-tuple-element.43), channel_id=1, source_target_pairs={{0,2},{1,3},{2,0},{3,1},{4,6},{5,7},{6,4},{7,5},{8,10},{9,11},{10,... | collective-permute-start | bytes 294920 | tf_op jit(solution)/shard_map/ppermute | solution.py:281
  19.6 1.6 %collective-permute-done.10.crossed_ref = bf16[64,768]{1,0:T(8,128)(2,1)S(1)} collective-permute-done((bf16[64,768]{1,0:T(8,128)(2,1)S(1)}, bf16[64,768]{1,0:T(8,128)(2,1)S(1)}, u32[]{:S(2)}, u32[]{:S(2)}) %collective-permute-start.10) | collective-permute-done | bytes 98336 | tf_op jit(solution)/shard_map/ppermute | solution.py:281
  21.2 2.1 %collective-permute-start.11 = (bf16[25,16,128]{2,1,0:T(8,128)(2,1)S(1)}, bf16[25,16,128]{2,1,0:T(8,128)(2,1)S(1)}, u32[]{:S(2)}, u32[]{:S(2)}) collective-permute-start(bf16[25,16,128]{2,1,0:T(8,128)(2,1)S(1)} %cross.7), channel_id=1, source_target_pairs={{0,24},{1,29},{2,26},{3,31},{4,28},{5,25},{6,30},{7,27},{8,16},{9,... | collective-permute-start | bytes 307208 | tf_op jit(solution)/shard_map/ppermute | solution.py:292
  23.4 0.9 %collective-permute-start.9 = (bf16[25,16,128]{2,1,0:T(8,128)(2,1)S(1)}, bf16[25,16,128]{2,1,0:T(8,128)(2,1)S(1)}, u32[]{:S(2)}, u32[]{:S(2)}) collective-permute-start(bf16[25,16,128]{2,1,0:T(8,128)(2,1)S(1)} %cross.6), channel_id=1, source_target_pairs={{0,16},{1,21},{2,18},{3,23},{4,20},{5,17},{6,22},{7,19},{8,24},{9,... | collective-permute-start | bytes 307208 | tf_op jit(solution)/shard_map/ppermute | solution.py:292
  24.4 1.0 %collective-permute-done.6.crossed_ref = bf16[64,768]{1,0:T(8,128)(2,1)S(1)} collective-permute-done((bf16[64,768]{1,0:T(8,128)(2,1)S(1)}, bf16[64,768]{1,0:T(8,128)(2,1)S(1)}, u32[]{:S(2)}, u32[]{:S(2)}) %collective-permute-start.6) | collective-permute-done | bytes 98336 | tf_op jit(solution)/shard_map/ppermute | solution.py:281
  25.4 1.3 %collective-permute-start.7 = (bf16[25,16,128]{2,1,0:T(8,128)(2,1)S(1)}, bf16[25,16,128]{2,1,0:T(8,128)(2,1)S(1)}, u32[]{:S(2)}, u32[]{:S(2)}) collective-permute-start(bf16[25,16,128]{2,1,0:T(8,128)(2,1)S(1)} %cross.5), channel_id=1, source_target_pairs={{0,8},{1,13},{2,10},{3,15},{4,12},{5,9},{6,14},{7,11},{8,0},{9,5},... | collective-permute-start | bytes 307208 | tf_op jit(solution)/shard_map/ppermute | solution.py:292
  26.8 0.7 %collective-permute-start.5 = (bf16[25,16,128]{2,1,0:T(8,128)(2,1)S(1)}, bf16[25,16,128]{2,1,0:T(8,128)(2,1)S(1)}, u32[]{:S(2)}, u32[]{:S(2)}) collective-permute-start(bf16[25,16,128]{2,1,0:T(8,128)(2,1)S(1)} %cross.4.refs_4_), channel_id=1, source_target_pairs={{1,5},{3,7},{5,1},{7,3},{9,13},{11,15},{13,9},{15,11},{17,21},{19,... | collective-permute-start | bytes 307208 | tf_op jit(solution)/shard_map/ppermute | solution.py:292
  27.5 0.4 %collective-permute-done.11.refs_3_ = bf16[25,16,128]{2,1,0:T(8,128)(2,1)S(1)} collective-permute-done((bf16[25,16,128]{2,1,0:T(8,128)(2,1)S(1)}, bf16[25,16,128]{2,1,0:T(8,128)(2,1)S(1)}, u32[]{:S(2)}, u32[]{:S(2)}) %collective-permute-start.11) | collective-permute-done | bytes 102432 | tf_op jit(solution)/shard_map/ppermute | solution.py:292
  27.9 4.1 %collective-permute-done.9.refs_2_ = bf16[25,16,128]{2,1,0:T(8,128)(2,1)S(1)} collective-permute-done((bf16[25,16,128]{2,1,0:T(8,128)(2,1)S(1)}, bf16[25,16,128]{2,1,0:T(8,128)(2,1)S(1)}, u32[]{:S(2)}, u32[]{:S(2)}) %collective-permute-start.9) | collective-permute-done | bytes 102432 | tf_op jit(solution)/shard_map/ppermute | solution.py:292
  32.0 0.2 captions.1
  32.2 0.2 collective-permute-start.12
  32.3 1.2 %collective-permute-done.12.came_ref = bf16[2,64,384]{2,1,0:T(8,128)(2,1)S(1)} collective-permute-done((bf16[2,64,384]{2,1,0:T(8,128)(2,1)S(1)}, bf16[2,64,384]{2,1,0:T(8,128)(2,1)S(1)}, u32[]{:S(2)}, u32[]{:S(2)}) %collective-permute-start.12) | collective-permute-done | bytes 98336 | tf_op jit(solution)/shard_map/ppermute | solution.py:281
  33.5 0.7 %final.1 = bf16[2,64,384]{2,1,0:T(8,128)(2,1)} custom-call(f32[2,64,384]{2,1,0:T(8,128)S(1)} %get-tuple-element.48.kept_ref, bf16[2,64,384]{2,1,0:T(8,128)(2,1)S(1)} %collective-permute-done.12.came_ref), custom_call_target="tpu_custom_call" | custom-call | bytes 3600000 | tf_op jit(solution)/shard_map/final/pallas_call | solution.py:297
  (14 shorter events, 0.4 us)
Async XLA Ops:
  1.9 9.9 %collective-permute-start = (bf16[2,128,384]{2,1,0:T(8,128)(2,1)S(1)}, bf16[2,128,384]{2,1,0:T(8,128)(2,1)S(1)}, u32[]{:S(2)}, u32[]{:S(2)}) collective-permute-start(bf16[2,128,384]{2,1,0:T(8,128)(2,1)S(1)} %get-tuple-element.31), channel_id=1, source_target_pairs={{0,24},{4,12},{8,0},{12,20},{16,8},{20,28},{24,16},{28,4},{1,25},{... | collective-permute-start | bytes 589832 | tf_op jit(solution)/shard_map/ppermute | solution.py:350
  7.0 6.4 %collective-permute-start.1 = (bf16[2,128,384]{2,1,0:T(8,128)(2,1)S(1)}, bf16[2,128,384]{2,1,0:T(8,128)(2,1)S(1)}, u32[]{:S(2)}, u32[]{:S(2)}) collective-permute-start(bf16[2,128,384]{2,1,0:T(8,128)(2,1)S(1)} %get-tuple-element.32), channel_id=1, source_target_pairs={{0,4},{4,0},{8,12},{12,8},{16,20},{20,16},{24,28},{28,24},{1,5},{5... | collective-permute-start | bytes 589832 | tf_op jit(solution)/shard_map/ppermute | solution.py:281
  13.6 1.8 %collective-permute-start.3 = (bf16[4,64,768]{2,1,0:T(8,128)(2,1)S(1)}, bf16[4,64,768]{2,1,0:T(8,128)(2,1)S(1)}, u32[]{:S(2)}, u32[]{:S(2)}) collective-permute-start(bf16[4,64,768]{2,1,0:T(8,128)(2,1)S(1)} %get-tuple-element.42), channel_id=1, source_target_pairs={{0,1},{1,0},{2,3},{3,2},{4,5},{5,4},{6,7},{7,6},{8,9},{9,8},{10,11... | collective-permute-start | bytes 1179656 | tf_op jit(solution)/shard_map/ppermute | solution.py:281
  14.8 4.8 %collective-permute-start.2 = (bf16[4,64,768]{2,1,0:T(8,128)(2,1)S(1)}, bf16[4,64,768]{2,1,0:T(8,128)(2,1)S(1)}, u32[]{:S(2)}, u32[]{:S(2)}) collective-permute-start(bf16[4,64,768]{2,1,0:T(8,128)(2,1)S(1)} %get-tuple-element.40), channel_id=1, source_target_pairs={{0,1},{1,0},{2,3},{3,2},{4,5},{5,4},{6,7},{7,6},{8,9},{9,8},{10,11... | collective-permute-start | bytes 1179656 | tf_op jit(solution)/shard_map/ppermute | solution.py:281
  15.5 5.7 %collective-permute-start.10 = (bf16[64,768]{1,0:T(8,128)(2,1)S(1)}, bf16[64,768]{1,0:T(8,128)(2,1)S(1)}, u32[]{:S(2)}, u32[]{:S(2)}) collective-permute-start(bf16[64,768]{1,0:T(8,128)(2,1)S(1)} %get-tuple-element.47), channel_id=1, source_target_pairs={{0,2},{1,3},{2,0},{3,1},{4,6},{5,7},{6,4},{7,5},{8,10},{9,11},{10,... | collective-permute-start | bytes 294920 | tf_op jit(solution)/shard_map/ppermute | solution.py:281
  17.1 6.3 %collective-permute-start.8 = (bf16[64,768]{1,0:T(8,128)(2,1)S(1)}, bf16[64,768]{1,0:T(8,128)(2,1)S(1)}, u32[]{:S(2)}, u32[]{:S(2)}) collective-permute-start(bf16[64,768]{1,0:T(8,128)(2,1)S(1)} %get-tuple-element.46), channel_id=1, source_target_pairs={{0,2},{1,3},{2,0},{3,1},{4,6},{5,7},{6,4},{7,5},{8,10},{9,11},{10,... | collective-permute-start | bytes 294920 | tf_op jit(solution)/shard_map/ppermute | solution.py:281
  17.6 7.8 %collective-permute-start.6 = (bf16[64,768]{1,0:T(8,128)(2,1)S(1)}, bf16[64,768]{1,0:T(8,128)(2,1)S(1)}, u32[]{:S(2)}, u32[]{:S(2)}) collective-permute-start(bf16[64,768]{1,0:T(8,128)(2,1)S(1)} %get-tuple-element.45), channel_id=1, source_target_pairs={{0,2},{1,3},{2,0},{3,1},{4,6},{5,7},{6,4},{7,5},{8,10},{9,11},{10,... | collective-permute-start | bytes 294920 | tf_op jit(solution)/shard_map/ppermute | solution.py:281
  19.1 7.7 %collective-permute-start.4 = (bf16[64,768]{1,0:T(8,128)(2,1)S(1)}, bf16[64,768]{1,0:T(8,128)(2,1)S(1)}, u32[]{:S(2)}, u32[]{:S(2)}) collective-permute-start(bf16[64,768]{1,0:T(8,128)(2,1)S(1)} %get-tuple-element.43), channel_id=1, source_target_pairs={{0,2},{1,3},{2,0},{3,1},{4,6},{5,7},{6,4},{7,5},{8,10},{9,11},{10,... | collective-permute-start | bytes 294920 | tf_op jit(solution)/shard_map/ppermute | solution.py:281
  21.2 6.6 %collective-permute-start.11 = (bf16[25,16,128]{2,1,0:T(8,128)(2,1)S(1)}, bf16[25,16,128]{2,1,0:T(8,128)(2,1)S(1)}, u32[]{:S(2)}, u32[]{:S(2)}) collective-permute-start(bf16[25,16,128]{2,1,0:T(8,128)(2,1)S(1)} %cross.7), channel_id=1, source_target_pairs={{0,24},{1,29},{2,26},{3,31},{4,28},{5,25},{6,30},{7,27},{8,16},{9,... | collective-permute-start | bytes 307208 | tf_op jit(solution)/shard_map/ppermute | solution.py:292
  23.4 8.5 %collective-permute-start.9 = (bf16[25,16,128]{2,1,0:T(8,128)(2,1)S(1)}, bf16[25,16,128]{2,1,0:T(8,128)(2,1)S(1)}, u32[]{:S(2)}, u32[]{:S(2)}) collective-permute-start(bf16[25,16,128]{2,1,0:T(8,128)(2,1)S(1)} %cross.6), channel_id=1, source_target_pairs={{0,16},{1,21},{2,18},{3,23},{4,20},{5,17},{6,22},{7,19},{8,24},{9,... | collective-permute-start | bytes 307208 | tf_op jit(solution)/shard_map/ppermute | solution.py:292
  25.4 6.5 %collective-permute-start.7 = (bf16[25,16,128]{2,1,0:T(8,128)(2,1)S(1)}, bf16[25,16,128]{2,1,0:T(8,128)(2,1)S(1)}, u32[]{:S(2)}, u32[]{:S(2)}) collective-permute-start(bf16[25,16,128]{2,1,0:T(8,128)(2,1)S(1)} %cross.5), channel_id=1, source_target_pairs={{0,8},{1,13},{2,10},{3,15},{4,12},{5,9},{6,14},{7,11},{8,0},{9,5},... | collective-permute-start | bytes 307208 | tf_op jit(solution)/shard_map/ppermute | solution.py:292
  26.8 5.1 %collective-permute-start.5 = (bf16[25,16,128]{2,1,0:T(8,128)(2,1)S(1)}, bf16[25,16,128]{2,1,0:T(8,128)(2,1)S(1)}, u32[]{:S(2)}, u32[]{:S(2)}) collective-permute-start(bf16[25,16,128]{2,1,0:T(8,128)(2,1)S(1)} %cross.4.refs_4_), channel_id=1, source_target_pairs={{1,5},{3,7},{5,1},{7,3},{9,13},{11,15},{13,9},{15,11},{17,21},{19,... | collective-permute-start | bytes 307208 | tf_op jit(solution)/shard_map/ppermute | solution.py:292
  32.2 1.4 %collective-permute-start.12 = (bf16[2,64,384]{2,1,0:T(8,128)(2,1)S(1)}, bf16[2,64,384]{2,1,0:T(8,128)(2,1)S(1)}, u32[]{:S(2)}, u32[]{:S(2)}) collective-permute-start(bf16[2,64,384]{2,1,0:T(8,128)(2,1)S(1)} %get-tuple-element.49), channel_id=1, source_target_pairs={{0,1},{1,0},{2,3},{3,2},{4,5},{5,4},{6,7},{7,6},{8,9},{9,8},{10,11... | collective-permute-start | bytes 294920 | tf_op jit(solution)/shard_map/ppermute | solution.py:281

commit v10 on v8

--- a/solution.py
+++ b/solution.py
@@ -220,9 +220,12 @@
             b[...] = a[...]
 
 
-def second_text_kernel(both_ref, weight_ref, sent_own_ref, kept_ref, kept_own_ref):
+def second_text_kernel(both_ref, weight_ref, sent_own_ref, kept_ref):
     project(both_ref[L // 2 :, :], weight_ref, 0, sent_own_ref)
     project(both_ref[: L // 2, :], weight_ref, 1, kept_ref)
+
+
+def third_text_kernel(both_ref, weight_ref, kept_own_ref):
     project(both_ref[: L // 2, :], weight_ref, 0, kept_own_ref)
 
 
@@ -388,14 +391,17 @@
         limit=KERNEL_LIMIT,
         hint_us=2.0,
     )
-    sent_own, kept, kept_own = call(
+    sent_own, kept = call(
         second_text_kernel,
         "second_text",
-        (half, half, half),
+        (half, half),
         (both, weight),
         [vmem] * 2,
         limit=KERNEL_LIMIT,
         hint_us=1.0,
+    )
+    kept_own = call(
+        third_text_kernel, "third_text", half, (both, weight), [vmem] * 2, limit=KERNEL_LIMIT, hint_us=1.0
     )
     block = like(block_rows, 2 * width)
     far = call(pair_kernel, "pair", (block,) * (seq_count // 2), (kept, swap(sent, "head", 1)), [vmem] * 2)

time: 34.4 us -> 34.4 us (level)
    pallas_call x12 -> x13, Pallas kernels: 8.49 us -> 8.68 us  [call(): pl.pallas_call(kernel, out_shape=out_shape, in_specs=specs, out_specs=out...]
  transfers between devices with their start and end apart: 13 -> 13, of which waited for: 6 -> 7; matrix products, arithmetic and copies ran while one was open for 0% -> 0% of each run, Pallas kernels for 18% -> 19%
where the time goes in v10:
time: 34.4 us; the launch traced here: 34.2 us
  starting transfers between devices  15.1 us (44%)
  waiting for transfers between devices  9.7 us (28%)
  Pallas kernels  8.68 us (25%)
  between operations  0.74 us (2%)
    pallas_call x13, Pallas kernels, call(): pl.pallas_call(kernel, out_shape=out_shape, in_specs=specs, out_specs=out...  8.68 us
    ppermute x8, waiting for transfers between devices, swap(): return lax.ppermute(array, axis, [(i, i ^ bit) for i in range(n)])  5.22 us
    ppermute x1, starting transfers between devices, shards_pairs(): lax.ppermute(to_z, 'seq', [(s, (s + (2 if s & 1 else -2)) % seq_count) fo...  5.1 us
    ppermute x4, starting transfers between devices, send(): return lax.ppermute(block, ('seq', 'head'), pairs)  5.07 us
    ppermute x8, starting transfers between devices, swap(): return lax.ppermute(array, axis, [(i, i ^ bit) for i in range(n)])  4.91 us
    ppermute x4, waiting for transfers between devices, send(): return lax.ppermute(block, ('seq', 'head'), pairs)  4.48 us
  transfers between devices with their start and end apart: 13, of which 7 were waited for; matrix products, arithmetic and copies ran while one was open for 0% of the time, Pallas kernels for 19%

profile of v10, /device:TPU:0, one launch (start us, length us, event | category | flops | bytes accessed | tf_op | source)
XLA Modules:
  0.0 34.2 jit_solution(17777251502011711607)
XLA Ops:
  0.6 1.3 %stage.1 = (bf16[2,128,384]{2,1,0:T(8,128)(2,1)S(1)}, bf16[2,128,384]{2,1,0:T(8,128)(2,1)S(1)}, bf16[384,384]{1,0:T(8,128)(2,1)S(1)}, bf16[384,384]{1,0:T(8,128)...) custom-call(s32[2,3]{1,0:T(2,128)} %bitcast.2, ...), custom_call_target="tpu_custom_call" | custom-call | bytes 3600000 | tf_op jit(solution)/shard_map/stage/pallas_call | solution.py:298
  1.9 5.1 %collective-permute-start = (bf16[2,128,384]{2,1,0:T(8,128)(2,1)S(1)}, bf16[2,128,384]{2,1,0:T(8,128)(2,1)S(1)}, u32[]{:S(2)}, u32[]{:S(2)}) collective-permute-start(bf16[2,128,384]{2,1,0:T(8,128)(2,1)S(1)} %get-tuple-element.30), channel_id=1, source_target_pairs={{0,24},{4,12},{8,0},{12,20},{16,8},{20,28},{24,16},{28,4},{1,25},{... | collective-permute-start | bytes 589832 | tf_op jit(solution)/shard_map/ppermute | solution.py:351
  7.0 4.0 %own_tiles.1 = (bf16[384,384]{1,0:T(8,128)(2,1)}, f32[2,512,384]{2,1,0:T(8,128)S(1)}, bf16[2,512,384]{2,1,0:T(8,128)(2,1)S(1)}, bf16[1536,768]{1,0:T(8,128)(2,1)S(1)}) custom-call(f32[8,128]{1,0:T(8,128)S(1)} %get-tuple-element.25.flags_ref, bf16[384,384]{1,0:T(8,128)(2,1)S(1)} %get-tuple-element.26.q_ref, bf16[384,384]{1,0:T(8,128)(2,1)S(1)} %get-tuple-element.27.g_ref, ...), custom_call_target="tpu_custom_call" | custom-call | bytes 18000000 | tf_op jit(solution)/shard_map/own_tiles/pallas_call | solution.py:298
  11.0 0.7 %early_text.1 = (bf16[512,768]{1,0:T(8,128)(2,1)S(1)}, bf16[4,64,768]{2,1,0:T(8,128)(2,1)S(1)}) custom-call(f32[8,128]{1,0:T(8,128)S(1)} %get-tuple-element.25.flags_ref, f32[2,512,384]{2,1,0:T(8,128)S(1)} %get-tuple-element.33.part_ref, bf16[1536,768]{1,0:T(8,128)(2,1)S(1)} %get-tuple-element.34.weight_ref), custom_call_target="tpu_custom_call" | custom-call | bytes 3600000 | tf_op jit(solution)/shard_map/early_text/pallas_call | solution.py:298
  11.8 1.6 %collective-permute-done.1.y_ref = bf16[2,128,384]{2,1,0:T(8,128)(2,1)S(1)} collective-permute-done((bf16[2,128,384]{2,1,0:T(8,128)(2,1)S(1)}, bf16[2,128,384]{2,1,0:T(8,128)(2,1)S(1)}, u32[]{:S(2)}, u32[]{:S(2)}) %collective-permute-start.1) | collective-permute-done | bytes 196640 | tf_op jit(solution)/shard_map/ppermute | solution.py:282
  13.4 0.2 first_text.1
  13.7 0.8 %second_text.1 = (bf16[4,64,768]{2,1,0:T(8,128)(2,1)S(1)}, bf16[4,64,768]{2,1,0:T(8,128)(2,1)S(1)}) custom-call(bf16[512,768]{1,0:T(8,128)(2,1)S(1)} %get-tuple-element.37.both_ref, bf16[1536,768]{1,0:T(8,128)(2,1)S(1)} %get-tuple-element.34.weight_ref), custom_call_target="tpu_custom_call" | custom-call | bytes 3600000 | tf_op jit(solution)/shard_map/second_text/pallas_call | solution.py:298
  14.5 0.6 %collective-permute-start.2 = (bf16[4,64,768]{2,1,0:T(8,128)(2,1)S(1)}, bf16[4,64,768]{2,1,0:T(8,128)(2,1)S(1)}, u32[]{:S(2)}, u32[]{:S(2)}) collective-permute-start(bf16[4,64,768]{2,1,0:T(8,128)(2,1)S(1)} %get-tuple-element.38), channel_id=1, source_target_pairs={{0,1},{1,0},{2,3},{3,2},{4,5},{5,4},{6,7},{7,6},{8,9},{9,8},{10,11... | collective-permute-start | bytes 1179656 | tf_op jit(solution)/shard_map/ppermute | solution.py:282
  15.0 0.3 collective-permute-done.3.came_ref
  15.5 1.6 %collective-permute-start.10 = (bf16[64,768]{1,0:T(8,128)(2,1)S(1)}, bf16[64,768]{1,0:T(8,128)(2,1)S(1)}, u32[]{:S(2)}, u32[]{:S(2)}) collective-permute-start(bf16[64,768]{1,0:T(8,128)(2,1)S(1)} %get-tuple-element.45), channel_id=1, source_target_pairs={{0,2},{1,3},{2,0},{3,1},{4,6},{5,7},{6,4},{7,5},{8,10},{9,11},{10,... | collective-permute-start | bytes 294920 | tf_op jit(solution)/shard_map/ppermute | solution.py:282
  17.1 0.5 %collective-permute-start.8 = (bf16[64,768]{1,0:T(8,128)(2,1)S(1)}, bf16[64,768]{1,0:T(8,128)(2,1)S(1)}, u32[]{:S(2)}, u32[]{:S(2)}) collective-permute-start(bf16[64,768]{1,0:T(8,128)(2,1)S(1)} %get-tuple-element.44), channel_id=1, source_target_pairs={{0,2},{1,3},{2,0},{3,1},{4,6},{5,7},{6,4},{7,5},{8,10},{9,11},{10,... | collective-permute-start | bytes 294920 | tf_op jit(solution)/shard_map/ppermute | solution.py:282
  17.6 1.5 %collective-permute-start.6 = (bf16[64,768]{1,0:T(8,128)(2,1)S(1)}, bf16[64,768]{1,0:T(8,128)(2,1)S(1)}, u32[]{:S(2)}, u32[]{:S(2)}) collective-permute-start(bf16[64,768]{1,0:T(8,128)(2,1)S(1)} %get-tuple-element.43), channel_id=1, source_target_pairs={{0,2},{1,3},{2,0},{3,1},{4,6},{5,7},{6,4},{7,5},{8,10},{9,11},{10,... | collective-permute-start | bytes 294920 | tf_op jit(solution)/shard_map/ppermute | solution.py:282
  19.1 0.5 %collective-permute-start.4 = (bf16[64,768]{1,0:T(8,128)(2,1)S(1)}, bf16[64,768]{1,0:T(8,128)(2,1)S(1)}, u32[]{:S(2)}, u32[]{:S(2)}) collective-permute-start(bf16[64,768]{1,0:T(8,128)(2,1)S(1)} %get-tuple-element.41), channel_id=1, source_target_pairs={{0,2},{1,3},{2,0},{3,1},{4,6},{5,7},{6,4},{7,5},{8,10},{9,11},{10,... | collective-permute-start | bytes 294920 | tf_op jit(solution)/shard_map/ppermute | solution.py:282
  19.6 0.5 %third_text.1.kept_ref = bf16[4,64,768]{2,1,0:T(8,128)(2,1)S(1)} custom-call(bf16[512,768]{1,0:T(8,128)(2,1)S(1)} %get-tuple-element.37.both_ref, bf16[1536,768]{1,0:T(8,128)(2,1)S(1)} %get-tuple-element.34.weight_ref), custom_call_target="tpu_custom_call" | custom-call | bytes 3600000 | tf_op jit(solution)/shard_map/third_text/pallas_call | solution.py:298
  20.1 1.1 %collective-permute-done.10.crossed_ref = bf16[64,768]{1,0:T(8,128)(2,1)S(1)} collective-permute-done((bf16[64,768]{1,0:T(8,128)(2,1)S(1)}, bf16[64,768]{1,0:T(8,128)(2,1)S(1)}, u32[]{:S(2)}, u32[]{:S(2)}) %collective-permute-start.10) | collective-permute-done | bytes 98336 | tf_op jit(solution)/shard_map/ppermute | solution.py:282
  21.2 2.1 %collective-permute-start.11 = (bf16[25,16,128]{2,1,0:T(8,128)(2,1)S(1)}, bf16[25,16,128]{2,1,0:T(8,128)(2,1)S(1)}, u32[]{:S(2)}, u32[]{:S(2)}) collective-permute-start(bf16[25,16,128]{2,1,0:T(8,128)(2,1)S(1)} %cross.7), channel_id=1, source_target_pairs={{0,24},{1,29},{2,26},{3,31},{4,28},{5,25},{6,30},{7,27},{8,16},{9,... | collective-permute-start | bytes 307208 | tf_op jit(solution)/shard_map/ppermute | solution.py:293
  23.4 0.9 %collective-permute-start.9 = (bf16[25,16,128]{2,1,0:T(8,128)(2,1)S(1)}, bf16[25,16,128]{2,1,0:T(8,128)(2,1)S(1)}, u32[]{:S(2)}, u32[]{:S(2)}) collective-permute-start(bf16[25,16,128]{2,1,0:T(8,128)(2,1)S(1)} %cross.6), channel_id=1, source_target_pairs={{0,16},{1,21},{2,18},{3,23},{4,20},{5,17},{6,22},{7,19},{8,24},{9,... | collective-permute-start | bytes 307208 | tf_op jit(solution)/shard_map/ppermute | solution.py:293
  24.4 1.0 %collective-permute-done.6.crossed_ref = bf16[64,768]{1,0:T(8,128)(2,1)S(1)} collective-permute-done((bf16[64,768]{1,0:T(8,128)(2,1)S(1)}, bf16[64,768]{1,0:T(8,128)(2,1)S(1)}, u32[]{:S(2)}, u32[]{:S(2)}) %collective-permute-start.6) | collective-permute-done | bytes 98336 | tf_op jit(solution)/shard_map/ppermute | solution.py:282
  25.4 1.3 %collective-permute-start.7 = (bf16[25,16,128]{2,1,0:T(8,128)(2,1)S(1)}, bf16[25,16,128]{2,1,0:T(8,128)(2,1)S(1)}, u32[]{:S(2)}, u32[]{:S(2)}) collective-permute-start(bf16[25,16,128]{2,1,0:T(8,128)(2,1)S(1)} %cross.5), channel_id=1, source_target_pairs={{0,8},{1,13},{2,10},{3,15},{4,12},{5,9},{6,14},{7,11},{8,0},{9,5},... | collective-permute-start | bytes 307208 | tf_op jit(solution)/shard_map/ppermute | solution.py:293
  26.8 0.7 %collective-permute-start.5 = (bf16[25,16,128]{2,1,0:T(8,128)(2,1)S(1)}, bf16[25,16,128]{2,1,0:T(8,128)(2,1)S(1)}, u32[]{:S(2)}, u32[]{:S(2)}) collective-permute-start(bf16[25,16,128]{2,1,0:T(8,128)(2,1)S(1)} %cross.4.refs_4_), channel_id=1, source_target_pairs={{1,5},{3,7},{5,1},{7,3},{9,13},{11,15},{13,9},{15,11},{17,21},{19,... | collective-permute-start | bytes 307208 | tf_op jit(solution)/shard_map/ppermute | solution.py:293
  27.5 0.4 %collective-permute-done.11.refs_3_ = bf16[25,16,128]{2,1,0:T(8,128)(2,1)S(1)} collective-permute-done((bf16[25,16,128]{2,1,0:T(8,128)(2,1)S(1)}, bf16[25,16,128]{2,1,0:T(8,128)(2,1)S(1)}, u32[]{:S(2)}, u32[]{:S(2)}) %collective-permute-start.11) | collective-permute-done | bytes 102432 | tf_op jit(solution)/shard_map/ppermute | solution.py:293
  27.9 4.1 %collective-permute-done.9.refs_2_ = bf16[25,16,128]{2,1,0:T(8,128)(2,1)S(1)} collective-permute-done((bf16[25,16,128]{2,1,0:T(8,128)(2,1)S(1)}, bf16[25,16,128]{2,1,0:T(8,128)(2,1)S(1)}, u32[]{:S(2)}, u32[]{:S(2)}) %collective-permute-start.9) | collective-permute-done | bytes 102432 | tf_op jit(solution)/shard_map/ppermute | solution.py:293
  32.3 1.2 %collective-permute-done.12.came_ref = bf16[2,64,384]{2,1,0:T(8,128)(2,1)S(1)} collective-permute-done((bf16[2,64,384]{2,1,0:T(8,128)(2,1)S(1)}, bf16[2,64,384]{2,1,0:T(8,128)(2,1)S(1)}, u32[]{:S(2)}, u32[]{:S(2)}) %collective-permute-start.12) | collective-permute-done | bytes 98336 | tf_op jit(solution)/shard_map/ppermute | solution.py:282
  33.5 0.7 %final.1 = bf16[2,64,384]{2,1,0:T(8,128)(2,1)} custom-call(f32[2,64,384]{2,1,0:T(8,128)S(1)} %get-tuple-element.46.kept_ref, bf16[2,64,384]{2,1,0:T(8,128)(2,1)S(1)} %collective-permute-done.12.came_ref), custom_call_target="tpu_custom_call" | custom-call | bytes 3600000 | tf_op jit(solution)/shard_map/final/pallas_call | solution.py:298
  (15 shorter events, 0.7 us)
Async XLA Ops:
  1.9 9.9 %collective-permute-start = (bf16[2,128,384]{2,1,0:T(8,128)(2,1)S(1)}, bf16[2,128,384]{2,1,0:T(8,128)(2,1)S(1)}, u32[]{:S(2)}, u32[]{:S(2)}) collective-permute-start(bf16[2,128,384]{2,1,0:T(8,128)(2,1)S(1)} %get-tuple-element.30), channel_id=1, source_target_pairs={{0,24},{4,12},{8,0},{12,20},{16,8},{20,28},{24,16},{28,4},{1,25},{... | collective-permute-start | bytes 589832 | tf_op jit(solution)/shard_map/ppermute | solution.py:351
  7.0 6.4 %collective-permute-start.1 = (bf16[2,128,384]{2,1,0:T(8,128)(2,1)S(1)}, bf16[2,128,384]{2,1,0:T(8,128)(2,1)S(1)}, u32[]{:S(2)}, u32[]{:S(2)}) collective-permute-start(bf16[2,128,384]{2,1,0:T(8,128)(2,1)S(1)} %get-tuple-element.31), channel_id=1, source_target_pairs={{0,4},{4,0},{8,12},{12,8},{16,20},{20,16},{24,28},{28,24},{1,5},{5... | collective-permute-start | bytes 589832 | tf_op jit(solution)/shard_map/ppermute | solution.py:282
  13.6 1.8 %collective-permute-start.3 = (bf16[4,64,768]{2,1,0:T(8,128)(2,1)S(1)}, bf16[4,64,768]{2,1,0:T(8,128)(2,1)S(1)}, u32[]{:S(2)}, u32[]{:S(2)}) collective-permute-start(bf16[4,64,768]{2,1,0:T(8,128)(2,1)S(1)} %get-tuple-element.40), channel_id=1, source_target_pairs={{0,1},{1,0},{2,3},{3,2},{4,5},{5,4},{6,7},{7,6},{8,9},{9,8},{10,11... | collective-permute-start | bytes 1179656 | tf_op jit(solution)/shard_map/ppermute | solution.py:282
  14.5 5.6 %collective-permute-start.2 = (bf16[4,64,768]{2,1,0:T(8,128)(2,1)S(1)}, bf16[4,64,768]{2,1,0:T(8,128)(2,1)S(1)}, u32[]{:S(2)}, u32[]{:S(2)}) collective-permute-start(bf16[4,64,768]{2,1,0:T(8,128)(2,1)S(1)} %get-tuple-element.38), channel_id=1, source_target_pairs={{0,1},{1,0},{2,3},{3,2},{4,5},{5,4},{6,7},{7,6},{8,9},{9,8},{10,11... | collective-permute-start | bytes 1179656 | tf_op jit(solution)/shard_map/ppermute | solution.py:282
  15.5 5.7 %collective-permute-start.10 = (bf16[64,768]{1,0:T(8,128)(2,1)S(1)}, bf16[64,768]{1,0:T(8,128)(2,1)S(1)}, u32[]{:S(2)}, u32[]{:S(2)}) collective-permute-start(bf16[64,768]{1,0:T(8,128)(2,1)S(1)} %get-tuple-element.45), channel_id=1, source_target_pairs={{0,2},{1,3},{2,0},{3,1},{4,6},{5,7},{6,4},{7,5},{8,10},{9,11},{10,... | collective-permute-start | bytes 294920 | tf_op jit(solution)/shard_map/ppermute | solution.py:282
  17.1 6.3 %collective-permute-start.8 = (bf16[64,768]{1,0:T(8,128)(2,1)S(1)}, bf16[64,768]{1,0:T(8,128)(2,1)S(1)}, u32[]{:S(2)}, u32[]{:S(2)}) collective-permute-start(bf16[64,768]{1,0:T(8,128)(2,1)S(1)} %get-tuple-element.44), channel_id=1, source_target_pairs={{0,2},{1,3},{2,0},{3,1},{4,6},{5,7},{6,4},{7,5},{8,10},{9,11},{10,... | collective-permute-start | bytes 294920 | tf_op jit(solution)/shard_map/ppermute | solution.py:282
  17.6 7.8 %collective-permute-start.6 = (bf16[64,768]{1,0:T(8,128)(2,1)S(1)}, bf16[64,768]{1,0:T(8,128)(2,1)S(1)}, u32[]{:S(2)}, u32[]{:S(2)}) collective-permute-start(bf16[64,768]{1,0:T(8,128)(2,1)S(1)} %get-tuple-element.43), channel_id=1, source_target_pairs={{0,2},{1,3},{2,0},{3,1},{4,6},{5,7},{6,4},{7,5},{8,10},{9,11},{10,... | collective-permute-start | bytes 294920 | tf_op jit(solution)/shard_map/ppermute | solution.py:282
  19.1 7.7 %collective-permute-start.4 = (bf16[64,768]{1,0:T(8,128)(2,1)S(1)}, bf16[64,768]{1,0:T(8,128)(2,1)S(1)}, u32[]{:S(2)}, u32[]{:S(2)}) collective-permute-start(bf16[64,768]{1,0:T(8,128)(2,1)S(1)} %get-tuple-element.41), channel_id=1, source_target_pairs={{0,2},{1,3},{2,0},{3,1},{4,6},{5,7},{6,4},{7,5},{8,10},{9,11},{10,... | collective-permute-start | bytes 294920 | tf_op jit(solution)/shard_map/ppermute | solution.py:282
  21.2 6.6 %collective-permute-start.11 = (bf16[25,16,128]{2,1,0:T(8,128)(2,1)S(1)}, bf16[25,16,128]{2,1,0:T(8,128)(2,1)S(1)}, u32[]{:S(2)}, u32[]{:S(2)}) collective-permute-start(bf16[25,16,128]{2,1,0:T(8,128)(2,1)S(1)} %cross.7), channel_id=1, source_target_pairs={{0,24},{1,29},{2,26},{3,31},{4,28},{5,25},{6,30},{7,27},{8,16},{9,... | collective-permute-start | bytes 307208 | tf_op jit(solution)/shard_map/ppermute | solution.py:293
  23.4 8.5 %collective-permute-start.9 = (bf16[25,16,128]{2,1,0:T(8,128)(2,1)S(1)}, bf16[25,16,128]{2,1,0:T(8,128)(2,1)S(1)}, u32[]{:S(2)}, u32[]{:S(2)}) collective-permute-start(bf16[25,16,128]{2,1,0:T(8,128)(2,1)S(1)} %cross.6), channel_id=1, source_target_pairs={{0,16},{1,21},{2,18},{3,23},{4,20},{5,17},{6,22},{7,19},{8,24},{9,... | collective-permute-start | bytes 307208 | tf_op jit(solution)/shard_map/ppermute | solution.py:293
  25.4 6.5 %collective-permute-start.7 = (bf16[25,16,128]{2,1,0:T(8,128)(2,1)S(1)}, bf16[25,16,128]{2,1,0:T(8,128)(2,1)S(1)}, u32[]{:S(2)}, u32[]{:S(2)}) collective-permute-start(bf16[25,16,128]{2,1,0:T(8,128)(2,1)S(1)} %cross.5), channel_id=1, source_target_pairs={{0,8},{1,13},{2,10},{3,15},{4,12},{5,9},{6,14},{7,11},{8,0},{9,5},... | collective-permute-start | bytes 307208 | tf_op jit(solution)/shard_map/ppermute | solution.py:293
  26.8 5.2 %collective-permute-start.5 = (bf16[25,16,128]{2,1,0:T(8,128)(2,1)S(1)}, bf16[25,16,128]{2,1,0:T(8,128)(2,1)S(1)}, u32[]{:S(2)}, u32[]{:S(2)}) collective-permute-start(bf16[25,16,128]{2,1,0:T(8,128)(2,1)S(1)} %cross.4.refs_4_), channel_id=1, source_target_pairs={{1,5},{3,7},{5,1},{7,3},{9,13},{11,15},{13,9},{15,11},{17,21},{19,... | collective-permute-start | bytes 307208 | tf_op jit(solution)/shard_map/ppermute | solution.py:293
  32.2 1.4 %collective-permute-start.12 = (bf16[2,64,384]{2,1,0:T(8,128)(2,1)S(1)}, bf16[2,64,384]{2,1,0:T(8,128)(2,1)S(1)}, u32[]{:S(2)}, u32[]{:S(2)}) collective-permute-start(bf16[2,64,384]{2,1,0:T(8,128)(2,1)S(1)} %get-tuple-element.47), channel_id=1, source_target_pairs={{0,1},{1,0},{2,3},{3,2},{4,5},{5,4},{6,7},{7,6},{8,9},{9,8},{10,11... | collective-permute-start | bytes 294920 | tf_op jit(solution)/shard_map/ppermute | solution.py:282
